TPU v7x, 512 devices: a whole 4x8x8 slice. The times are simulated.
512 devices in a mesh: gx: 16 (over y_lo, x, core), gy: 32 (over z, y_hi).
Axes of the slice: x: 4, y: 8 (y_hi: 4, y_lo: 2; y = y_hi * 2 + y_lo), z: 8, core: 2. Of those that a mesh axis runs over, the one named last changes fastest.
Arguments:
- fine_nodes: bfloat16 [16, 32, 512, 128], P('gx', 'gy'), may hold values from -6 to 6
- fine_edges: int32 [16, 32, 2, 1536], P('gx', 'gy'), may hold values from 0 to 1023, as said below
- fine_live: int32 [16, 32], P('gx', 'gy'), may hold values from 512 to 1536, as said below
- fine_halo: int32 [16, 32, 4, 1], P('gx', 'gy'), may hold values from 0 to 3, as said below
- pool_map: int32 [16, 32, 512], P('gx', 'gy'), may hold values from 0 to 255, as said below
- coarse_edges: int32 [16, 32, 2, 2048], P('gx', 'gy'), may hold values from 0 to 767, as said below
- coarse_halo: int32 [16, 32, 4, 1], P('gx', 'gy'), may hold values from 0 to 1, as said below
- fine_weights: bfloat16 [5, 128, 128], replicated, may hold values from -0.5 to 0.5
- fine_bias: float32 [128], replicated, may hold values from -3 to 3
- fine_gain: float32 [128], replicated, may hold values from 0.25 to 1.75
- coarse_weights: bfloat16 [2, 5, 128, 128], replicated, may hold values from -0.5 to 0.5
- coarse_bias: float32 [2, 128], replicated, may hold values from -3 to 3
- coarse_gain: float32 [2, 128], replicated, may hold values from 0.25 to 1.75
- cotangent: bfloat16 [16, 32, 512, 128], P('gx', 'gy'), may hold values from -6 to 6
Outputs:
- fine_out: bfloat16 [16, 32, 512, 128], P('gx', 'gy')
- grad_fine_weights: float32 [5, 128, 128], replicated
- grad_fine_bias: float32 [128], replicated
- grad_fine_gain: float32 [128], replicated
- grad_coarse_weights: float32 [2, 5, 128, 128], replicated
- grad_coarse_bias: float32 [2, 128], replicated
- grad_coarse_gain: float32 [2, 128], replicated
- grad_pooled: float32 [16, 32, 256, 128], P('gx', 'gy')
Inputs may be any that keep to these rules, and one draw needn't show every extreme that they name: `fine_edges`: row 0 of each device's slots names senders: below 512 a node of the device, from 512 on a row of the four halo groups; row 1 names receivers among the device's 512 nodes. `fine_live`: A multiple of 512; in every draw some device has all 1536 slots live. `fine_halo`: block numbers of the device's fine nodes; within one device and direction they differ. `pool_map`: every coarse node of a device is named by at least one of its fine nodes. `coarse_edges`: row 0 names senders: below 256 a coarse node of the device, from 256 on a row of the four coarse halo groups; row 1 names receivers among the device's 256 coarse nodes. `coarse_halo`: block numbers of the device's coarse nodes.
All inputs are finite; a program needn't handle non-finite values.
Results may differ from a plain program's by a relative error of at most 0.009.
Values may be sent and summed in bfloat16 or wider, within the bound.
No kernel may reach another device: no remote copies, remote signals or barrier semaphores. Data moves between devices by JAX's collectives and lax.ppermute only.
A program may use at most 64 MiB of HBM per device.

v0:
```python
import math

import jax
import jax.numpy as jnp
from jax import lax
from jax.sharding import PartitionSpec as P

BLOCK = 128
EDGE_BLOCK = 512
COARSE_STEPS = 2
NC_DEV = 256


EPSILON = 1e-05


def extended_2(x, sides, width):
    for axis, dim in sides:
        peers, length = (lax.axis_size(axis), x.shape[dim])
        up = [(i, (i + 1) % peers) for i in range(peers - 1)]
        down = [(j, i) for i, j in up]
        last = lax.slice_in_dim(x, length - width, length, axis=dim)
        initial = lax.slice_in_dim(x, 0, width, axis=dim)
        before = lax.ppermute(last, axis, up)
        after = lax.ppermute(initial, axis, down)
        x = jnp.concatenate([before, x, after], axis=dim)
    return x


def layer_norm(values):
    centred = values - jnp.mean(values, axis=-1, keepdims=True)
    spread = jnp.mean(centred * centred, axis=-1, keepdims=True)
    return centred * lax.rsqrt(spread + EPSILON)


def split_parts(values):
    high = values.astype(jnp.bfloat16)
    low = (values - high.astype(jnp.float32)).astype(jnp.bfloat16)
    return (high, low)


def contract_rows(left, right):
    high, low = split_parts(right)
    numbers = (((0,), (0,)), ((), ()))
    return lax.dot_general(
        left, high, numbers, preferred_element_type=jnp.float32
    ) + lax.dot_general(left, low, numbers, preferred_element_type=jnp.float32)


def times_transpose(left, weight):
    high, low = split_parts(left)
    numbers = (((1,), (1,)), ((), ()))
    return lax.dot_general(
        high, weight, numbers, preferred_element_type=jnp.float32
    ) + lax.dot_general(low, weight, numbers, preferred_element_type=jnp.float32)


def make_one_hot(pool_rows, coarse_count):
    return (pool_rows[:, None] == lax.iota(jnp.int32, coarse_count)[None, :]).astype(jnp.bfloat16)


def pick_blocks(node_rows, block_lists):
    features = node_rows.shape[-1]
    blocked = node_rows.reshape(-1, BLOCK, features)
    return blocked[block_lists].reshape(4, -1, features)


def put_blocks(returned, block_lists, row_count):
    features = returned.shape[-1]
    total = (
        jnp.zeros((row_count // BLOCK, BLOCK, features), jnp.float32)
        .at[block_lists.reshape(-1)]
        .add(returned)
    )
    return total.reshape(row_count, features)


def slot_block(edge_list, live_slots, first_slot, block_width):
    senders = lax.dynamic_slice_in_dim(edge_list[0], first_slot, block_width)
    receivers = lax.dynamic_slice_in_dim(edge_list[1], first_slot, block_width)
    weights_live = (first_slot + lax.iota(jnp.int32, block_width) < live_slots).astype(jnp.float32)
    return (senders, receivers, weights_live)


def step_forward(
    node_rows,
    halo_rows,
    edge_list,
    live_slots,
    turn_count,
    weights,
    edge_bias,
    norm_gain,
    block_width,
):
    row_count = node_rows.shape[0]
    extended = jnp.concatenate([node_rows, halo_rows], axis=0)
    proj_send = jnp.dot(extended, weights[0], preferred_element_type=jnp.float32)
    proj_recv = jnp.dot(node_rows, weights[1], preferred_element_type=jnp.float32)

    def one_turn(turn_index, running):
        first_slot = (turn_index * block_width).astype(jnp.int32)
        senders, receivers, weights_live = slot_block(
            edge_list, live_slots, first_slot, block_width
        )
        hidden = jax.nn.silu(proj_send[senders] + proj_recv[receivers] + edge_bias).astype(
            jnp.bfloat16
        )
        message = (
            jnp.dot(hidden, weights[2], preferred_element_type=jnp.float32) * weights_live[:, None]
        )
        return running.at[receivers].add(message)

    summed = lax.fori_loop(
        0, turn_count, one_turn, jnp.zeros((row_count, proj_recv.shape[1]), jnp.float32)
    )
    agg_low = summed.astype(jnp.bfloat16)
    node_pre = jnp.dot(node_rows, weights[3], preferred_element_type=jnp.float32) + jnp.dot(
        agg_low, weights[4], preferred_element_type=jnp.float32
    )
    output = (node_rows.astype(jnp.float32) + norm_gain * layer_norm(node_pre)).astype(jnp.bfloat16)
    return (output, (extended, proj_send, proj_recv, agg_low, node_pre))


def step_backward(
    upstream,
    node_rows,
    saved_state,
    edge_list,
    live_slots,
    turn_count,
    weights,
    edge_bias,
    norm_gain,
    block_width,
    want_input,
):
    extended, proj_send, proj_recv, agg_low, node_pre = saved_state
    row_count = node_rows.shape[0]
    features = proj_recv.shape[1]
    normed, norm_back = jax.vjp(layer_norm, node_pre)
    grad_gain = jnp.sum(upstream * normed, axis=0)
    grad_pre = norm_back(upstream * norm_gain)[0]
    grad_self = contract_rows(node_rows, grad_pre)
    grad_agg_weight = contract_rows(agg_low, grad_pre)
    grad_agg = times_transpose(grad_pre, weights[4])

    def one_turn(turn_index, running):
        grad_send, grad_recv, grad_bias, grad_msg = running
        first_slot = (turn_index * block_width).astype(jnp.int32)
        senders, receivers, weights_live = slot_block(
            edge_list, live_slots, first_slot, block_width
        )
        pre_act = proj_send[senders] + proj_recv[receivers] + edge_bias
        hidden = jax.nn.silu(pre_act).astype(jnp.bfloat16)
        grad_message = grad_agg[receivers] * weights_live[:, None]
        grad_msg = grad_msg + contract_rows(hidden, grad_message)
        sigmoid = jax.nn.sigmoid(pre_act)
        grad_act = (
            times_transpose(grad_message, weights[2]) * sigmoid * (1.0 + pre_act * (1.0 - sigmoid))
        )
        return (
            grad_send.at[senders].add(grad_act),
            grad_recv.at[receivers].add(grad_act),
            grad_bias + jnp.sum(grad_act, axis=0),
            grad_msg,
        )

    start_state = (
        jnp.zeros(proj_send.shape, jnp.float32),
        jnp.zeros(proj_recv.shape, jnp.float32),
        jnp.zeros((features,), jnp.float32),
        jnp.zeros((features, features), jnp.float32),
    )
    grad_send, grad_recv, grad_bias, grad_msg = lax.fori_loop(0, turn_count, one_turn, start_state)
    grad_weights = jnp.stack(
        [
            contract_rows(extended, grad_send),
            contract_rows(node_rows, grad_recv),
            grad_msg,
            grad_self,
            grad_agg_weight,
        ]
    )
    if not want_input:
        return ((grad_weights, grad_bias, grad_gain), None, None)
    grad_ext = times_transpose(grad_send, weights[0])
    grad_nodes = (
        upstream
        + times_transpose(grad_pre, weights[3])
        + times_transpose(grad_recv, weights[1])
        + grad_ext[:row_count]
    )
    return ((grad_weights, grad_bias, grad_gain), grad_nodes, grad_ext[row_count:])


def fine_exchange(node_rows, block_lists):
    sends = pick_blocks(node_rows, block_lists)
    across = extended_2(sends[0:2], (("gx", 0),), 1)
    along = extended_2(sends[2:4], (("gy", 0),), 1)
    return jnp.concatenate([across[0], across[3], along[0], along[3]], axis=0)


def coarse_exchange(node_rows, block_lists):
    sends = pick_blocks(node_rows, block_lists)
    across = extended_2(sends[0:2], (("gx", 0),), 1)
    along = extended_2(sends[2:4], (("gy", 0),), 1)
    return jnp.concatenate([across[0], across[3], along[0], along[3]], axis=0)


def coarse_return(halo_grads, block_lists, row_count):
    split = halo_grads.reshape(4, -1, halo_grads.shape[-1])
    across = extended_2(split[0:2].astype(jnp.bfloat16), (("gx", 0),), 1).astype(jnp.float32)
    along = extended_2(split[2:4].astype(jnp.bfloat16), (("gy", 0),), 1).astype(jnp.float32)
    returned = jnp.stack([across[0], across[3], along[0], along[3]])
    return put_blocks(returned, block_lists, row_count)


def body(
    fine_nodes,
    fine_edges,
    fine_live,
    fine_halo,
    pool_map,
    coarse_edges,
    coarse_halo,
    fine_weights,
    fine_bias,
    fine_gain,
    coarse_weights,
    coarse_bias,
    coarse_gain,
    cotangent,
):
    node_rows = fine_nodes[0, 0]
    edge_list = fine_edges[0, 0]
    live_slots = fine_live[0, 0]
    pool_rows = pool_map[0, 0]
    coarse_list = coarse_edges[0, 0]
    coarse_blocks = coarse_halo[0, 0]
    coarse_slots = coarse_list.shape[1]
    coarse_turns = coarse_slots // EDGE_BLOCK
    fine_turns = live_slots // EDGE_BLOCK
    halo_rows = fine_exchange(node_rows, fine_halo[0, 0])
    fine_mid, fine_saved = step_forward(
        node_rows,
        halo_rows,
        edge_list,
        live_slots,
        fine_turns,
        fine_weights,
        fine_bias,
        fine_gain,
        EDGE_BLOCK,
    )
    one_hot = make_one_hot(pool_rows, NC_DEV)
    pooled_sums = lax.dot_general(
        one_hot, fine_mid, (((0,), (0,)), ((), ())), preferred_element_type=jnp.float32
    )
    counts = jnp.sum(one_hot, axis=0, dtype=jnp.float32)
    current = (pooled_sums / counts[:, None]).astype(jnp.bfloat16)
    states = []
    for step_index in range(COARSE_STEPS):
        coarse_rows = coarse_exchange(current, coarse_blocks)
        following, saved_state = step_forward(
            current,
            coarse_rows,
            coarse_list,
            coarse_slots,
            coarse_turns,
            coarse_weights[step_index],
            coarse_bias[step_index],
            coarse_gain[step_index],
            EDGE_BLOCK,
        )
        states.append((current, saved_state))
        current = following
    lifted = jnp.dot(one_hot, current, preferred_element_type=jnp.float32)
    fine_out = (fine_mid.astype(jnp.float32) + lifted).astype(jnp.bfloat16)
    total_nodes = node_rows.shape[0] * lax.axis_size("gx") * lax.axis_size("gy")
    loss_scale = 1.0 / math.sqrt(total_nodes)
    direct = cotangent[0, 0].astype(jnp.float32) * loss_scale
    upstream = jax.ops.segment_sum(direct, pool_rows, num_segments=NC_DEV)
    coarse_terms = [None] * COARSE_STEPS
    for step_index in reversed(range(COARSE_STEPS)):
        inputs_now, saved_state = states[step_index]
        step_terms, grad_nodes, grad_halo = step_backward(
            upstream,
            inputs_now,
            saved_state,
            coarse_list,
            coarse_slots,
            coarse_turns,
            coarse_weights[step_index],
            coarse_bias[step_index],
            coarse_gain[step_index],
            EDGE_BLOCK,
            True,
        )
        upstream = grad_nodes + coarse_return(grad_halo, coarse_blocks, NC_DEV)
        coarse_terms[step_index] = step_terms
    grad_pooled = upstream * math.sqrt(total_nodes)
    coarse_stacked = (
        jnp.stack([entry[0] for entry in coarse_terms]),
        jnp.stack([entry[1] for entry in coarse_terms]),
        jnp.stack([entry[2] for entry in coarse_terms]),
    )
    fine_seed = direct + (upstream / counts[:, None])[pool_rows]
    fine_terms = step_backward(
        fine_seed,
        node_rows,
        fine_saved,
        edge_list,
        live_slots,
        fine_turns,
        fine_weights,
        fine_bias,
        fine_gain,
        EDGE_BLOCK,
        False,
    )[0]
    everything = lax.psum(
        (
            fine_terms[0],
            fine_terms[1],
            fine_terms[2],
            coarse_stacked[0],
            coarse_stacked[1],
            coarse_stacked[2],
        ),
        ("gx", "gy"),
    )
    fine_total = everything[0:3]
    coarse_total = everything[3:6]
    return (
        fine_out[None, None],
        fine_total[0],
        fine_total[1],
        fine_total[2],
        coarse_total[0],
        coarse_total[1],
        coarse_total[2],
        grad_pooled[None, None],
    )


def solution(mesh):
    return jax.shard_map(
        body,
        mesh=mesh,
        in_specs=(
            P("gx", "gy", None, None),
            P("gx", "gy", None, None),
            P("gx", "gy"),
            P("gx", "gy", None, None),
            P("gx", "gy", None),
            P("gx", "gy", None, None),
            P("gx", "gy", None, None),
            P(),
            P(),
            P(),
            P(),
            P(),
            P(),
            P("gx", "gy", None, None),
        ),
        out_specs=(
            P("gx", "gy", None, None),
            P(),
            P(),
            P(),
            P(),
            P(),
            P(),
            P("gx", "gy", None, None),
        ),
        check_vma=False,
    )
```

profile of v0, /device:TPU:1, one launch (start us, length us, event | category | flops | bytes accessed | tf_op | source)
XLA Modules:
  0.0 698.2 jit_solution(15708051236267008273)
XLA Ops:
  9.5 4.5 collective-permute-start
  14.1 5.6 collective-permute-start.1
  33.5 6.4 while.92
  36.5 3.4 scatter_fusion
  43.0 3.2 collective-permute-start.4
  48.3 6.1 collective-permute-start.6
  55.7 5.7 collective-permute-done.7
  62.8 23.1 %while.93 = (s32[]{:T(128)}, f32[256,128]{1,0:T(8,128)S(1)}, s32[2,2048]{1,0:T(2,128)S(1)}, f32[768,128]{1,0:T(8,128)S(1)}, f32[256,128]{1,0:T(8,128)S(1)}, /*in...) while((s32[]{:T(128)}, f32[256,128]{1,0:T(8,128)S(1)}, ...), condition=%wide.region_8.9_spmd, body=%wide.region_6.8_spmd.sunk | while | flops 17373700 | bytes 2718371 | solution.py:114
  65.2 3.4 scatter_fusion.1
  71.0 3.4 scatter_fusion.1
  76.7 3.4 scatter_fusion.1
  82.5 3.4 scatter_fusion.1
  88.6 5.1 collective-permute-start.8
  96.5 5.4 collective-permute-start.10
  103.8 3.7 collective-permute-done.11
  108.8 26.1 %while.94 = (s32[]{:T(128)}, f32[256,128]{1,0:T(8,128)S(1)}, s32[2,2048]{1,0:T(2,128)S(1)}, f32[768,128]{1,0:T(8,128)S(1)}, f32[256,128]{1,0:T(8,128)S(1)}, /*in...) while((s32[]{:T(128)}, f32[256,128]{1,0:T(8,128)S(1)}, ...), condition=%wide.region_13.14_spmd, body=%wide.region_11.13_spmd.sunk | while | flops 17373700 | bytes 2718371 | solution.py:114
  112.0 3.4 scatter_fusion.2
  118.5 3.4 scatter_fusion.2
  125.0 3.4 scatter_fusion.2
  131.6 3.4 scatter_fusion.2
  139.4 75.2 %while.96 = (s32[]{:T(128)}, f32[768,128]{1,0:T(8,128)S(1)}, f32[256,128]{1,0:T(8,128)S(1)}, f32[128]{0:T(128)}, f32[128,128]{1,0:T(8,128)}, /*index=5*/s32[2,20...) while((s32[]{:T(128)}, f32[768,128]{1,0:T(8,128)S(1)}, ...), condition=%wide.region_23.24_spmd.clone, body=%wide.region_19.23_spmd.clone.sunk | while | flops 69458560 | bytes 10022430 | solution.py:175
  149.5 3.5 scatter_fusion.5
  152.9 3.4 scatter_fusion.6
  168.5 3.5 scatter_fusion.5
  172.0 3.4 scatter_fusion.6
  187.5 3.5 scatter_fusion.5
  191.0 3.4 scatter_fusion.6
  206.5 3.5 scatter_fusion.5
  210.0 3.4 scatter_fusion.6
  221.2 5.1 collective-permute-start.12
  229.9 12.4 %collective-permute-start.14 = (bf16[1,128,128]{2,1,0:T(8,128)(2,1)S(1)}, bf16[1,128,128]{2,1,0:T(8,128)(2,1)S(1)}, u32[]{:S(2)}, u32[]{:S(2)}) collective-permute-start(bf16[1,128,128]{2,1,0:T(8,128)(2,1)S(1)} %get-tuple-element.1040), channel_id=1, source_target_pairs={{0,1},{1,2},{2,3},{3,4},{4,5},{5,6},{6,7},{7,8},{8,9},{9,10},{10,1... | collective-permute-start | bytes 98312 | tf_op jit(solution)/shard_map/ppermute | solution.py:24
  243.8 4.3 collective-permute-done.15
  255.6 65.9 %while.97 = (s32[]{:T(128)}, f32[768,128]{1,0:T(8,128)S(1)}, f32[256,128]{1,0:T(8,128)S(1)}, f32[128]{0:T(128)}, f32[128,128]{1,0:T(8,128)S(1)}, /*index=5*/s32[...) while((s32[]{:T(128)}, f32[768,128]{1,0:T(8,128)S(1)}, ...), condition=%wide.region_31.32_spmd.clone, body=%wide.region_27.0_spmd.clone.sunk | while | flops 69458560 | bytes 6876626 | solution.py:175
  263.4 3.5 scatter_fusion.7
  266.8 3.4 scatter_fusion.8
  279.9 3.5 scatter_fusion.7
  283.3 3.4 scatter_fusion.8
  296.3 3.5 scatter_fusion.7
  299.8 3.4 scatter_fusion.8
  312.8 3.5 scatter_fusion.7
  316.3 3.4 scatter_fusion.8
  328.5 4.8 collective-permute-start.16
  335.3 6.5 collective-permute-start.18
  357.7 13.8 %while.95 = (s32[]{:T(128)}, f32[1024,128]{1,0:T(8,128)S(1)}, f32[512,128]{1,0:T(8,128)S(1)}, f32[128]{0:T(128)S(1)}, f32[128,128]{1,0:T(8,128)S(1)}, /*index=5*...) while((s32[]{:T(128)}, f32[1024,128]{1,0:T(8,128)S(1)}, ...), condition=%wide.region_39.40_spmd, body=%wide.region_35.39_spmd.sunk | while | flops 69442048 | bytes 6819031 | solution.py:175
  364.6 3.5 scatter_fusion.3
  368.1 3.4 scatter_fusion.4
  379.0 139.6 %all-reduce = (f32[128]{0:T(128)}, f32[128]{0:T(128)}, f32[2,128]{1,0:T(2,128)}, f32[2,128]{1,0:T(2,128)}) all-reduce(f32[128]{0:T(128)S(1)} %get-tuple-element.759, f32[128]{0:T(128)S(1)} %get-tuple-element.860, f32[2,128]{1,0:T(2,128)S(1)} %pad_maximum_fusion.11, ...), channel_id=1, replica_groups=mesh['gx'=16,'gy'=32] {'gx','gy'}, use_global_device_ids=true, to_apply=%region_41.42 | all-reduce | flops 768 | bytes 6144 | tf_op jit(solution)/shard_map/psum | solution.py:322
  518.7 169.8 %all-reduce.4.cloned.1.call-done = (f32[5,128,128]{2,1,0:T(8,128)}, f32[2,5,128,128]{3,2,1,0:T(8,128)}) async-done(((f32[5,128,128]{2,1,0:T(8,128)}, f32[2,5,128,128]{3,2,1,0:T(8,128)}), (f32[5,128,128]{2,1,0:T(8,128)}, f32[2,5,128,128]{3,2,1,0:T(8,128)})) %all-reduce.4.cloned.1.call-update) | async-done | bytes 983056 | tf_op jit(solution)/shard_map/psum | solution.py:322
  (742 shorter events, 205.4 us)
Async XLA Ops:
  7.2 681.3 %all-reduce.4.cloned.1.call-start = ((), (), s32[]{:S(2)}) async-start(), calls=%async_computation | async-start | bytes 1966080 | tf_op jit(solution)/shard_map/psum | solution.py:322
  9.4 13.2 %copy-start.3 = (bf16[1,1,512,128]{3,2,1,0:T(8,128)(2,1)S(1)}, bf16[1,1,512,128]{3,2,1,0:T(8,128)(2,1)}, u32[]{:S(2)}) copy-start(bf16[1,1,512,128]{3,2,1,0:T(8,128)(2,1)} %param.26) | copy-start | bytes 393220
  9.5 22.5 %collective-permute-start = (bf16[1,128,128]{1,2,0:T(8,128)(2,1)S(1)}, bf16[1,128,128]{1,2,0:T(8,128)(2,1)S(1)}, u32[]{:S(2)}, u32[]{:S(2)}) collective-permute-start(bf16[1,128,128]{1,2,0:T(8,128)(2,1)S(1)} %copy.88), channel_id=1, source_target_pairs={{0,32},{32,64},{64,96},{96,128},{128,160},{160,192},{192,224},{224... | collective-permute-start | bytes 98312 | tf_op jit(solution)/shard_map/ppermute | solution.py:24
  14.1 17.9 %collective-permute-start.1 = (bf16[1,128,128]{1,2,0:T(8,128)(2,1)S(1)}, bf16[1,128,128]{1,2,0:T(8,128)(2,1)S(1)}, u32[]{:S(2)}, u32[]{:S(2)}) collective-permute-start(bf16[1,128,128]{1,2,0:T(8,128)(2,1)S(1)} %copy.89), channel_id=1, source_target_pairs={{32,0},{64,32},{96,64},{128,96},{160,128},{192,160},{224,192},{256... | collective-permute-start | bytes 98312 | tf_op jit(solution)/shard_map/ppermute | solution.py:25
  19.8 12.2 %collective-permute-start.2 = (bf16[1,128,128]{1,2,0:T(8,128)(2,1)S(1)}, bf16[1,128,128]{1,2,0:T(8,128)(2,1)S(1)}, u32[]{:S(2)}, u32[]{:S(2)}) collective-permute-start(bf16[1,128,128]{1,2,0:T(8,128)(2,1)S(1)} %copy.90), channel_id=1, source_target_pairs={{0,1},{1,2},{2,3},{3,4},{4,5},{5,6},{6,7},{7,8},{8,9},{9,10},{10,1... | collective-permute-start | bytes 98312 | tf_op jit(solution)/shard_map/ppermute | solution.py:24
  21.3 10.8 %collective-permute-start.3 = (bf16[1,128,128]{1,2,0:T(8,128)(2,1)S(1)}, bf16[1,128,128]{1,2,0:T(8,128)(2,1)S(1)}, u32[]{:S(2)}, u32[]{:S(2)}) collective-permute-start(bf16[1,128,128]{1,2,0:T(8,128)(2,1)S(1)} %copy.91), channel_id=1, source_target_pairs={{1,0},{2,1},{3,2},{4,3},{5,4},{6,5},{7,6},{8,7},{9,8},{10,9},{11,1... | collective-permute-start | bytes 98312 | tf_op jit(solution)/shard_map/ppermute | solution.py:25
  22.9 2.1 copy-start.12
  25.0 16.1 %copy-start.106 = (f32[256]{0:T(256)}, f32[256]{0:T(256)S(1)}, u32[]{:S(2)}) copy-start(f32[256]{0:T(256)S(1)} %convert_reduce_fusion) | copy-start | bytes 3076
  25.0 2.0 copy-start.65
  26.9 60.4 %copy-start.98 = (f32[128]{0:T(128)}, f32[128]{0:T(128)S(1)}, u32[]{:S(2)}) copy-start(f32[128]{0:T(128)S(1)} %get-tuple-element.1067) | copy-start | bytes 1540
  42.2 45.1 %copy-start.10 = (bf16[256,128]{1,0:T(8,128)(2,1)}, bf16[256,128]{1,0:T(8,128)(2,1)S(1)}, u32[]{:S(2)}) copy-start(bf16[256,128]{1,0:T(8,128)(2,1)S(1)} %get-tuple-element.1073) | copy-start | bytes 196612
  43.0 12.6 %collective-permute-start.4 = (bf16[1,128,128]{2,1,0:T(8,128)(2,1)S(1)}, bf16[1,128,128]{2,1,0:T(8,128)(2,1)S(1)}, u32[]{:S(2)}, u32[]{:S(2)}) collective-permute-start(bf16[1,128,128]{2,1,0:T(8,128)(2,1)S(1)} %get-tuple-element.1061), channel_id=1, source_target_pairs={{0,32},{32,64},{64,96},{96,128},{128,160},{160,192},{192,224},{224... | collective-permute-start | bytes 98312 | tf_op jit(solution)/shard_map/ppermute | solution.py:24
  46.3 9.3 %collective-permute-start.5 = (bf16[1,128,128]{2,1,0:T(8,128)(2,1)S(1)}, bf16[1,128,128]{2,1,0:T(8,128)(2,1)S(1)}, u32[]{:S(2)}, u32[]{:S(2)}) collective-permute-start(bf16[1,128,128]{2,1,0:T(8,128)(2,1)S(1)} %get-tuple-element.1060), channel_id=1, source_target_pairs={{32,0},{64,32},{96,64},{128,96},{160,128},{192,160},{224,192},{256... | collective-permute-start | bytes 98312 | tf_op jit(solution)/shard_map/ppermute | solution.py:25
  48.3 7.4 %collective-permute-start.6 = (bf16[1,128,128]{2,1,0:T(8,128)(2,1)S(1)}, bf16[1,128,128]{2,1,0:T(8,128)(2,1)S(1)}, u32[]{:S(2)}, u32[]{:S(2)}) collective-permute-start(bf16[1,128,128]{2,1,0:T(8,128)(2,1)S(1)} %get-tuple-element.1059), channel_id=1, source_target_pairs={{0,1},{1,2},{2,3},{3,4},{4,5},{5,6},{6,7},{7,8},{8,9},{9,10},{10,1... | collective-permute-start | bytes 98312 | tf_op jit(solution)/shard_map/ppermute | solution.py:24
  54.3 7.1 %collective-permute-start.7 = (bf16[1,128,128]{2,1,0:T(8,128)(2,1)S(1)}, bf16[1,128,128]{2,1,0:T(8,128)(2,1)S(1)}, u32[]{:S(2)}, u32[]{:S(2)}) collective-permute-start(bf16[1,128,128]{2,1,0:T(8,128)(2,1)S(1)} %get-tuple-element.1058), channel_id=1, source_target_pairs={{1,0},{2,1},{3,2},{4,3},{5,4},{6,5},{7,6},{8,7},{9,8},{10,9},{11,1... | collective-permute-start | bytes 98312 | tf_op jit(solution)/shard_map/ppermute | solution.py:25
  87.9 5.9 copy-start.8
  88.6 15.1 %collective-permute-start.8 = (bf16[1,128,128]{2,1,0:T(8,128)(2,1)S(1)}, bf16[1,128,128]{2,1,0:T(8,128)(2,1)S(1)}, u32[]{:S(2)}, u32[]{:S(2)}) collective-permute-start(bf16[1,128,128]{2,1,0:T(8,128)(2,1)S(1)} %get-tuple-element.1057), channel_id=1, source_target_pairs={{0,32},{32,64},{64,96},{96,128},{128,160},{160,192},{192,224},{224... | collective-permute-start | bytes 98312 | tf_op jit(solution)/shard_map/ppermute | solution.py:24
  94.6 9.1 %collective-permute-start.9 = (bf16[1,128,128]{2,1,0:T(8,128)(2,1)S(1)}, bf16[1,128,128]{2,1,0:T(8,128)(2,1)S(1)}, u32[]{:S(2)}, u32[]{:S(2)}) collective-permute-start(bf16[1,128,128]{2,1,0:T(8,128)(2,1)S(1)} %get-tuple-element.1056), channel_id=1, source_target_pairs={{32,0},{64,32},{96,64},{128,96},{160,128},{192,160},{224,192},{256... | collective-permute-start | bytes 98312 | tf_op jit(solution)/shard_map/ppermute | solution.py:25
  96.5 7.2 %collective-permute-start.10 = (bf16[1,128,128]{2,1,0:T(8,128)(2,1)S(1)}, bf16[1,128,128]{2,1,0:T(8,128)(2,1)S(1)}, u32[]{:S(2)}, u32[]{:S(2)}) collective-permute-start(bf16[1,128,128]{2,1,0:T(8,128)(2,1)S(1)} %get-tuple-element.1055), channel_id=1, source_target_pairs={{0,1},{1,2},{2,3},{3,4},{4,5},{5,6},{6,7},{7,8},{8,9},{9,10},{10,1... | collective-permute-start | bytes 98312 | tf_op jit(solution)/shard_map/ppermute | solution.py:24
  101.9 5.6 collective-permute-start.11
  141.1 1.7 copy-start
  149.5 3.5 copy-start.55
  159.2 1.7 copy-start
  163.0 2.1 copy-start.43
  168.5 3.5 copy-start.55
  178.2 1.7 copy-start
  182.0 2.1 copy-start.43
  187.5 3.5 copy-start.55
  197.2 1.7 copy-start
  201.0 2.1 copy-start.43
  206.5 3.5 copy-start.55
  221.2 22.6 %collective-permute-start.12 = (bf16[1,128,128]{2,1,0:T(8,128)(2,1)S(1)}, bf16[1,128,128]{2,1,0:T(8,128)(2,1)S(1)}, u32[]{:S(2)}, u32[]{:S(2)}) collective-permute-start(bf16[1,128,128]{2,1,0:T(8,128)(2,1)S(1)} %get-tuple-element.1038), channel_id=1, source_target_pairs={{0,32},{32,64},{64,96},{96,128},{128,160},{160,192},{192,224},{224... | collective-permute-start | bytes 98312 | tf_op jit(solution)/shard_map/ppermute | solution.py:24
  226.3 17.5 %collective-permute-start.13 = (bf16[1,128,128]{2,1,0:T(8,128)(2,1)S(1)}, bf16[1,128,128]{2,1,0:T(8,128)(2,1)S(1)}, u32[]{:S(2)}, u32[]{:S(2)}) collective-permute-start(bf16[1,128,128]{2,1,0:T(8,128)(2,1)S(1)} %get-tuple-element.1041), channel_id=1, source_target_pairs={{32,0},{64,32},{96,64},{128,96},{160,128},{192,160},{224,192},{256... | collective-permute-start | bytes 98312 | tf_op jit(solution)/shard_map/ppermute | solution.py:25
  229.9 18.3 %copy-start.52 = (f32[5,128,128]{2,1,0:T(8,128)}, f32[5,128,128]{2,1,0:T(8,128)S(1)}, u32[]{:S(2)}) copy-start(f32[5,128,128]{2,1,0:T(8,128)S(1)} %fusion.58) | copy-start | bytes 983044
  229.9 13.9 %collective-permute-start.14 = (bf16[1,128,128]{2,1,0:T(8,128)(2,1)S(1)}, bf16[1,128,128]{2,1,0:T(8,128)(2,1)S(1)}, u32[]{:S(2)}, u32[]{:S(2)}) collective-permute-start(bf16[1,128,128]{2,1,0:T(8,128)(2,1)S(1)} %get-tuple-element.1040), channel_id=1, source_target_pairs={{0,1},{1,2},{2,3},{3,4},{4,5},{5,6},{6,7},{7,8},{8,9},{9,10},{10,1... | collective-permute-start | bytes 98312 | tf_op jit(solution)/shard_map/ppermute | solution.py:24
  242.3 5.8 collective-permute-start.15
  263.4 3.5 copy-start.57
  279.9 3.5 copy-start.57
  296.3 3.5 copy-start.57
  312.8 3.5 copy-start.57
  328.5 16.9 %collective-permute-start.16 = (bf16[1,128,128]{2,1,0:T(8,128)(2,1)S(1)}, bf16[1,128,128]{2,1,0:T(8,128)(2,1)S(1)}, u32[]{:S(2)}, u32[]{:S(2)}) collective-permute-start(bf16[1,128,128]{2,1,0:T(8,128)(2,1)S(1)} %get-tuple-element.1032), channel_id=1, source_target_pairs={{0,32},{32,64},{64,96},{96,128},{128,160},{160,192},{192,224},{224... | collective-permute-start | bytes 98312 | tf_op jit(solution)/shard_map/ppermute | solution.py:24
  333.3 12.1 %collective-permute-start.17 = (bf16[1,128,128]{2,1,0:T(8,128)(2,1)S(1)}, bf16[1,128,128]{2,1,0:T(8,128)(2,1)S(1)}, u32[]{:S(2)}, u32[]{:S(2)}) collective-permute-start(bf16[1,128,128]{2,1,0:T(8,128)(2,1)S(1)} %get-tuple-element.1035), channel_id=1, source_target_pairs={{32,0},{64,32},{96,64},{128,96},{160,128},{192,160},{224,192},{256... | collective-permute-start | bytes 98312 | tf_op jit(solution)/shard_map/ppermute | solution.py:25
  335.3 10.2 %collective-permute-start.18 = (bf16[1,128,128]{2,1,0:T(8,128)(2,1)S(1)}, bf16[1,128,128]{2,1,0:T(8,128)(2,1)S(1)}, u32[]{:S(2)}, u32[]{:S(2)}) collective-permute-start(bf16[1,128,128]{2,1,0:T(8,128)(2,1)S(1)} %get-tuple-element.1034), channel_id=1, source_target_pairs={{0,1},{1,2},{2,3},{3,4},{4,5},{5,6},{6,7},{7,8},{8,9},{9,10},{10,1... | collective-permute-start | bytes 98312 | tf_op jit(solution)/shard_map/ppermute | solution.py:24
  341.8 5.8 collective-permute-start.19
  344.5 6.8 copy-start.97
  351.4 2.2 copy-start.73
  353.8 2.2 copy-start.27
  688.5 1.8 copy-start.47
  (151 other events, 128.5 us)
Sparse Core Ops, SparseCore 0:
  376.3 312.1 all-reduce.3
where the time goes:
time: 712 us; the launch traced here: 698 us
  waiting for transfers between devices  186 us (26%)
  blocking collectives  140 us (20%)
  other arithmetic  108 us (15%)
  local copies, waits for them, and re-layouts  107 us (15%)
  starting transfers between devices  74.8 us (11%)
  matrix products  63.9 us (9%)
  between operations  16.6 us (2%)
    psum x1, waiting for transfers between devices, body(): lax.psum((fine_terms[0], fine_terms[1], fine_terms[2], coarse_stacked[0],...  170 us
    psum x1, blocking collectives, body(): lax.psum((fine_terms[0], fine_terms[1], fine_terms[2], coarse_stacked[0],...  140 us
    ppermute x10, starting transfers between devices, extended_2(): before = lax.ppermute(last, axis, up)  54.4 us
    scatter-add x9, other arithmetic, one_turn(): grad_send.at[senders].add(grad_act)  31.1 us
    scatter-add x9, other arithmetic, one_turn(): grad_recv.at[receivers].add(grad_act)  30.3 us
    scatter-add x9, other arithmetic, one_turn(): return running.at[receivers].add(message)  30.3 us
    unnamed x210, local copies, waits for them, and re-layouts  29.4 us
    while x168, local copies, waits for them, and re-layouts  22.1 us
  transfers between devices with their start and end apart: 21, of which 5 were waited for; matrix products, arithmetic and copies ran while one was open for 2% of the time, Pallas kernels for 0%

commit v1 on v0

v1 whole, which is shorter than its diff:
```python
import functools
import math

import jax
import jax.numpy as jnp
from jax import lax
from jax.experimental import pallas as pl
from jax.experimental.pallas import tpu as pltpu
from jax.sharding import PartitionSpec as P

BLOCK = 128
H = 128
COARSE_STEPS = 2
NC_DEV = 256
CHUNK = 256
GRAD_ROWS = 5 * H + 8
EPSILON = 1e-05
F32 = jnp.float32
BF16 = jnp.bfloat16


def halves(values):
    high = values.astype(BF16)
    low = (values - high.astype(F32)).astype(BF16)
    return jnp.concatenate([high, low], axis=1)


def joined(values):
    return values[:, :H] + values[:, H:]


def matmul(left, right):
    return jnp.dot(left, right, preferred_element_type=F32)


def matmul_nt(left, right):
    return lax.dot_general(left, right, (((1,), (1,)), ((), ())), preferred_element_type=F32)


def matmul_tn(left, right):
    return lax.dot_general(left, right, (((0,), (0,)), ((), ())), preferred_element_type=F32)


def twice(weight):
    return jnp.concatenate([weight, weight], axis=1)


def column_of(row):
    pieces = []
    for start in range(0, row.shape[1], 128):
        wide = jnp.broadcast_to(row[:, start : start + 128], (128, 128))
        pieces.append(wide.T)
    return pieces[0] if len(pieces) == 1 else jnp.concatenate(pieces, axis=0)


def one_hot_rows(row, width):
    spread = column_of(row)
    spread = spread - lax.broadcasted_iota(jnp.int32, spread.shape, 1)
    tiles = [jnp.where(spread == start, 1.0, 0.0).astype(BF16) for start in range(0, width, 128)]
    return jnp.concatenate(tiles, axis=1)


def one_hot_columns(row, first, count):
    shape = (count, row.shape[1])
    marks = lax.broadcasted_iota(jnp.int32, shape, 0) + first == jnp.broadcast_to(row, shape)
    return jnp.where(marks, 1.0, 0.0).astype(BF16)


def normalise(node_pre):
    centred = node_pre - jnp.mean(node_pre, axis=1, keepdims=True)
    spread = jnp.mean(centred * centred, axis=1, keepdims=True)
    scale = lax.rsqrt(spread + EPSILON)
    return centred * scale, scale


def forward_step(x, halos, senders, receivers, weights, bias, gain, hidden_ref, slope_ref):
    rows = x.shape[0]
    slots = senders.shape[1]
    extended = jnp.concatenate([x] + halos, axis=0)
    width = extended.shape[0]
    projected = jnp.concatenate(
        [halves(matmul(extended, weights[0])), halves(matmul(x, weights[1]))], axis=0
    )
    for first in range(0, slots, CHUNK):
        marks = jnp.concatenate(
            [
                one_hot_rows(senders[:, first : first + CHUNK], width),
                one_hot_rows(receivers[:, first : first + CHUNK], rows),
            ],
            axis=1,
        )
        pre_act = joined(matmul(marks, projected)) + bias
        sigmoid = jax.nn.sigmoid(pre_act)
        hidden_ref[first : first + CHUNK, :] = (pre_act * sigmoid).astype(BF16)
        slope_ref[first : first + CHUNK, :] = sigmoid * (1.0 + pre_act * (1.0 - sigmoid))
    hidden = hidden_ref[...]
    gathered = jnp.concatenate(
        [
            matmul(one_hot_columns(receivers, first, CHUNK), hidden)
            for first in range(0, rows, CHUNK)
        ],
        axis=0,
    )
    edge_sums = halves(gathered)
    agg = matmul(edge_sums, jnp.concatenate([weights[2], weights[2]], axis=0)).astype(BF16)
    both = jnp.concatenate([x, agg], axis=1)
    node_pre = matmul(both, jnp.concatenate([weights[3], weights[4]], axis=0))
    normed, _ = normalise(node_pre)
    output = (x.astype(F32) + gain * normed).astype(BF16)
    return output, edge_sums, agg, node_pre


def backward_step(
    upstream,
    x,
    halos,
    senders,
    receivers,
    weights,
    gain,
    edge_sums,
    agg,
    node_pre,
    slope_ref,
    act_ref,
    grads_ref,
    want_input,
):
    rows = x.shape[0]
    slots = senders.shape[1]
    normed, scale = normalise(node_pre)
    grad_gain = jnp.sum(upstream * normed, axis=0, keepdims=True)
    seed = upstream * gain
    grad_pre = scale * (
        seed
        - jnp.mean(seed, axis=1, keepdims=True)
        - normed * jnp.mean(seed * normed, axis=1, keepdims=True)
    )
    pre_parts = halves(grad_pre)
    both = jnp.concatenate([x, agg], axis=1)
    terms = joined(matmul_tn(both, pre_parts))
    grads_ref[3 * H : 5 * H, :] = terms
    back = matmul_nt(pre_parts, jnp.concatenate([twice(weights[4]), twice(weights[3])], axis=0))
    agg_parts = halves(back[:, :H])
    quads = matmul_tn(edge_sums, agg_parts)
    grads_ref[2 * H : 3 * H, :] = joined(quads[:H] + quads[H:])
    message_parts = halves(matmul_nt(agg_parts, twice(weights[2])))
    for first in range(0, slots, CHUNK):
        marks = one_hot_rows(receivers[:, first : first + CHUNK], rows)
        grad_act = joined(matmul(marks, message_parts)) * slope_ref[first : first + CHUNK, :]
        act_ref[first : first + CHUNK, :] = halves(grad_act)
    act = act_ref[...]
    extended = jnp.concatenate([x] + halos, axis=0)
    width = extended.shape[0]
    send_parts = halves(
        jnp.concatenate(
            [
                joined(matmul(one_hot_columns(senders, first, CHUNK), act))
                for first in range(0, width, CHUNK)
            ],
            axis=0,
        )
    )
    grad_recv = jnp.concatenate(
        [
            joined(matmul(one_hot_columns(receivers, first, CHUNK), act))
            for first in range(0, rows, CHUNK)
        ],
        axis=0,
    )
    recv_parts = halves(grad_recv)
    grads_ref[0:H, :] = joined(matmul_tn(extended, send_parts))
    grads_ref[H : 2 * H, :] = joined(matmul_tn(x, recv_parts))
    grad_bias = jnp.sum(grad_recv, axis=0, keepdims=True)
    grads_ref[5 * H :, :] = jnp.concatenate(
        [grad_bias, grad_gain, jnp.zeros((GRAD_ROWS - 5 * H - 2, H), F32)], axis=0
    )
    if not want_input:
        return None, None
    grad_ext = matmul_nt(send_parts, twice(weights[0]))
    grad_nodes = (
        upstream + back[:, H:] + matmul_nt(recv_parts, twice(weights[1])) + grad_ext[:rows]
    )
    return grad_nodes, grad_ext[rows:]


def pool_counts(pool_row):
    shape = (NC_DEV, pool_row.shape[1])
    marks = lax.broadcasted_iota(jnp.int32, shape, 0) == jnp.broadcast_to(pool_row, shape)
    return jnp.sum(jnp.where(marks, 1.0, 0.0), axis=1, keepdims=True)


def send_blocks(source_ref, blocks_ref, out_refs):
    for direction, out_ref in enumerate(out_refs):
        start = pl.multiple_of(blocks_ref[direction] * BLOCK, BLOCK)
        out_ref[...] = source_ref[pl.ds(start, BLOCK), :]


def live_receivers(edges_ref, live_ref):
    receivers = edges_ref[1:2, :]
    slot = lax.broadcasted_iota(jnp.int32, receivers.shape, 1)
    return jnp.where(slot < live_ref[0], receivers, -1)


def fine_ahead(
    live_ref, blocks_ref, x_ref, h0, h1, h2, h3, edges_ref, pool_ref, w_ref, bias_ref, gain_ref,
    mid_ref, coarse_ref, s0, s1, s2, s3, sums_ref, agg_ref, pre_ref, slope_ref,
    hidden_ref,
):
    output, edge_sums, agg, node_pre = forward_step(
        x_ref[...],
        [h0[...], h1[...], h2[...], h3[...]],
        edges_ref[0:1, :],
        live_receivers(edges_ref, live_ref),
        w_ref,
        bias_ref[...],
        gain_ref[...],
        hidden_ref,
        slope_ref,
    )
    mid_ref[...] = output
    sums_ref[...] = edge_sums
    agg_ref[...] = agg
    pre_ref[...] = node_pre
    pool_row = pool_ref[...]
    pooled = matmul(one_hot_columns(pool_row, 0, NC_DEV), output)
    coarse_ref[...] = (pooled / pool_counts(pool_row)).astype(BF16)
    send_blocks(coarse_ref, blocks_ref, (s0, s1, s2, s3))


def coarse_ahead(
    blocks_ref, x_ref, h0, h1, h2, h3, edges_ref, w_ref, bias_ref, gain_ref,
    out_ref, s0, s1, s2, s3, sums_ref, agg_ref, pre_ref, slope_ref,
    hidden_ref,
):
    output, edge_sums, agg, node_pre = forward_step(
        x_ref[...],
        [h0[...], h1[...], h2[...], h3[...]],
        edges_ref[0:1, :],
        edges_ref[1:2, :],
        w_ref.at[0],
        bias_ref[0:1, :],
        gain_ref[0:1, :],
        hidden_ref,
        slope_ref,
    )
    out_ref[...] = output
    sums_ref[...] = edge_sums
    agg_ref[...] = agg
    pre_ref[...] = node_pre
    send_blocks(out_ref, blocks_ref, (s0, s1, s2, s3))


def put_halo_grads(grad_halo, out_refs):
    for group, out_ref in enumerate(out_refs):
        out_ref[...] = grad_halo[group * BLOCK : (group + 1) * BLOCK].astype(BF16)


def coarse_turn(
    loss_scale, x_ref, h0, h1, h2, h3, edges_ref, w_ref, bias_ref, gain_ref, pool_ref, mid_ref, cot_ref,
    out_ref, grad_ref, g0, g1, g2, g3, grads_ref,
    hidden_ref, slope_ref, act_ref,
):
    x = x_ref[...]
    halos = [h0[...], h1[...], h2[...], h3[...]]
    senders, receivers = edges_ref[0:1, :], edges_ref[1:2, :]
    gain = gain_ref[1:2, :]
    weights = w_ref.at[1]
    output, edge_sums, agg, node_pre = forward_step(
        x, halos, senders, receivers, weights, bias_ref[1:2, :], gain, hidden_ref, slope_ref
    )
    pool_row = pool_ref[...]
    lifted = matmul(one_hot_rows(pool_row, NC_DEV), output)
    out_ref[...] = (mid_ref[...].astype(F32) + lifted).astype(BF16)
    upstream = matmul(one_hot_columns(pool_row, 0, NC_DEV), cot_ref[...]) * loss_scale
    grad_nodes, grad_halo = backward_step(
        upstream, x, halos, senders, receivers, weights, gain, edge_sums, agg, node_pre,
        slope_ref, act_ref, grads_ref, True,
    )
    grad_ref[...] = grad_nodes
    put_halo_grads(grad_halo, (g0, g1, g2, g3))


def add_returned(grad_ref, returned, blocks_ref, total_ref):
    total_ref[...] = grad_ref[...]
    for direction, piece in enumerate(returned):
        start = pl.multiple_of(blocks_ref[direction] * BLOCK, BLOCK)
        total_ref[pl.ds(start, BLOCK), :] += piece[...].astype(F32)


def coarse_behind(
    blocks_ref, grad_in_ref, r0, r1, r2, r3, x_ref, h0, h1, h2, h3, edges_ref, w_ref, gain_ref,
    sums_ref, agg_ref, pre_ref, slope_ref,
    grad_ref, g0, g1, g2, g3, grads_ref,
    total_ref, act_ref,
):
    add_returned(grad_in_ref, (r0, r1, r2, r3), blocks_ref, total_ref)
    grad_nodes, grad_halo = backward_step(
        total_ref[...],
        x_ref[...],
        [h0[...], h1[...], h2[...], h3[...]],
        edges_ref[0:1, :],
        edges_ref[1:2, :],
        w_ref.at[0],
        gain_ref[0:1, :],
        sums_ref[...],
        agg_ref[...],
        pre_ref[...],
        slope_ref,
        act_ref,
        grads_ref,
        True,
    )
    grad_ref[...] = grad_nodes
    put_halo_grads(grad_halo, (g0, g1, g2, g3))


def fine_behind(
    loss_scale, root, live_ref, blocks_ref, grad_in_ref, r0, r1, r2, r3, x_ref, h0, h1, h2, h3, edges_ref,
    pool_ref, cot_ref, w_ref, gain_ref, sums_ref, agg_ref, pre_ref, slope_ref,
    pooled_ref, grads_ref,
    total_ref, act_ref,
):
    add_returned(grad_in_ref, (r0, r1, r2, r3), blocks_ref, total_ref)
    total = total_ref[...]
    pooled_ref[...] = total * root
    pool_row = pool_ref[...]
    shared = halves(total / pool_counts(pool_row))
    upstream = cot_ref[...].astype(F32) * loss_scale + joined(
        matmul(one_hot_rows(pool_row, NC_DEV), shared)
    )
    backward_step(
        upstream,
        x_ref[...],
        [h0[...], h1[...], h2[...], h3[...]],
        edges_ref[0:1, :],
        live_receivers(edges_ref, live_ref),
        w_ref,
        gain_ref[...],
        sums_ref[...],
        agg_ref[...],
        pre_ref[...],
        slope_ref,
        act_ref,
        grads_ref,
        False,
    )


def call(kernel, scalars, arrays, outs, scratch):
    vmem = pl.BlockSpec(memory_space=pltpu.VMEM)
    smem = pl.BlockSpec(memory_space=pltpu.SMEM)
    return pl.pallas_call(
        kernel,
        out_shape=[jax.ShapeDtypeStruct(shape, dtype) for shape, dtype in outs],
        in_specs=[smem] * len(scalars) + [vmem] * len(arrays),
        out_specs=[vmem] * len(outs),
        scratch_shapes=[pltpu.VMEM(shape, dtype) for shape, dtype in scratch],
        compiler_params=pltpu.CompilerParams(vmem_limit_bytes=40 * 1024 * 1024),
    )(*scalars, *arrays)


def exchange(pieces):
    received = []
    for axis, (lower, upper) in (("gx", pieces[0:2]), ("gy", pieces[2:4])):
        peers = lax.axis_size(axis)
        up = [(i, i + 1) for i in range(peers - 1)]
        down = [(i + 1, i) for i in range(peers - 1)]
        received.append(lax.ppermute(upper, axis, up))
        received.append(lax.ppermute(lower, axis, down))
    return received


def reduce_all(terms):
    return lax.psum(terms, ("gx", "gy"))


def body(
    fine_nodes,
    fine_edges,
    fine_live,
    fine_halo,
    pool_map,
    coarse_edges,
    coarse_halo,
    fine_weights,
    fine_bias,
    fine_gain,
    coarse_weights,
    coarse_bias,
    coarse_gain,
    cotangent,
):
    x = fine_nodes[0, 0]
    edges = fine_edges[0, 0]
    live = fine_live.reshape(1)
    pool = pool_map[0]
    coarse_list = coarse_edges[0, 0]
    blocks = coarse_halo.reshape(4)
    cot = cotangent[0, 0]
    bias = fine_bias.reshape(1, H)
    gain = fine_gain.reshape(1, H)
    rows, slots, coarse_slots = x.shape[0], edges.shape[1], coarse_list.shape[1]
    total_nodes = rows * lax.axis_size("gx") * lax.axis_size("gy")
    root = math.sqrt(total_nodes)
    block = ((BLOCK, H), BF16)

    def saved(count, edge_count):
        return [
            ((count, 2 * H), BF16),
            ((count, H), BF16),
            ((count, H), F32),
            ((edge_count, H), F32),
        ]

    picks = fine_halo.reshape(4)
    sends = [
        lax.dynamic_slice_in_dim(x, picks[direction] * BLOCK, BLOCK) for direction in range(4)
    ]
    halos = exchange(sends)
    fine_out = call(
        fine_ahead,
        [live, blocks],
        [x, *halos, edges, pool, fine_weights, bias, gain],
        [((rows, H), BF16), ((NC_DEV, H), BF16)] + [block] * 4 + saved(rows, slots),
        [((slots, H), BF16)],
    )
    mid, coarse_0, sends, fine_saved = fine_out[0], fine_out[1], fine_out[2:6], fine_out[6:]
    halos_0 = exchange(sends)
    ahead = call(
        coarse_ahead,
        [blocks],
        [coarse_0, *halos_0, coarse_list, coarse_weights, coarse_bias, coarse_gain],
        [((NC_DEV, H), BF16)] + [block] * 4 + saved(NC_DEV, coarse_slots),
        [((coarse_slots, H), BF16)],
    )
    coarse_1, sends, coarse_saved = ahead[0], ahead[1:5], ahead[5:]
    halos_1 = exchange(sends)
    grads = ((GRAD_ROWS, H), F32)
    turned = call(
        functools.partial(coarse_turn, 1.0 / root),
        [],
        [coarse_1, *halos_1, coarse_list, coarse_weights, coarse_bias, coarse_gain, pool, mid, cot],
        [((rows, H), BF16), ((NC_DEV, H), F32)] + [block] * 4 + [grads],
        [((coarse_slots, H), BF16), ((coarse_slots, H), F32), ((coarse_slots, 2 * H), BF16)],
    )
    result, grad_nodes, grad_halo, grads_1 = turned[0], turned[1], turned[2:6], turned[6]
    returned = exchange(grad_halo)
    behind = call(
        coarse_behind,
        [blocks],
        [grad_nodes, *returned, coarse_0, *halos_0, coarse_list]
        + [coarse_weights, coarse_gain, *coarse_saved],
        [((NC_DEV, H), F32)] + [block] * 4 + [grads],
        [((NC_DEV, H), F32), ((coarse_slots, 2 * H), BF16)],
    )
    grad_nodes, grad_halo, grads_0 = behind[0], behind[1:5], behind[5]
    returned = exchange(grad_halo)
    grad_pooled, grads_f = call(
        functools.partial(fine_behind, 1.0 / root, root),
        [live, blocks],
        [grad_nodes, *returned, x, *halos, edges, pool, cot, fine_weights, gain, *fine_saved],
        [((NC_DEV, H), F32), grads],
        [((NC_DEV, H), F32), ((slots, 2 * H), BF16)],
    )
    total = reduce_all(jnp.concatenate([grads_f, grads_0, grads_1], axis=0))
    total = total.reshape(3, GRAD_ROWS, H)
    weights = total[:, : 5 * H].reshape(3, 5, H, H)
    return (
        result[None, None],
        weights[0],
        total[0, 5 * H],
        total[0, 5 * H + 1],
        weights[1:],
        total[1:, 5 * H],
        total[1:, 5 * H + 1],
        grad_pooled[None, None],
    )


def solution(mesh):
    tiled = P("gx", "gy", None, None)
    return jax.shard_map(
        body,
        mesh=mesh,
        in_specs=(
            tiled,
            tiled,
            P("gx", "gy"),
            tiled,
            P("gx", "gy", None),
            tiled,
            tiled,
            P(),
            P(),
            P(),
            P(),
            P(),
            P(),
            tiled,
        ),
        out_specs=(tiled, P(), P(), P(), P(), P(), P(), tiled),
        check_vma=False,
    )
```

time: 712 us -> 419 us (0.59); the launches traced: 698 us -> 418 us
  blocking collectives: 140 us -> 0 us
  waiting for transfers between devices: 186 us -> 303 us
  other arithmetic: 108 us -> 1.01 us
  local copies, waits for them, and re-layouts: 107 us -> 9.33 us
  matrix products: 63.9 us -> 0 us
  Pallas kernels: 0 us -> 17.7 us
    psum x1 -> x0, blocking collectives: 140 us -> none  [body(): lax.psum((fine_terms[0], fine_terms[1], fine_terms[2], coarse_stacked[0],...]
    psum x1, waiting for transfers between devices: 170 us -> 285 us  [reduce_all(): return lax.psum(terms, ('gx', 'gy'))]
    scatter-add x30 -> x0, other arithmetic: 96.1 us -> none  [the longest x9 31.1 us: one_turn(): grad_send.at[senders].add(grad_act)]
    dot_general x101 -> x0, matrix products: 63.9 us -> none  [the longest x18 21.8 us: times_transpose(): lax.dot_general(low, weight, numbers, preferred_element_type=jnp.float32)]
    gather x50 -> x0, local copies, waits for them, and re-layouts: 52.8 us -> none  [the longest x18 21.1 us: one_turn(): pre_act = proj_send[senders] + proj_recv[receivers] + edge_bias]
    unnamed x210 -> x24, local copies, waits for them, and re-layouts: 29.4 us -> 0.73 us
    while x168 -> x0, local copies, waits for them, and re-layouts: 22.1 us -> none
    pallas_call x0 -> x5, Pallas kernels: none -> 17.7 us  [call(): pl.pallas_call(kernel, out_shape=[jax.ShapeDtypeStruct(shape, dtype) for...]
  transfers between devices with their start and end apart: 21 -> 21, of which waited for: 5 -> 6; matrix products, arithmetic and copies ran while one was open for 2% -> 0% of each run, Pallas kernels for 0% -> 0%
where the time goes in v1:
time: 419 us; the launch traced here: 418 us
  waiting for transfers between devices  303 us (72%)
  starting transfers between devices  68.7 us (16%)
  between operations  17.8 us (4%)
  Pallas kernels  17.7 us (4%)
  local copies, waits for them, and re-layouts  9.33 us (2%)
    psum x1, waiting for transfers between devices, reduce_all(): return lax.psum(terms, ('gx', 'gy'))  285 us
    ppermute x10, starting transfers between devices, exchange(): received.append(lax.ppermute(upper, axis, up))  44.9 us
    ppermute x10, starting transfers between devices, exchange(): received.append(lax.ppermute(lower, axis, down))  23.8 us
    pallas_call x5, Pallas kernels, call(): pl.pallas_call(kernel, out_shape=[jax.ShapeDtypeStruct(shape, dtype) for...  17.7 us
    ppermute x10, waiting for transfers between devices, exchange(): received.append(lax.ppermute(lower, axis, down))  17.6 us
  transfers between devices with their start and end apart: 21, of which 6 were waited for; matrix products, arithmetic and copies ran while one was open for 0% of the time, Pallas kernels for 0%

profile of v1, /device:TPU:1, one launch (start us, length us, event | category | flops | bytes accessed | tf_op | source)
XLA Modules:
  0.0 417.9 jit_solution(15085979607353996078)
XLA Ops:
  7.2 0.0 all-reduce.2.cloned.1.call-start
  7.2 1.4 fusion.1
  9.3 0.0 copy-start.2
  11.3 0.0 copy-start.8
  11.3 0.0 copy-start.10
  11.3 0.0 copy-start.5
  11.3 0.0 copy-start
  11.4 0.9 dynamic-slice_bitcast_fusion
  12.3 1.3 collective-permute-start.3
  13.6 8.8 %collective-permute-start.1 = (bf16[128,128]{1,0:T(8,128)(2,1)S(1)}, bf16[128,128]{1,0:T(8,128)(2,1)S(1)}, u32[]{:S(2)}, u32[]{:S(2)}) collective-permute-start(bf16[128,128]{1,0:T(8,128)(2,1)S(1)} %get-tuple-element.81), channel_id=1, source_target_pairs={{32,0},{64,32},{96,64},{128,96},{160,128},{192,160},{224,192},{256... | collective-permute-start | bytes 98312 | tf_op jit(solution)/shard_map/ppermute | solution.py:370
  22.4 1.9 collective-permute-start
  24.3 5.2 %collective-permute-start.2 = (bf16[128,128]{1,0:T(8,128)(2,1)S(1)}, bf16[128,128]{1,0:T(8,128)(2,1)S(1)}, u32[]{:S(2)}, u32[]{:S(2)}) collective-permute-start(bf16[128,128]{1,0:T(8,128)(2,1)S(1)} %get-tuple-element.83), channel_id=1, source_target_pairs={{0,1},{1,2},{2,3},{3,4},{4,5},{5,6},{6,7},{7,8},{8,9},{9,10},{10,1... | collective-permute-start | bytes 98312 | tf_op jit(solution)/shard_map/ppermute | solution.py:369
  30.1 0.3 collective-permute-done.2.h2
  30.5 0.0 copy-start.4
  30.5 3.4 shard_map.197
  33.9 0.0 copy-start.9
  33.9 1.9 collective-permute-start.4
  35.8 2.6 collective-permute-start.5
  38.5 5.0 %collective-permute-start.6 = (bf16[128,128]{1,0:T(8,128)(2,1)S(1)}, bf16[128,128]{1,0:T(8,128)(2,1)S(1)}, u32[]{:S(2)}, u32[]{:S(2)}) collective-permute-start(bf16[128,128]{1,0:T(8,128)(2,1)S(1)} %get-tuple-element.45), channel_id=1, source_target_pairs={{0,1},{1,2},{2,3},{3,4},{4,5},{5,6},{6,7},{7,8},{8,9},{9,10},{10,1... | collective-permute-start | bytes 98312 | tf_op jit(solution)/shard_map/ppermute | solution.py:369
  43.4 1.3 collective-permute-start.7
  44.8 4.8 %collective-permute-done.7.h3 = bf16[128,128]{1,0:T(8,128)(2,1)S(1)} collective-permute-done((bf16[128,128]{1,0:T(8,128)(2,1)S(1)}, bf16[128,128]{1,0:T(8,128)(2,1)S(1)}, u32[]{:S(2)}, u32[]{:S(2)}) %collective-permute-start.7) | collective-permute-done | bytes 32800 | tf_op jit(solution)/shard_map/ppermute | solution.py:370
  49.6 0.7 copy-done.7
  50.2 2.8 shard_map.198
  53.1 3.8 collective-permute-start.8
  56.8 1.9 collective-permute-start.9
  58.8 5.5 %collective-permute-start.10 = (bf16[128,128]{1,0:T(8,128)(2,1)S(1)}, bf16[128,128]{1,0:T(8,128)(2,1)S(1)}, u32[]{:S(2)}, u32[]{:S(2)}) collective-permute-start(bf16[128,128]{1,0:T(8,128)(2,1)S(1)} %get-tuple-element.50), channel_id=1, source_target_pairs={{0,1},{1,2},{2,3},{3,4},{4,5},{5,6},{6,7},{7,8},{8,9},{9,10},{10,1... | collective-permute-start | bytes 98312 | tf_op jit(solution)/shard_map/ppermute | solution.py:369
  64.2 1.3 collective-permute-start.11
  65.6 4.2 %collective-permute-done.11.h3 = bf16[128,128]{1,0:T(8,128)(2,1)S(1)} collective-permute-done((bf16[128,128]{1,0:T(8,128)(2,1)S(1)}, bf16[128,128]{1,0:T(8,128)(2,1)S(1)}, u32[]{:S(2)}, u32[]{:S(2)}) %collective-permute-start.11) | collective-permute-done | bytes 32800 | tf_op jit(solution)/shard_map/ppermute | solution.py:370
  69.8 5.1 %shard_map.199 = (bf16[512,128]{1,0:T(8,128)(2,1)}, f32[256,128]{1,0:T(8,128)S(1)}, bf16[128,128]{1,0:T(8,128)(2,1)S(1)}, bf16[128,128]{1,0:T(8,128)(2,1)S(1)}, ...) custom-call(bf16[256,128]{1,0:T(8,128)(2,1)S(1)} %get-tuple-element.47.x_ref, ...), custom_call_target="tpu_custom_call" | custom-call | tf_op jit(solution)/shard_map/pallas_call | solution.py:353
  74.9 5.4 %collective-permute-start.12 = (bf16[128,128]{1,0:T(8,128)(2,1)S(1)}, bf16[128,128]{1,0:T(8,128)(2,1)S(1)}, u32[]{:S(2)}, u32[]{:S(2)}) collective-permute-start(bf16[128,128]{1,0:T(8,128)(2,1)S(1)} %get-tuple-element.55), channel_id=1, source_target_pairs={{0,32},{32,64},{64,96},{96,128},{128,160},{160,192},{192,224},{224... | collective-permute-start | bytes 98312 | tf_op jit(solution)/shard_map/ppermute | solution.py:369
  80.4 1.9 collective-permute-start.13
  82.3 5.7 %collective-permute-start.14 = (bf16[128,128]{1,0:T(8,128)(2,1)S(1)}, bf16[128,128]{1,0:T(8,128)(2,1)S(1)}, u32[]{:S(2)}, u32[]{:S(2)}) collective-permute-start(bf16[128,128]{1,0:T(8,128)(2,1)S(1)} %get-tuple-element.57), channel_id=1, source_target_pairs={{0,1},{1,2},{2,3},{3,4},{4,5},{5,6},{6,7},{7,8},{8,9},{9,10},{10,1... | collective-permute-start | bytes 98312 | tf_op jit(solution)/shard_map/ppermute | solution.py:369
  88.0 1.5 collective-permute-start.15
  89.5 4.3 %collective-permute-done.15.r3 = bf16[128,128]{1,0:T(8,128)(2,1)S(1)} collective-permute-done((bf16[128,128]{1,0:T(8,128)(2,1)S(1)}, bf16[128,128]{1,0:T(8,128)(2,1)S(1)}, u32[]{:S(2)}, u32[]{:S(2)}) %collective-permute-start.15) | collective-permute-done | bytes 32800 | tf_op jit(solution)/shard_map/ppermute | solution.py:370
  93.9 3.0 shard_map.200
  96.9 4.9 %collective-permute-start.16 = (bf16[128,128]{1,0:T(8,128)(2,1)S(1)}, bf16[128,128]{1,0:T(8,128)(2,1)S(1)}, u32[]{:S(2)}, u32[]{:S(2)}) collective-permute-start(bf16[128,128]{1,0:T(8,128)(2,1)S(1)} %get-tuple-element.64), channel_id=1, source_target_pairs={{0,32},{32,64},{64,96},{96,128},{128,160},{160,192},{192,224},{224... | collective-permute-start | bytes 98312 | tf_op jit(solution)/shard_map/ppermute | solution.py:369
  101.8 1.9 collective-permute-start.17
  103.7 5.6 %collective-permute-start.18 = (bf16[128,128]{1,0:T(8,128)(2,1)S(1)}, bf16[128,128]{1,0:T(8,128)(2,1)S(1)}, u32[]{:S(2)}, u32[]{:S(2)}) collective-permute-start(bf16[128,128]{1,0:T(8,128)(2,1)S(1)} %get-tuple-element.66), channel_id=1, source_target_pairs={{0,1},{1,2},{2,3},{3,4},{4,5},{5,6},{6,7},{7,8},{8,9},{9,10},{10,1... | collective-permute-start | bytes 98312 | tf_op jit(solution)/shard_map/ppermute | solution.py:369
  109.4 1.3 collective-permute-start.19
  110.7 4.2 %collective-permute-done.19.r3 = bf16[128,128]{1,0:T(8,128)(2,1)S(1)} collective-permute-done((bf16[128,128]{1,0:T(8,128)(2,1)S(1)}, bf16[128,128]{1,0:T(8,128)(2,1)S(1)}, u32[]{:S(2)}, u32[]{:S(2)}) %collective-permute-start.19) | collective-permute-done | bytes 32800 | tf_op jit(solution)/shard_map/ppermute | solution.py:370
  114.9 3.4 shard_map.201
  118.3 1.0 pad_maximum_fusion
  119.3 0.0 all-reduce.2.cloned.1.call-update
  119.3 285.4 %all-reduce.2.cloned.1.call-done = f32[3,648,128]{2,1,0:T(8,128)} async-done(((f32[3,648,128]{2,1,0:T(8,128)}), f32[3,648,128]{2,1,0:T(8,128)}) %all-reduce.2.cloned.1.call-update) | async-done | bytes 995344 | tf_op jit(solution)/shard_map/psum | solution.py:375
  404.8 1.3 slice_bitcast_fusion
  406.1 1.3 fusion
  407.4 1.7 slice.52
  409.1 2.0 slice.55
  (31 shorter events, 0.1 us)
Async XLA Ops:
  7.2 397.6 %all-reduce.2.cloned.1.call-start = ((), (), s32[]{:S(2)}) async-start(), calls=%async_computation | async-start | bytes 1990656 | tf_op jit(solution)/shard_map/psum | solution.py:375
  9.3 21.2 %copy-start.2 = (bf16[5,128,128]{2,1,0:T(8,128)(2,1)S(1)}, bf16[5,128,128]{2,1,0:T(8,128)(2,1)}, u32[]{:S(2)}) copy-start(bf16[5,128,128]{2,1,0:T(8,128)(2,1)} %w_ref.9) | copy-start | bytes 491524
  11.3 19.2 %copy-start.1 = (bf16[1,1,512,128]{3,2,1,0:T(8,128)(2,1)S(1)}, bf16[1,1,512,128]{3,2,1,0:T(8,128)(2,1)}, u32[]{:S(2)}) copy-start(bf16[1,1,512,128]{3,2,1,0:T(8,128)(2,1)} %param.14) | copy-start | bytes 393220
  11.3 19.2 %copy-start.6 = (s32[1,1,512]{2,1,0:T(1,128)S(1)}, s32[1,1,512]{2,1,0:T(1,128)}, u32[]{:S(2)}) copy-start(s32[1,1,512]{2,1,0:T(1,128)} %param.18) | copy-start | bytes 6148
  11.3 19.2 %copy-start.8 = (s32[1,1,4,1]{2,3,1,0:T(1,128)S(1)}, s32[1,1,4,1]{2,3,1,0:T(1,128)}, u32[]{:S(2)}) copy-start(s32[1,1,4,1]{2,3,1,0:T(1,128)} %param.20) | copy-start | bytes 52
  11.3 19.2 %copy-start.10 = (f32[128]{0:T(128)S(1)}, f32[128]{0:T(128)}, u32[]{:S(2)}) copy-start(f32[128]{0:T(128)} %param.23) | copy-start | bytes 1540
  11.3 19.2 %copy-start.11 = (f32[128]{0:T(128)S(1)}, f32[128]{0:T(128)}, u32[]{:S(2)}) copy-start(f32[128]{0:T(128)} %param.22) | copy-start | bytes 1540
  11.3 19.2 %copy-start.5 = (s32[1,1,2,1536]{3,2,1,0:T(2,128)S(1)}, s32[1,1,2,1536]{3,2,1,0:T(2,128)}, u32[]{:S(2)}) copy-start(s32[1,1,2,1536]{3,2,1,0:T(2,128)} %param.15) | copy-start | bytes 36868
  11.3 38.2 %copy-start = (bf16[2,5,128,128]{3,2,1,0:T(8,128)(2,1)S(1)}, bf16[2,5,128,128]{3,2,1,0:T(8,128)(2,1)}, u32[]{:S(2)}) copy-start(bf16[2,5,128,128]{3,2,1,0:T(8,128)(2,1)} %w_ref.8) | copy-start | bytes 983044
  12.3 17.8 %collective-permute-start.3 = (bf16[128,128]{1,0:T(8,128)(2,1)S(1)}, bf16[128,128]{1,0:T(8,128)(2,1)S(1)}, u32[]{:S(2)}, u32[]{:S(2)}) collective-permute-start(bf16[128,128]{1,0:T(8,128)(2,1)S(1)} %get-tuple-element.80), channel_id=1, source_target_pairs={{1,0},{2,1},{3,2},{4,3},{5,4},{6,5},{7,6},{8,7},{9,8},{10,9},{11,1... | collective-permute-start | bytes 98312 | tf_op jit(solution)/shard_map/ppermute | solution.py:370
  13.6 16.6 %collective-permute-start.1 = (bf16[128,128]{1,0:T(8,128)(2,1)S(1)}, bf16[128,128]{1,0:T(8,128)(2,1)S(1)}, u32[]{:S(2)}, u32[]{:S(2)}) collective-permute-start(bf16[128,128]{1,0:T(8,128)(2,1)S(1)} %get-tuple-element.81), channel_id=1, source_target_pairs={{32,0},{64,32},{96,64},{128,96},{160,128},{192,160},{224,192},{256... | collective-permute-start | bytes 98312 | tf_op jit(solution)/shard_map/ppermute | solution.py:370
  22.4 7.8 %collective-permute-start = (bf16[128,128]{1,0:T(8,128)(2,1)S(1)}, bf16[128,128]{1,0:T(8,128)(2,1)S(1)}, u32[]{:S(2)}, u32[]{:S(2)}) collective-permute-start(bf16[128,128]{1,0:T(8,128)(2,1)S(1)} %get-tuple-element.82), channel_id=1, source_target_pairs={{0,32},{32,64},{64,96},{96,128},{128,160},{160,192},{192,224},{224... | collective-permute-start | bytes 98312 | tf_op jit(solution)/shard_map/ppermute | solution.py:369
  24.3 6.2 %collective-permute-start.2 = (bf16[128,128]{1,0:T(8,128)(2,1)S(1)}, bf16[128,128]{1,0:T(8,128)(2,1)S(1)}, u32[]{:S(2)}, u32[]{:S(2)}) collective-permute-start(bf16[128,128]{1,0:T(8,128)(2,1)S(1)} %get-tuple-element.83), channel_id=1, source_target_pairs={{0,1},{1,2},{2,3},{3,4},{4,5},{5,6},{6,7},{7,8},{8,9},{9,10},{10,1... | collective-permute-start | bytes 98312 | tf_op jit(solution)/shard_map/ppermute | solution.py:369
  30.5 19.0 %copy-start.4 = (s32[1,1,2,2048]{3,2,1,0:T(2,128)S(1)}, s32[1,1,2,2048]{3,2,1,0:T(2,128)}, u32[]{:S(2)}) copy-start(s32[1,1,2,2048]{3,2,1,0:T(2,128)} %param.19) | copy-start | bytes 49156
  33.9 15.7 %copy-start.9 = (f32[2,128]{1,0:T(2,128)S(1)}, f32[2,128]{1,0:T(2,128)}, u32[]{:S(2)}) copy-start(f32[2,128]{1,0:T(2,128)} %bias_ref.3) | copy-start | bytes 3076
  33.9 10.9 %collective-permute-start.4 = (bf16[128,128]{1,0:T(8,128)(2,1)S(1)}, bf16[128,128]{1,0:T(8,128)(2,1)S(1)}, u32[]{:S(2)}, u32[]{:S(2)}) collective-permute-start(bf16[128,128]{1,0:T(8,128)(2,1)S(1)} %get-tuple-element.43), channel_id=1, source_target_pairs={{0,32},{32,64},{64,96},{96,128},{128,160},{160,192},{192,224},{224... | collective-permute-start | bytes 98312 | tf_op jit(solution)/shard_map/ppermute | solution.py:369
  35.8 8.9 %collective-permute-start.5 = (bf16[128,128]{1,0:T(8,128)(2,1)S(1)}, bf16[128,128]{1,0:T(8,128)(2,1)S(1)}, u32[]{:S(2)}, u32[]{:S(2)}) collective-permute-start(bf16[128,128]{1,0:T(8,128)(2,1)S(1)} %get-tuple-element.44), channel_id=1, source_target_pairs={{32,0},{64,32},{96,64},{128,96},{160,128},{192,160},{224,192},{256... | collective-permute-start | bytes 98312 | tf_op jit(solution)/shard_map/ppermute | solution.py:370
  38.5 6.3 %collective-permute-start.6 = (bf16[128,128]{1,0:T(8,128)(2,1)S(1)}, bf16[128,128]{1,0:T(8,128)(2,1)S(1)}, u32[]{:S(2)}, u32[]{:S(2)}) collective-permute-start(bf16[128,128]{1,0:T(8,128)(2,1)S(1)} %get-tuple-element.45), channel_id=1, source_target_pairs={{0,1},{1,2},{2,3},{3,4},{4,5},{5,6},{6,7},{7,8},{8,9},{9,10},{10,1... | collective-permute-start | bytes 98312 | tf_op jit(solution)/shard_map/ppermute | solution.py:369
  43.4 6.1 %collective-permute-start.7 = (bf16[128,128]{1,0:T(8,128)(2,1)S(1)}, bf16[128,128]{1,0:T(8,128)(2,1)S(1)}, u32[]{:S(2)}, u32[]{:S(2)}) collective-permute-start(bf16[128,128]{1,0:T(8,128)(2,1)S(1)} %get-tuple-element.46), channel_id=1, source_target_pairs={{1,0},{2,1},{3,2},{4,3},{5,4},{6,5},{7,6},{8,7},{9,8},{10,9},{11,1... | collective-permute-start | bytes 98312 | tf_op jit(solution)/shard_map/ppermute | solution.py:370
  49.5 0.7 copy-start.7
  50.2 19.6 %copy-start.3 = (bf16[1,1,512,128]{3,2,1,0:T(8,128)(2,1)S(1)}, bf16[1,1,512,128]{3,2,1,0:T(8,128)(2,1)}, u32[]{:S(2)}) copy-start(bf16[1,1,512,128]{3,2,1,0:T(8,128)(2,1)} %param.27) | copy-start | bytes 393220
  53.1 12.5 %collective-permute-start.8 = (bf16[128,128]{1,0:T(8,128)(2,1)S(1)}, bf16[128,128]{1,0:T(8,128)(2,1)S(1)}, u32[]{:S(2)}, u32[]{:S(2)}) collective-permute-start(bf16[128,128]{1,0:T(8,128)(2,1)S(1)} %get-tuple-element.48), channel_id=1, source_target_pairs={{0,32},{32,64},{64,96},{96,128},{128,160},{160,192},{192,224},{224... | collective-permute-start | bytes 98312 | tf_op jit(solution)/shard_map/ppermute | solution.py:369
  56.8 8.7 %collective-permute-start.9 = (bf16[128,128]{1,0:T(8,128)(2,1)S(1)}, bf16[128,128]{1,0:T(8,128)(2,1)S(1)}, u32[]{:S(2)}, u32[]{:S(2)}) collective-permute-start(bf16[128,128]{1,0:T(8,128)(2,1)S(1)} %get-tuple-element.49), channel_id=1, source_target_pairs={{32,0},{64,32},{96,64},{128,96},{160,128},{192,160},{224,192},{256... | collective-permute-start | bytes 98312 | tf_op jit(solution)/shard_map/ppermute | solution.py:370
  58.8 6.8 %collective-permute-start.10 = (bf16[128,128]{1,0:T(8,128)(2,1)S(1)}, bf16[128,128]{1,0:T(8,128)(2,1)S(1)}, u32[]{:S(2)}, u32[]{:S(2)}) collective-permute-start(bf16[128,128]{1,0:T(8,128)(2,1)S(1)} %get-tuple-element.50), channel_id=1, source_target_pairs={{0,1},{1,2},{2,3},{3,4},{4,5},{5,6},{6,7},{7,8},{8,9},{9,10},{10,1... | collective-permute-start | bytes 98312 | tf_op jit(solution)/shard_map/ppermute | solution.py:369
  64.2 5.6 %collective-permute-start.11 = (bf16[128,128]{1,0:T(8,128)(2,1)S(1)}, bf16[128,128]{1,0:T(8,128)(2,1)S(1)}, u32[]{:S(2)}, u32[]{:S(2)}) collective-permute-start(bf16[128,128]{1,0:T(8,128)(2,1)S(1)} %get-tuple-element.51), channel_id=1, source_target_pairs={{1,0},{2,1},{3,2},{4,3},{5,4},{6,5},{7,6},{8,7},{9,8},{10,9},{11,1... | collective-permute-start | bytes 98312 | tf_op jit(solution)/shard_map/ppermute | solution.py:370
  74.9 14.6 %collective-permute-start.12 = (bf16[128,128]{1,0:T(8,128)(2,1)S(1)}, bf16[128,128]{1,0:T(8,128)(2,1)S(1)}, u32[]{:S(2)}, u32[]{:S(2)}) collective-permute-start(bf16[128,128]{1,0:T(8,128)(2,1)S(1)} %get-tuple-element.55), channel_id=1, source_target_pairs={{0,32},{32,64},{64,96},{96,128},{128,160},{160,192},{192,224},{224... | collective-permute-start | bytes 98312 | tf_op jit(solution)/shard_map/ppermute | solution.py:369
  80.4 9.2 %collective-permute-start.13 = (bf16[128,128]{1,0:T(8,128)(2,1)S(1)}, bf16[128,128]{1,0:T(8,128)(2,1)S(1)}, u32[]{:S(2)}, u32[]{:S(2)}) collective-permute-start(bf16[128,128]{1,0:T(8,128)(2,1)S(1)} %get-tuple-element.56), channel_id=1, source_target_pairs={{32,0},{64,32},{96,64},{128,96},{160,128},{192,160},{224,192},{256... | collective-permute-start | bytes 98312 | tf_op jit(solution)/shard_map/ppermute | solution.py:370
  82.3 7.2 %collective-permute-start.14 = (bf16[128,128]{1,0:T(8,128)(2,1)S(1)}, bf16[128,128]{1,0:T(8,128)(2,1)S(1)}, u32[]{:S(2)}, u32[]{:S(2)}) collective-permute-start(bf16[128,128]{1,0:T(8,128)(2,1)S(1)} %get-tuple-element.57), channel_id=1, source_target_pairs={{0,1},{1,2},{2,3},{3,4},{4,5},{5,6},{6,7},{7,8},{8,9},{9,10},{10,1... | collective-permute-start | bytes 98312 | tf_op jit(solution)/shard_map/ppermute | solution.py:369
  88.0 5.8 %collective-permute-start.15 = (bf16[128,128]{1,0:T(8,128)(2,1)S(1)}, bf16[128,128]{1,0:T(8,128)(2,1)S(1)}, u32[]{:S(2)}, u32[]{:S(2)}) collective-permute-start(bf16[128,128]{1,0:T(8,128)(2,1)S(1)} %get-tuple-element.58), channel_id=1, source_target_pairs={{1,0},{2,1},{3,2},{4,3},{5,4},{6,5},{7,6},{8,7},{9,8},{10,9},{11,1... | collective-permute-start | bytes 98312 | tf_op jit(solution)/shard_map/ppermute | solution.py:370
  96.9 13.8 %collective-permute-start.16 = (bf16[128,128]{1,0:T(8,128)(2,1)S(1)}, bf16[128,128]{1,0:T(8,128)(2,1)S(1)}, u32[]{:S(2)}, u32[]{:S(2)}) collective-permute-start(bf16[128,128]{1,0:T(8,128)(2,1)S(1)} %get-tuple-element.64), channel_id=1, source_target_pairs={{0,32},{32,64},{64,96},{96,128},{128,160},{160,192},{192,224},{224... | collective-permute-start | bytes 98312 | tf_op jit(solution)/shard_map/ppermute | solution.py:369
  101.8 8.9 %collective-permute-start.17 = (bf16[128,128]{1,0:T(8,128)(2,1)S(1)}, bf16[128,128]{1,0:T(8,128)(2,1)S(1)}, u32[]{:S(2)}, u32[]{:S(2)}) collective-permute-start(bf16[128,128]{1,0:T(8,128)(2,1)S(1)} %get-tuple-element.65), channel_id=1, source_target_pairs={{32,0},{64,32},{96,64},{128,96},{160,128},{192,160},{224,192},{256... | collective-permute-start | bytes 98312 | tf_op jit(solution)/shard_map/ppermute | solution.py:370
  103.7 7.0 %collective-permute-start.18 = (bf16[128,128]{1,0:T(8,128)(2,1)S(1)}, bf16[128,128]{1,0:T(8,128)(2,1)S(1)}, u32[]{:S(2)}, u32[]{:S(2)}) collective-permute-start(bf16[128,128]{1,0:T(8,128)(2,1)S(1)} %get-tuple-element.66), channel_id=1, source_target_pairs={{0,1},{1,2},{2,3},{3,4},{4,5},{5,6},{6,7},{7,8},{8,9},{9,10},{10,1... | collective-permute-start | bytes 98312 | tf_op jit(solution)/shard_map/ppermute | solution.py:369
  109.4 5.6 %collective-permute-start.19 = (bf16[128,128]{1,0:T(8,128)(2,1)S(1)}, bf16[128,128]{1,0:T(8,128)(2,1)S(1)}, u32[]{:S(2)}, u32[]{:S(2)}) collective-permute-start(bf16[128,128]{1,0:T(8,128)(2,1)S(1)} %get-tuple-element.67), channel_id=1, source_target_pairs={{1,0},{2,1},{3,2},{4,3},{5,4},{6,5},{7,6},{8,7},{9,8},{10,9},{11,1... | collective-permute-start | bytes 98312 | tf_op jit(solution)/shard_map/ppermute | solution.py:370
Sparse Core Ops, SparseCore 0:
  119.5 285.2 all-reduce.1

commit v2 on v1

--- a/solution.py
+++ b/solution.py
@@ -14,9 +14,12 @@
 NC_DEV = 256
 CHUNK = 256
 GRAD_ROWS = 5 * H + 8
+PACKED = 2048
+SMALL = 15 * H
 EPSILON = 1e-05
 F32 = jnp.float32
 BF16 = jnp.bfloat16
+GATHER_WIRE = BF16
 
 
 def halves(values):
@@ -66,6 +69,22 @@
     return jnp.where(marks, 1.0, 0.0).astype(BF16)
 
 
+def place():
+    across, along = lax.axis_index("gx") % 2, lax.axis_index("gy") % 2
+    return (3 - along, 2 + along, across, 1 - across)
+
+
+def rows_at(index, count):
+    return pl.ds(pl.multiple_of(index * count, count), count)
+
+
+def gather_halos(x_ref, halos, extended_ref):
+    rows = x_ref.shape[0]
+    extended_ref[0:rows, :] = x_ref[...]
+    for group, halo in zip(place(), halos, strict=True):
+        extended_ref[pl.ds(pl.multiple_of(rows + group * BLOCK, BLOCK), BLOCK), :] = halo[...]
+
+
 def normalise(node_pre):
     centred = node_pre - jnp.mean(node_pre, axis=1, keepdims=True)
     spread = jnp.mean(centred * centred, axis=1, keepdims=True)
@@ -73,10 +92,9 @@
     return centred * scale, scale
 
 
-def forward_step(x, halos, senders, receivers, weights, bias, gain, hidden_ref, slope_ref):
+def forward_step(x, extended, senders, receivers, weights, bias, gain, hidden_ref, slope_ref):
     rows = x.shape[0]
     slots = senders.shape[1]
-    extended = jnp.concatenate([x] + halos, axis=0)
     width = extended.shape[0]
     projected = jnp.concatenate(
         [halves(matmul(extended, weights[0])), halves(matmul(x, weights[1]))], axis=0
@@ -113,7 +131,7 @@
 def backward_step(
     upstream,
     x,
-    halos,
+    extended,
     senders,
     receivers,
     weights,
@@ -150,7 +168,6 @@
         grad_act = joined(matmul(marks, message_parts)) * slope_ref[first : first + CHUNK, :]
         act_ref[first : first + CHUNK, :] = halves(grad_act)
     act = act_ref[...]
-    extended = jnp.concatenate([x] + halos, axis=0)
     width = extended.shape[0]
     send_parts = halves(
         jnp.concatenate(
@@ -191,7 +208,7 @@
 
 
 def send_blocks(source_ref, blocks_ref, out_refs):
-    for direction, out_ref in enumerate(out_refs):
+    for direction, out_ref in zip(place(), out_refs, strict=True):
         start = pl.multiple_of(blocks_ref[direction] * BLOCK, BLOCK)
         out_ref[...] = source_ref[pl.ds(start, BLOCK), :]
 
@@ -205,11 +222,12 @@
 def fine_ahead(
     live_ref, blocks_ref, x_ref, h0, h1, h2, h3, edges_ref, pool_ref, w_ref, bias_ref, gain_ref,
     mid_ref, coarse_ref, s0, s1, s2, s3, sums_ref, agg_ref, pre_ref, slope_ref,
-    hidden_ref,
-):
+    extended_ref, hidden_ref,
+):
+    gather_halos(x_ref, (h0, h1, h2, h3), extended_ref)
     output, edge_sums, agg, node_pre = forward_step(
         x_ref[...],
-        [h0[...], h1[...], h2[...], h3[...]],
+        extended_ref[...],
         edges_ref[0:1, :],
         live_receivers(edges_ref, live_ref),
         w_ref,
@@ -231,11 +249,12 @@
 def coarse_ahead(
     blocks_ref, x_ref, h0, h1, h2, h3, edges_ref, w_ref, bias_ref, gain_ref,
     out_ref, s0, s1, s2, s3, sums_ref, agg_ref, pre_ref, slope_ref,
-    hidden_ref,
-):
+    extended_ref, hidden_ref,
+):
+    gather_halos(x_ref, (h0, h1, h2, h3), extended_ref)
     output, edge_sums, agg, node_pre = forward_step(
         x_ref[...],
-        [h0[...], h1[...], h2[...], h3[...]],
+        extended_ref[...],
         edges_ref[0:1, :],
         edges_ref[1:2, :],
         w_ref.at[0],
@@ -251,39 +270,41 @@
     send_blocks(out_ref, blocks_ref, (s0, s1, s2, s3))
 
 
-def put_halo_grads(grad_halo, out_refs):
-    for group, out_ref in enumerate(out_refs):
-        out_ref[...] = grad_halo[group * BLOCK : (group + 1) * BLOCK].astype(BF16)
+def put_halo_grads(grad_halo, halo_ref, out_refs):
+    halo_ref[...] = grad_halo.astype(BF16)
+    for group, out_ref in zip(place(), out_refs, strict=True):
+        out_ref[...] = halo_ref[rows_at(group, BLOCK), :]
 
 
 def coarse_turn(
     loss_scale, x_ref, h0, h1, h2, h3, edges_ref, w_ref, bias_ref, gain_ref, pool_ref, mid_ref, cot_ref,
     out_ref, grad_ref, g0, g1, g2, g3, grads_ref,
-    hidden_ref, slope_ref, act_ref,
-):
+    extended_ref, hidden_ref, slope_ref, act_ref, halo_ref,
+):
+    gather_halos(x_ref, (h0, h1, h2, h3), extended_ref)
     x = x_ref[...]
-    halos = [h0[...], h1[...], h2[...], h3[...]]
+    extended = extended_ref[...]
     senders, receivers = edges_ref[0:1, :], edges_ref[1:2, :]
     gain = gain_ref[1:2, :]
     weights = w_ref.at[1]
     output, edge_sums, agg, node_pre = forward_step(
-        x, halos, senders, receivers, weights, bias_ref[1:2, :], gain, hidden_ref, slope_ref
+        x, extended, senders, receivers, weights, bias_ref[1:2, :], gain, hidden_ref, slope_ref
     )
     pool_row = pool_ref[...]
     lifted = matmul(one_hot_rows(pool_row, NC_DEV), output)
     out_ref[...] = (mid_ref[...].astype(F32) + lifted).astype(BF16)
     upstream = matmul(one_hot_columns(pool_row, 0, NC_DEV), cot_ref[...]) * loss_scale
     grad_nodes, grad_halo = backward_step(
-        upstream, x, halos, senders, receivers, weights, gain, edge_sums, agg, node_pre,
+        upstream, x, extended, senders, receivers, weights, gain, edge_sums, agg, node_pre,
         slope_ref, act_ref, grads_ref, True,
     )
     grad_ref[...] = grad_nodes
-    put_halo_grads(grad_halo, (g0, g1, g2, g3))
+    put_halo_grads(grad_halo, halo_ref, (g0, g1, g2, g3))
 
 
 def add_returned(grad_ref, returned, blocks_ref, total_ref):
     total_ref[...] = grad_ref[...]
-    for direction, piece in enumerate(returned):
+    for direction, piece in zip(place(), returned, strict=True):
         start = pl.multiple_of(blocks_ref[direction] * BLOCK, BLOCK)
         total_ref[pl.ds(start, BLOCK), :] += piece[...].astype(F32)
 
@@ -292,13 +313,14 @@
     blocks_ref, grad_in_ref, r0, r1, r2, r3, x_ref, h0, h1, h2, h3, edges_ref, w_ref, gain_ref,
     sums_ref, agg_ref, pre_ref, slope_ref,
     grad_ref, g0, g1, g2, g3, grads_ref,
-    total_ref, act_ref,
-):
+    extended_ref, total_ref, act_ref, halo_ref,
+):
+    gather_halos(x_ref, (h0, h1, h2, h3), extended_ref)
     add_returned(grad_in_ref, (r0, r1, r2, r3), blocks_ref, total_ref)
     grad_nodes, grad_halo = backward_step(
         total_ref[...],
         x_ref[...],
-        [h0[...], h1[...], h2[...], h3[...]],
+        extended_ref[...],
         edges_ref[0:1, :],
         edges_ref[1:2, :],
         w_ref.at[0],
@@ -312,15 +334,16 @@
         True,
     )
     grad_ref[...] = grad_nodes
-    put_halo_grads(grad_halo, (g0, g1, g2, g3))
+    put_halo_grads(grad_halo, halo_ref, (g0, g1, g2, g3))
 
 
 def fine_behind(
     loss_scale, root, live_ref, blocks_ref, grad_in_ref, r0, r1, r2, r3, x_ref, h0, h1, h2, h3, edges_ref,
-    pool_ref, cot_ref, w_ref, gain_ref, sums_ref, agg_ref, pre_ref, slope_ref,
-    pooled_ref, grads_ref,
-    total_ref, act_ref,
-):
+    pool_ref, cot_ref, w_ref, gain_ref, sums_ref, agg_ref, pre_ref, slope_ref, grads_0_ref, grads_1_ref,
+    pooled_ref, packed_ref,
+    extended_ref, total_ref, act_ref, grads_ref,
+):
+    gather_halos(x_ref, (h0, h1, h2, h3), extended_ref)
     add_returned(grad_in_ref, (r0, r1, r2, r3), blocks_ref, total_ref)
     total = total_ref[...]
     pooled_ref[...] = total * root
@@ -332,7 +355,7 @@
     backward_step(
         upstream,
         x_ref[...],
-        [h0[...], h1[...], h2[...], h3[...]],
+        extended_ref[...],
         edges_ref[0:1, :],
         live_receivers(edges_ref, live_ref),
         w_ref,
@@ -345,6 +368,61 @@
         grads_ref,
         False,
     )
+    for index, source in enumerate((grads_ref, grads_0_ref, grads_1_ref)):
+        packed_ref[index * 5 * H : (index + 1) * 5 * H, :] = source[0 : 5 * H, :]
+        packed_ref[SMALL + index * 8 : SMALL + index * 8 + 8, :] = source[5 * H :, :]
+    packed_ref[SMALL + 24 :, :] = jnp.zeros((PACKED - SMALL - 24, H), F32)
+
+
+def sum_parts(parts_ref, out_ref):
+    values = [parts_ref[index] for index in range(parts_ref.shape[0])]
+    while len(values) > 1:
+        values = [a + b for a, b in zip(values[0::2], values[1::2], strict=True)]
+    out_ref[...] = values[0]
+
+
+def sum_and_spread(parts_ref, out_ref):
+    values = [parts_ref[index] for index in range(parts_ref.shape[0])]
+    while len(values) > 1:
+        values = [a + b for a, b in zip(values[0::2], values[1::2], strict=True)]
+    for index in range(out_ref.shape[0]):
+        out_ref[index] = values[0]
+
+
+def spread(piece_ref, out_ref):
+    piece = piece_ref[...].astype(out_ref.dtype)
+    for index in range(out_ref.shape[0]):
+        out_ref[index] = piece
+
+
+def finish(all_ref, fine_ref, coarse_ref, fb_ref, fg_ref, cb_ref, cg_ref):
+    fine_ref[...] = all_ref[0 : 5 * H, :].astype(F32)
+    coarse_ref[...] = all_ref[5 * H : SMALL, :].astype(F32)
+    small = all_ref[SMALL : SMALL + 32, :].astype(F32)
+    fb_ref[...] = small[0:1]
+    fg_ref[...] = small[1:2]
+    cb_ref[...] = jnp.concatenate([small[8:9], small[16:17]], axis=0)
+    cg_ref[...] = jnp.concatenate([small[9:10], small[17:18]], axis=0)
+
+
+def reduce_all(packed):
+    across, along = lax.axis_size("gx"), lax.axis_size("gy")
+    rows = PACKED // across
+    part = rows // along
+    pieces = lax.all_to_all(packed.reshape(across, rows, H), "gx", 0, 0)
+    (mine,) = call(sum_parts, [], [pieces], [((rows, H), F32)], [])
+    pieces = lax.all_to_all(mine.reshape(along, part, H), "gy", 0, 0)
+    (shared,) = call(sum_and_spread, [], [pieces], [((along, part, H), F32)], [])
+    mine = lax.all_to_all(shared, "gy", 0, 0).reshape(rows, H)
+    (shared,) = call(spread, [], [mine], [((across, rows, H), GATHER_WIRE)], [])
+    everything = lax.all_to_all(shared, "gx", 0, 0).reshape(PACKED, H)
+    return call(
+        finish,
+        [],
+        [everything],
+        [((5 * H, H), F32), ((10 * H, H), F32)] + [((1, H), F32)] * 2 + [((2, H), F32)] * 2,
+        [],
+    )
 
 
 def call(kernel, scalars, arrays, outs, scratch):
@@ -362,17 +440,16 @@
 
 def exchange(pieces):
     received = []
-    for axis, (lower, upper) in (("gx", pieces[0:2]), ("gy", pieces[2:4])):
-        peers = lax.axis_size(axis)
-        up = [(i, i + 1) for i in range(peers - 1)]
-        down = [(i + 1, i) for i in range(peers - 1)]
-        received.append(lax.ppermute(upper, axis, up))
-        received.append(lax.ppermute(lower, axis, down))
+    for piece, (axis, first) in zip(pieces, (("gy", 0), ("gy", 1), ("gx", 1), ("gx", 0)), strict=True):
+        pairs = []
+        for i in range(first, lax.axis_size(axis) - 1, 2):
+            pairs += [(i, i + 1), (i + 1, i)]
+        received.append(lax.ppermute(piece, axis, pairs))
     return received
 
 
-def reduce_all(terms):
-    return lax.psum(terms, ("gx", "gy"))
+def pick(blocks_ref, x_ref, s0, s1, s2, s3):
+    send_blocks(x_ref, blocks_ref, (s0, s1, s2, s3))
 
 
 def body(
@@ -413,26 +490,24 @@
             ((edge_count, H), F32),
         ]
 
-    picks = fine_halo.reshape(4)
-    sends = [
-        lax.dynamic_slice_in_dim(x, picks[direction] * BLOCK, BLOCK) for direction in range(4)
-    ]
-    halos = exchange(sends)
+    halos = exchange(call(pick, [fine_halo.reshape(4)], [x], [block] * 4, []))
     fine_out = call(
         fine_ahead,
         [live, blocks],
         [x, *halos, edges, pool, fine_weights, bias, gain],
         [((rows, H), BF16), ((NC_DEV, H), BF16)] + [block] * 4 + saved(rows, slots),
-        [((slots, H), BF16)],
+        [((rows + 4 * BLOCK, H), BF16), ((slots, H), BF16)],
     )
     mid, coarse_0, sends, fine_saved = fine_out[0], fine_out[1], fine_out[2:6], fine_out[6:]
     halos_0 = exchange(sends)
+    coarse_extended = ((NC_DEV + 4 * BLOCK, H), BF16)
+    halo_grads = ((4 * BLOCK, H), BF16)
     ahead = call(
         coarse_ahead,
         [blocks],
         [coarse_0, *halos_0, coarse_list, coarse_weights, coarse_bias, coarse_gain],
         [((NC_DEV, H), BF16)] + [block] * 4 + saved(NC_DEV, coarse_slots),
-        [((coarse_slots, H), BF16)],
+        [coarse_extended, ((coarse_slots, H), BF16)],
     )
     coarse_1, sends, coarse_saved = ahead[0], ahead[1:5], ahead[5:]
     halos_1 = exchange(sends)
@@ -442,7 +517,8 @@
         [],
         [coarse_1, *halos_1, coarse_list, coarse_weights, coarse_bias, coarse_gain, pool, mid, cot],
         [((rows, H), BF16), ((NC_DEV, H), F32)] + [block] * 4 + [grads],
-        [((coarse_slots, H), BF16), ((coarse_slots, H), F32), ((coarse_slots, 2 * H), BF16)],
+        [coarse_extended, ((coarse_slots, H), BF16), ((coarse_slots, H), F32)]
+        + [((coarse_slots, 2 * H), BF16), halo_grads],
     )
     result, grad_nodes, grad_halo, grads_1 = turned[0], turned[1], turned[2:6], turned[6]
     returned = exchange(grad_halo)
@@ -452,28 +528,27 @@
         [grad_nodes, *returned, coarse_0, *halos_0, coarse_list]
         + [coarse_weights, coarse_gain, *coarse_saved],
         [((NC_DEV, H), F32)] + [block] * 4 + [grads],
-        [((NC_DEV, H), F32), ((coarse_slots, 2 * H), BF16)],
+        [coarse_extended, ((NC_DEV, H), F32), ((coarse_slots, 2 * H), BF16), halo_grads],
     )
     grad_nodes, grad_halo, grads_0 = behind[0], behind[1:5], behind[5]
     returned = exchange(grad_halo)
-    grad_pooled, grads_f = call(
+    grad_pooled, packed = call(
         functools.partial(fine_behind, 1.0 / root, root),
         [live, blocks],
-        [grad_nodes, *returned, x, *halos, edges, pool, cot, fine_weights, gain, *fine_saved],
-        [((NC_DEV, H), F32), grads],
-        [((NC_DEV, H), F32), ((slots, 2 * H), BF16)],
-    )
-    total = reduce_all(jnp.concatenate([grads_f, grads_0, grads_1], axis=0))
-    total = total.reshape(3, GRAD_ROWS, H)
-    weights = total[:, : 5 * H].reshape(3, 5, H, H)
+        [grad_nodes, *returned, x, *halos, edges, pool, cot, fine_weights, gain, *fine_saved]
+        + [grads_0, grads_1],
+        [((NC_DEV, H), F32), ((PACKED, H), F32)],
+        [((rows + 4 * BLOCK, H), BF16), ((NC_DEV, H), F32), ((slots, 2 * H), BF16), grads],
+    )
+    fine_w, coarse_w, fine_b, fine_g, coarse_b, coarse_g = reduce_all(packed)
     return (
         result[None, None],
-        weights[0],
-        total[0, 5 * H],
-        total[0, 5 * H + 1],
-        weights[1:],
-        total[1:, 5 * H],
-        total[1:, 5 * H + 1],
+        fine_w.reshape(5, H, H),
+        fine_b.reshape(H),
+        fine_g.reshape(H),
+        coarse_w.reshape(2, 5, H, H),
+        coarse_b,
+        coarse_g,
         grad_pooled[None, None],
     )
 

time: 419 us -> 180 us (0.43)
  waiting for transfers between devices: 303 us -> 4.6 us
  blocking collectives: 0 us -> 78.3 us
  between operations: 17.8 us -> 1.63 us
    psum x1 -> x0, waiting for transfers between devices: 285 us -> none  [reduce_all(): return lax.psum(terms, ('gx', 'gy'))]
    all_to_all x0 -> x4, blocking collectives: none -> 78.3 us  [the longest x1 25.2 us: reduce_all(): pieces = lax.all_to_all(mine.reshape(along, part, H), 'gy', 0, 0)]
    ppermute x20, waiting for transfers between devices: 17.9 us -> 4.6 us  [exchange(): received.append(lax.ppermute(piece, axis, pairs))]
    unnamed x24 -> x38, local copies, waits for them, and re-layouts: 0.73 us -> 8.79 us
    slice x4 -> x0, local copies, waits for them, and re-layouts: 6.42 us -> none  [the longest x1 1.97 us: body(): weights[1:]]
    pallas_call x5 -> x10, Pallas kernels: 17.7 us -> 19.5 us  [call(): pl.pallas_call(kernel, out_shape=[jax.ShapeDtypeStruct(shape, dtype) for...]
  transfers between devices with their start and end apart: 21 -> 20, of which waited for: 6 -> 7; matrix products, arithmetic and copies ran while one was open for 0% -> 0% of each run, Pallas kernels for 0% -> 0%
where the time goes in v2:
time: 180 us; the launch traced here: 179 us
  blocking collectives  78.3 us (44%)
  starting transfers between devices  66.2 us (37%)
  Pallas kernels  19.5 us (11%)
  local copies, waits for them, and re-layouts  8.79 us (5%)
  waiting for transfers between devices  4.6 us (3%)
    ppermute x20, starting transfers between devices, exchange(): received.append(lax.ppermute(piece, axis, pairs))  66.2 us
    all_to_all x1, blocking collectives, reduce_all(): pieces = lax.all_to_all(mine.reshape(along, part, H), 'gy', 0, 0)  25.2 us
    all_to_all x1, blocking collectives, reduce_all(): pieces = lax.all_to_all(packed.reshape(across, rows, H), 'gx', 0, 0)  22.9 us
    pallas_call x10, Pallas kernels, call(): pl.pallas_call(kernel, out_shape=[jax.ShapeDtypeStruct(shape, dtype) for...  19.5 us
    all_to_all x1, blocking collectives, reduce_all(): everything = lax.all_to_all(shared, 'gx', 0, 0).reshape(PACKED, H)  16 us
    all_to_all x1, blocking collectives, reduce_all(): mine = lax.all_to_all(shared, 'gy', 0, 0).reshape(rows, H)  14.1 us
    unnamed x38, local copies, waits for them, and re-layouts  8.79 us
    ppermute x20, waiting for transfers between devices, exchange(): received.append(lax.ppermute(piece, axis, pairs))  4.6 us
  transfers between devices with their start and end apart: 20, of which 7 were waited for; matrix products, arithmetic and copies ran while one was open for 0% of the time, Pallas kernels for 0%

profile of v2, /device:TPU:1, one launch (start us, length us, event | category | flops | bytes accessed | tf_op | source)
XLA Modules:
  0.0 179.1 jit_solution(17063978317312772787)
XLA Ops:
  0.7 0.9 copy-done.1
  1.6 0.7 copy-done.17
  2.3 0.6 shard_map.197
  2.8 5.0 %collective-permute-start = (bf16[128,128]{1,0:T(8,128)(2,1)S(1)}, bf16[128,128]{1,0:T(8,128)(2,1)S(1)}, u32[]{:S(2)}, u32[]{:S(2)}) collective-permute-start(bf16[128,128]{1,0:T(8,128)(2,1)S(1)} %get-tuple-element.52), channel_id=1, source_target_pairs={{0,1},{1,0},{2,3},{3,2},{4,5},{5,4},{6,7},{7,6},{8,9},{9,8},{10,11... | collective-permute-start | bytes 98312 | tf_op jit(solution)/shard_map/ppermute | solution.py:447
  7.9 0.7 collective-permute-start.1
  8.6 4.0 %collective-permute-start.2 = (bf16[128,128]{1,0:T(8,128)(2,1)S(1)}, bf16[128,128]{1,0:T(8,128)(2,1)S(1)}, u32[]{:S(2)}, u32[]{:S(2)}) collective-permute-start(bf16[128,128]{1,0:T(8,128)(2,1)S(1)} %get-tuple-element.54), channel_id=1, source_target_pairs={{32,64},{64,32},{96,128},{128,96},{160,192},{192,160},{224,256},{2... | collective-permute-start | bytes 98312 | tf_op jit(solution)/shard_map/ppermute | solution.py:447
  12.5 2.4 %collective-permute-start.3 = (bf16[128,128]{1,0:T(8,128)(2,1)S(1)}, bf16[128,128]{1,0:T(8,128)(2,1)S(1)}, u32[]{:S(2)}, u32[]{:S(2)}) collective-permute-start(bf16[128,128]{1,0:T(8,128)(2,1)S(1)} %get-tuple-element.55), channel_id=1, source_target_pairs={{0,32},{32,0},{64,96},{96,64},{128,160},{160,128},{192,224},{224,1... | collective-permute-start | bytes 98312 | tf_op jit(solution)/shard_map/ppermute | solution.py:447
  15.7 0.9 copy-done.2
  16.6 0.9 copy-done.4
  17.6 0.7 copy-done.7
  18.3 0.7 copy-done.9
  18.9 0.7 copy-done.12
  19.6 0.7 copy-done.15
  20.3 0.7 copy-done.18
  20.9 3.3 %shard_map.198 = (bf16[512,128]{1,0:T(8,128)(2,1)S(1)}, bf16[256,128]{1,0:T(8,128)(2,1)S(1)}, bf16[128,128]{1,0:T(8,128)(2,1)S(1)}, bf16[128,128]{1,0:T(8,128)(2...) custom-call(s32[1]{0:T(128)} %bitcast.20.live_ref, ...), custom_call_target="tpu_custom_call" | custom-call | tf_op jit(solution)/shard_map/pallas_call | solution.py:431
  24.2 7.4 %collective-permute-start.4 = (bf16[128,128]{1,0:T(8,128)(2,1)S(1)}, bf16[128,128]{1,0:T(8,128)(2,1)S(1)}, u32[]{:S(2)}, u32[]{:S(2)}) collective-permute-start(bf16[128,128]{1,0:T(8,128)(2,1)S(1)} %get-tuple-element.57), channel_id=1, source_target_pairs={{0,1},{1,0},{2,3},{3,2},{4,5},{5,4},{6,7},{7,6},{8,9},{9,8},{10,11... | collective-permute-start | bytes 98312 | tf_op jit(solution)/shard_map/ppermute | solution.py:447
  31.6 0.7 collective-permute-start.5
  32.3 3.4 %collective-permute-start.6 = (bf16[128,128]{1,0:T(8,128)(2,1)S(1)}, bf16[128,128]{1,0:T(8,128)(2,1)S(1)}, u32[]{:S(2)}, u32[]{:S(2)}) collective-permute-start(bf16[128,128]{1,0:T(8,128)(2,1)S(1)} %get-tuple-element.59), channel_id=1, source_target_pairs={{32,64},{64,32},{96,128},{128,96},{160,192},{192,160},{224,256},{2... | collective-permute-start | bytes 98312 | tf_op jit(solution)/shard_map/ppermute | solution.py:447
  35.7 1.9 %collective-permute-start.7 = (bf16[128,128]{1,0:T(8,128)(2,1)S(1)}, bf16[128,128]{1,0:T(8,128)(2,1)S(1)}, u32[]{:S(2)}, u32[]{:S(2)}) collective-permute-start(bf16[128,128]{1,0:T(8,128)(2,1)S(1)} %get-tuple-element.60), channel_id=1, source_target_pairs={{0,32},{32,0},{64,96},{96,64},{128,160},{160,128},{192,224},{224,1... | collective-permute-start | bytes 98312 | tf_op jit(solution)/shard_map/ppermute | solution.py:447
  37.7 1.1 collective-permute-done.7.h3
  38.8 0.7 copy-done.11
  39.5 2.9 %shard_map.199 = (bf16[256,128]{1,0:T(8,128)(2,1)S(1)}, bf16[128,128]{1,0:T(8,128)(2,1)S(1)}, bf16[128,128]{1,0:T(8,128)(2,1)S(1)}, bf16[128,128]{1,0:T(8,128)(2...) custom-call(s32[4]{0:T(128)S(1)} %bitcast.40, ...), custom_call_target="tpu_custom_call" | custom-call | tf_op jit(solution)/shard_map/pallas_call | solution.py:431
  42.4 7.2 %collective-permute-start.8 = (bf16[128,128]{1,0:T(8,128)(2,1)S(1)}, bf16[128,128]{1,0:T(8,128)(2,1)S(1)}, u32[]{:S(2)}, u32[]{:S(2)}) collective-permute-start(bf16[128,128]{1,0:T(8,128)(2,1)S(1)} %get-tuple-element.62), channel_id=1, source_target_pairs={{0,1},{1,0},{2,3},{3,2},{4,5},{5,4},{6,7},{7,6},{8,9},{9,8},{10,11... | collective-permute-start | bytes 98312 | tf_op jit(solution)/shard_map/ppermute | solution.py:447
  49.5 0.7 collective-permute-start.9
  50.2 3.2 %collective-permute-start.10 = (bf16[128,128]{1,0:T(8,128)(2,1)S(1)}, bf16[128,128]{1,0:T(8,128)(2,1)S(1)}, u32[]{:S(2)}, u32[]{:S(2)}) collective-permute-start(bf16[128,128]{1,0:T(8,128)(2,1)S(1)} %get-tuple-element.64), channel_id=1, source_target_pairs={{32,64},{64,32},{96,128},{128,96},{160,192},{192,160},{224,256},{2... | collective-permute-start | bytes 98312 | tf_op jit(solution)/shard_map/ppermute | solution.py:447
  53.4 1.9 %collective-permute-start.11 = (bf16[128,128]{1,0:T(8,128)(2,1)S(1)}, bf16[128,128]{1,0:T(8,128)(2,1)S(1)}, u32[]{:S(2)}, u32[]{:S(2)}) collective-permute-start(bf16[128,128]{1,0:T(8,128)(2,1)S(1)} %get-tuple-element.65), channel_id=1, source_target_pairs={{0,32},{32,0},{64,96},{96,64},{128,160},{160,128},{192,224},{224,1... | collective-permute-start | bytes 98312 | tf_op jit(solution)/shard_map/ppermute | solution.py:447
  55.4 1.0 collective-permute-done.11.h3
  56.5 4.7 %shard_map.200 = (bf16[512,128]{1,0:T(8,128)(2,1)}, f32[256,128]{1,0:T(8,128)S(1)}, bf16[128,128]{1,0:T(8,128)(2,1)S(1)}, bf16[128,128]{1,0:T(8,128)(2,1)S(1)}, ...) custom-call(bf16[256,128]{1,0:T(8,128)(2,1)S(1)} %get-tuple-element.61.x_ref, ...), custom_call_target="tpu_custom_call" | custom-call | tf_op jit(solution)/shard_map/pallas_call | solution.py:431
  61.1 7.4 %collective-permute-start.12 = (bf16[128,128]{1,0:T(8,128)(2,1)S(1)}, bf16[128,128]{1,0:T(8,128)(2,1)S(1)}, u32[]{:S(2)}, u32[]{:S(2)}) collective-permute-start(bf16[128,128]{1,0:T(8,128)(2,1)S(1)} %get-tuple-element.69), channel_id=1, source_target_pairs={{0,1},{1,0},{2,3},{3,2},{4,5},{5,4},{6,7},{7,6},{8,9},{9,8},{10,11... | collective-permute-start | bytes 98312 | tf_op jit(solution)/shard_map/ppermute | solution.py:447
  68.6 0.7 collective-permute-start.13
  69.3 2.5 %collective-permute-start.14 = (bf16[128,128]{1,0:T(8,128)(2,1)S(1)}, bf16[128,128]{1,0:T(8,128)(2,1)S(1)}, u32[]{:S(2)}, u32[]{:S(2)}) collective-permute-start(bf16[128,128]{1,0:T(8,128)(2,1)S(1)} %get-tuple-element.71), channel_id=1, source_target_pairs={{32,64},{64,32},{96,128},{128,96},{160,192},{192,160},{224,256},{2... | collective-permute-start | bytes 98312 | tf_op jit(solution)/shard_map/ppermute | solution.py:447
  71.8 2.1 %collective-permute-start.15 = (bf16[128,128]{1,0:T(8,128)(2,1)S(1)}, bf16[128,128]{1,0:T(8,128)(2,1)S(1)}, u32[]{:S(2)}, u32[]{:S(2)}) collective-permute-start(bf16[128,128]{1,0:T(8,128)(2,1)S(1)} %get-tuple-element.72), channel_id=1, source_target_pairs={{0,32},{32,0},{64,96},{96,64},{128,160},{160,128},{192,224},{224,1... | collective-permute-start | bytes 98312 | tf_op jit(solution)/shard_map/ppermute | solution.py:447
  73.9 0.5 collective-permute-done.14.r2
  74.5 0.4 collective-permute-done.15.r3
  74.9 0.7 copy-done.13
  75.6 3.0 %shard_map.201 = (f32[256,128]{1,0:T(8,128)S(1)}, bf16[128,128]{1,0:T(8,128)(2,1)S(1)}, bf16[128,128]{1,0:T(8,128)(2,1)S(1)}, bf16[128,128]{1,0:T(8,128)(2,1)S(1...) custom-call(s32[4]{0:T(128)S(1)} %bitcast.41, f32[256,128]{1,0:T(8,128)S(1)} %get-tuple-element.68.grad_in_ref, ...), custom_call_target="tpu_custom_call" | custom-call | tf_op jit(solution)/shard_map/pallas_call | solution.py:431
  78.6 8.1 %collective-permute-start.16 = (bf16[128,128]{1,0:T(8,128)(2,1)S(1)}, bf16[128,128]{1,0:T(8,128)(2,1)S(1)}, u32[]{:S(2)}, u32[]{:S(2)}) collective-permute-start(bf16[128,128]{1,0:T(8,128)(2,1)S(1)} %get-tuple-element.78), channel_id=1, source_target_pairs={{0,1},{1,0},{2,3},{3,2},{4,5},{5,4},{6,7},{7,6},{8,9},{9,8},{10,11... | collective-permute-start | bytes 98312 | tf_op jit(solution)/shard_map/ppermute | solution.py:447
  86.7 0.7 collective-permute-start.17
  87.3 4.5 %collective-permute-start.18 = (bf16[128,128]{1,0:T(8,128)(2,1)S(1)}, bf16[128,128]{1,0:T(8,128)(2,1)S(1)}, u32[]{:S(2)}, u32[]{:S(2)}) collective-permute-start(bf16[128,128]{1,0:T(8,128)(2,1)S(1)} %get-tuple-element.80), channel_id=1, source_target_pairs={{32,64},{64,32},{96,128},{128,96},{160,192},{192,160},{224,256},{2... | collective-permute-start | bytes 98312 | tf_op jit(solution)/shard_map/ppermute | solution.py:447
  91.9 1.9 %collective-permute-start.19 = (bf16[128,128]{1,0:T(8,128)(2,1)S(1)}, bf16[128,128]{1,0:T(8,128)(2,1)S(1)}, u32[]{:S(2)}, u32[]{:S(2)}) collective-permute-start(bf16[128,128]{1,0:T(8,128)(2,1)S(1)} %get-tuple-element.81), channel_id=1, source_target_pairs={{0,32},{32,0},{64,96},{96,64},{128,160},{160,128},{192,224},{224,1... | collective-permute-start | bytes 98312 | tf_op jit(solution)/shard_map/ppermute | solution.py:447
  93.8 1.1 collective-permute-done.19.r3
  95.0 0.7 copy-done.10
  95.6 4.0 %shard_map.202 = (f32[256,128]{1,0:T(8,128)}, f32[2048,128]{1,0:T(8,128)S(1)}) custom-call(s32[1]{0:T(128)} %bitcast.21.live_ref, s32[4]{0:T(128)S(1)} %bitcast.42, f32[256,128]{1,0:T(8,128)S(1)} %get-tuple-element.77.grad_in_ref, bf16[128,128]{1,0:T(8,128)(2,1)S(1)} %collective-permute-done.16.r0, bf16[128,128]{1,0:T(8,128)(2,1)S(1)} %collective-permute-done.17.r1, ...), custom_call_target="tpu_custom_call" | custom-call | tf_op jit(solution)/shard_map/pallas_call | solution.py:431
  99.7 22.9 %all_to_all.20.parts_ref = f32[16,128,128]{2,1,0:T(8,128)S(1)} all-to-all(f32[16,128,128]{2,1,0:T(8,128)S(1)} %bitcast.26), channel_id=1, replica_groups=mesh['gx'=16,'gy'=32] {'gx'}, dimensions={0} | all-to-all | bytes 2097152 | tf_op jit(solution)/shard_map/all_to_all | solution.py:412
  122.6 25.2 %all_to_all.21.parts_ref = f32[32,4,128]{2,1,0:T(4,128)S(1)} all-to-all(f32[32,4,128]{2,1,0:T(4,128)S(1)} %bitcast.29), channel_id=1, replica_groups=mesh['gx'=16,'gy'=32] {'gy'}, dimensions={0} | all-to-all | bytes 131072 | tf_op jit(solution)/shard_map/all_to_all | solution.py:414
  147.9 14.1 %all_to_all.22 = f32[32,4,128]{2,1,0:T(4,128)S(1)} all-to-all(f32[32,4,128]{2,1,0:T(4,128)S(1)} %shard_map.204), channel_id=1, replica_groups=mesh['gx'=16,'gy'=32] {'gy'}, dimensions={0} | all-to-all | bytes 131072 | tf_op jit(solution)/shard_map/all_to_all | solution.py:416
  162.1 16.0 %all_to_all.23 = bf16[16,128,128]{2,1,0:T(8,128)(2,1)S(1)} all-to-all(bf16[16,128,128]{2,1,0:T(8,128)(2,1)S(1)} %shard_map.205), channel_id=1, replica_groups=mesh['gx'=16,'gy'=32] {'gx'}, dimensions={0} | all-to-all | bytes 1048576 | tf_op jit(solution)/shard_map/all_to_all | solution.py:418
  178.1 1.0 shard_map.206
  (44 shorter events, 0.5 us)
Async XLA Ops:
  0.6 38.2 %copy-start = (bf16[2,5,128,128]{3,2,1,0:T(8,128)(2,1)S(1)}, bf16[2,5,128,128]{3,2,1,0:T(8,128)(2,1)}, u32[]{:S(2)}) copy-start(bf16[2,5,128,128]{3,2,1,0:T(8,128)(2,1)} %w_ref.8) | copy-start | bytes 983044
  0.6 1.0 copy-start.1
  1.6 0.7 copy-start.17
  2.8 12.7 %collective-permute-start = (bf16[128,128]{1,0:T(8,128)(2,1)S(1)}, bf16[128,128]{1,0:T(8,128)(2,1)S(1)}, u32[]{:S(2)}, u32[]{:S(2)}) collective-permute-start(bf16[128,128]{1,0:T(8,128)(2,1)S(1)} %get-tuple-element.52), channel_id=1, source_target_pairs={{0,1},{1,0},{2,3},{3,2},{4,5},{5,4},{6,7},{7,6},{8,9},{9,8},{10,11... | collective-permute-start | bytes 98312 | tf_op jit(solution)/shard_map/ppermute | solution.py:447
  7.9 7.7 %collective-permute-start.1 = (bf16[128,128]{1,0:T(8,128)(2,1)S(1)}, bf16[128,128]{1,0:T(8,128)(2,1)S(1)}, u32[]{:S(2)}, u32[]{:S(2)}) collective-permute-start(bf16[128,128]{1,0:T(8,128)(2,1)S(1)} %get-tuple-element.53), channel_id=1, source_target_pairs={{1,2},{2,1},{3,4},{4,3},{5,6},{6,5},{7,8},{8,7},{9,10},{10,9},{11,... | collective-permute-start | bytes 98312 | tf_op jit(solution)/shard_map/ppermute | solution.py:447
  8.6 7.0 %collective-permute-start.2 = (bf16[128,128]{1,0:T(8,128)(2,1)S(1)}, bf16[128,128]{1,0:T(8,128)(2,1)S(1)}, u32[]{:S(2)}, u32[]{:S(2)}) collective-permute-start(bf16[128,128]{1,0:T(8,128)(2,1)S(1)} %get-tuple-element.54), channel_id=1, source_target_pairs={{32,64},{64,32},{96,128},{128,96},{160,192},{192,160},{224,256},{2... | collective-permute-start | bytes 98312 | tf_op jit(solution)/shard_map/ppermute | solution.py:447
  12.5 3.2 %collective-permute-start.3 = (bf16[128,128]{1,0:T(8,128)(2,1)S(1)}, bf16[128,128]{1,0:T(8,128)(2,1)S(1)}, u32[]{:S(2)}, u32[]{:S(2)}) collective-permute-start(bf16[128,128]{1,0:T(8,128)(2,1)S(1)} %get-tuple-element.55), channel_id=1, source_target_pairs={{0,32},{32,0},{64,96},{96,64},{128,160},{160,128},{192,224},{224,1... | collective-permute-start | bytes 98312 | tf_op jit(solution)/shard_map/ppermute | solution.py:447
  15.7 0.9 copy-start.2
  16.6 0.9 copy-start.4
  17.6 0.7 copy-start.7
  18.3 0.7 copy-start.9
  18.9 0.7 copy-start.12
  19.6 0.7 copy-start.15
  20.3 0.7 copy-start.18
  20.9 17.9 %copy-start.6 = (s32[1,1,2,2048]{3,2,1,0:T(2,128)S(1)}, s32[1,1,2,2048]{3,2,1,0:T(2,128)}, u32[]{:S(2)}) copy-start(s32[1,1,2,2048]{3,2,1,0:T(2,128)} %param.19) | copy-start | bytes 49156
  24.2 13.4 %collective-permute-start.4 = (bf16[128,128]{1,0:T(8,128)(2,1)S(1)}, bf16[128,128]{1,0:T(8,128)(2,1)S(1)}, u32[]{:S(2)}, u32[]{:S(2)}) collective-permute-start(bf16[128,128]{1,0:T(8,128)(2,1)S(1)} %get-tuple-element.57), channel_id=1, source_target_pairs={{0,1},{1,0},{2,3},{3,2},{4,5},{5,4},{6,7},{7,6},{8,9},{9,8},{10,11... | collective-permute-start | bytes 98312 | tf_op jit(solution)/shard_map/ppermute | solution.py:447
  31.6 7.3 %copy-start.14 = (f32[2,128]{1,0:T(2,128)S(1)}, f32[2,128]{1,0:T(2,128)}, u32[]{:S(2)}) copy-start(f32[2,128]{1,0:T(2,128)} %bias_ref.3) | copy-start | bytes 3076
  31.6 6.1 %collective-permute-start.5 = (bf16[128,128]{1,0:T(8,128)(2,1)S(1)}, bf16[128,128]{1,0:T(8,128)(2,1)S(1)}, u32[]{:S(2)}, u32[]{:S(2)}) collective-permute-start(bf16[128,128]{1,0:T(8,128)(2,1)S(1)} %get-tuple-element.58), channel_id=1, source_target_pairs={{1,2},{2,1},{3,4},{4,3},{5,6},{6,5},{7,8},{8,7},{9,10},{10,9},{11,... | collective-permute-start | bytes 98312 | tf_op jit(solution)/shard_map/ppermute | solution.py:447
  32.3 5.4 %collective-permute-start.6 = (bf16[128,128]{1,0:T(8,128)(2,1)S(1)}, bf16[128,128]{1,0:T(8,128)(2,1)S(1)}, u32[]{:S(2)}, u32[]{:S(2)}) collective-permute-start(bf16[128,128]{1,0:T(8,128)(2,1)S(1)} %get-tuple-element.59), channel_id=1, source_target_pairs={{32,64},{64,32},{96,128},{128,96},{160,192},{192,160},{224,256},{2... | collective-permute-start | bytes 98312 | tf_op jit(solution)/shard_map/ppermute | solution.py:447
  35.7 3.1 %collective-permute-start.7 = (bf16[128,128]{1,0:T(8,128)(2,1)S(1)}, bf16[128,128]{1,0:T(8,128)(2,1)S(1)}, u32[]{:S(2)}, u32[]{:S(2)}) collective-permute-start(bf16[128,128]{1,0:T(8,128)(2,1)S(1)} %get-tuple-element.60), channel_id=1, source_target_pairs={{0,32},{32,0},{64,96},{96,64},{128,160},{160,128},{192,224},{224,1... | collective-permute-start | bytes 98312 | tf_op jit(solution)/shard_map/ppermute | solution.py:447
  38.8 0.7 copy-start.11
  39.5 17.0 %copy-start.5 = (bf16[1,1,512,128]{3,2,1,0:T(8,128)(2,1)S(1)}, bf16[1,1,512,128]{3,2,1,0:T(8,128)(2,1)}, u32[]{:S(2)}) copy-start(bf16[1,1,512,128]{3,2,1,0:T(8,128)(2,1)} %param.27) | copy-start | bytes 393220
  42.4 12.9 %collective-permute-start.8 = (bf16[128,128]{1,0:T(8,128)(2,1)S(1)}, bf16[128,128]{1,0:T(8,128)(2,1)S(1)}, u32[]{:S(2)}, u32[]{:S(2)}) collective-permute-start(bf16[128,128]{1,0:T(8,128)(2,1)S(1)} %get-tuple-element.62), channel_id=1, source_target_pairs={{0,1},{1,0},{2,3},{3,2},{4,5},{5,4},{6,7},{7,6},{8,9},{9,8},{10,11... | collective-permute-start | bytes 98312 | tf_op jit(solution)/shard_map/ppermute | solution.py:447
  49.5 5.8 %collective-permute-start.9 = (bf16[128,128]{1,0:T(8,128)(2,1)S(1)}, bf16[128,128]{1,0:T(8,128)(2,1)S(1)}, u32[]{:S(2)}, u32[]{:S(2)}) collective-permute-start(bf16[128,128]{1,0:T(8,128)(2,1)S(1)} %get-tuple-element.63), channel_id=1, source_target_pairs={{1,2},{2,1},{3,4},{4,3},{5,6},{6,5},{7,8},{8,7},{9,10},{10,9},{11,... | collective-permute-start | bytes 98312 | tf_op jit(solution)/shard_map/ppermute | solution.py:447
  50.2 5.2 %collective-permute-start.10 = (bf16[128,128]{1,0:T(8,128)(2,1)S(1)}, bf16[128,128]{1,0:T(8,128)(2,1)S(1)}, u32[]{:S(2)}, u32[]{:S(2)}) collective-permute-start(bf16[128,128]{1,0:T(8,128)(2,1)S(1)} %get-tuple-element.64), channel_id=1, source_target_pairs={{32,64},{64,32},{96,128},{128,96},{160,192},{192,160},{224,256},{2... | collective-permute-start | bytes 98312 | tf_op jit(solution)/shard_map/ppermute | solution.py:447
  53.4 3.1 %collective-permute-start.11 = (bf16[128,128]{1,0:T(8,128)(2,1)S(1)}, bf16[128,128]{1,0:T(8,128)(2,1)S(1)}, u32[]{:S(2)}, u32[]{:S(2)}) collective-permute-start(bf16[128,128]{1,0:T(8,128)(2,1)S(1)} %get-tuple-element.65), channel_id=1, source_target_pairs={{0,32},{32,0},{64,96},{96,64},{128,160},{160,128},{192,224},{224,1... | collective-permute-start | bytes 98312 | tf_op jit(solution)/shard_map/ppermute | solution.py:447
  61.1 12.8 %collective-permute-start.12 = (bf16[128,128]{1,0:T(8,128)(2,1)S(1)}, bf16[128,128]{1,0:T(8,128)(2,1)S(1)}, u32[]{:S(2)}, u32[]{:S(2)}) collective-permute-start(bf16[128,128]{1,0:T(8,128)(2,1)S(1)} %get-tuple-element.69), channel_id=1, source_target_pairs={{0,1},{1,0},{2,3},{3,2},{4,5},{5,4},{6,7},{7,6},{8,9},{9,8},{10,11... | collective-permute-start | bytes 98312 | tf_op jit(solution)/shard_map/ppermute | solution.py:447
  68.6 5.4 %collective-permute-start.13 = (bf16[128,128]{1,0:T(8,128)(2,1)S(1)}, bf16[128,128]{1,0:T(8,128)(2,1)S(1)}, u32[]{:S(2)}, u32[]{:S(2)}) collective-permute-start(bf16[128,128]{1,0:T(8,128)(2,1)S(1)} %get-tuple-element.70), channel_id=1, source_target_pairs={{1,2},{2,1},{3,4},{4,3},{5,6},{6,5},{7,8},{8,7},{9,10},{10,9},{11,... | collective-permute-start | bytes 98312 | tf_op jit(solution)/shard_map/ppermute | solution.py:447
  69.3 5.2 %collective-permute-start.14 = (bf16[128,128]{1,0:T(8,128)(2,1)S(1)}, bf16[128,128]{1,0:T(8,128)(2,1)S(1)}, u32[]{:S(2)}, u32[]{:S(2)}) collective-permute-start(bf16[128,128]{1,0:T(8,128)(2,1)S(1)} %get-tuple-element.71), channel_id=1, source_target_pairs={{32,64},{64,32},{96,128},{128,96},{160,192},{192,160},{224,256},{2... | collective-permute-start | bytes 98312 | tf_op jit(solution)/shard_map/ppermute | solution.py:447
  71.8 3.1 %collective-permute-start.15 = (bf16[128,128]{1,0:T(8,128)(2,1)S(1)}, bf16[128,128]{1,0:T(8,128)(2,1)S(1)}, u32[]{:S(2)}, u32[]{:S(2)}) collective-permute-start(bf16[128,128]{1,0:T(8,128)(2,1)S(1)} %get-tuple-element.72), channel_id=1, source_target_pairs={{0,32},{32,0},{64,96},{96,64},{128,160},{160,128},{192,224},{224,1... | collective-permute-start | bytes 98312 | tf_op jit(solution)/shard_map/ppermute | solution.py:447
  74.9 0.7 copy-start.13
  75.6 19.4 %copy-start.3 = (bf16[1,1,512,128]{3,2,1,0:T(8,128)(2,1)S(1)}, bf16[1,1,512,128]{3,2,1,0:T(8,128)(2,1)}, u32[]{:S(2)}) copy-start(bf16[1,1,512,128]{3,2,1,0:T(8,128)(2,1)} %param.14) | copy-start | bytes 393220
  78.6 16.4 %copy-start.8 = (s32[1,1,2,1536]{3,2,1,0:T(2,128)S(1)}, s32[1,1,2,1536]{3,2,1,0:T(2,128)}, u32[]{:S(2)}) copy-start(s32[1,1,2,1536]{3,2,1,0:T(2,128)} %param.15) | copy-start | bytes 36868
  78.6 15.2 %collective-permute-start.16 = (bf16[128,128]{1,0:T(8,128)(2,1)S(1)}, bf16[128,128]{1,0:T(8,128)(2,1)S(1)}, u32[]{:S(2)}, u32[]{:S(2)}) collective-permute-start(bf16[128,128]{1,0:T(8,128)(2,1)S(1)} %get-tuple-element.78), channel_id=1, source_target_pairs={{0,1},{1,0},{2,3},{3,2},{4,5},{5,4},{6,7},{7,6},{8,9},{9,8},{10,11... | collective-permute-start | bytes 98312 | tf_op jit(solution)/shard_map/ppermute | solution.py:447
  86.7 7.1 %collective-permute-start.17 = (bf16[128,128]{1,0:T(8,128)(2,1)S(1)}, bf16[128,128]{1,0:T(8,128)(2,1)S(1)}, u32[]{:S(2)}, u32[]{:S(2)}) collective-permute-start(bf16[128,128]{1,0:T(8,128)(2,1)S(1)} %get-tuple-element.79), channel_id=1, source_target_pairs={{1,2},{2,1},{3,4},{4,3},{5,6},{6,5},{7,8},{8,7},{9,10},{10,9},{11,... | collective-permute-start | bytes 98312 | tf_op jit(solution)/shard_map/ppermute | solution.py:447
  87.3 6.5 %collective-permute-start.18 = (bf16[128,128]{1,0:T(8,128)(2,1)S(1)}, bf16[128,128]{1,0:T(8,128)(2,1)S(1)}, u32[]{:S(2)}, u32[]{:S(2)}) collective-permute-start(bf16[128,128]{1,0:T(8,128)(2,1)S(1)} %get-tuple-element.80), channel_id=1, source_target_pairs={{32,64},{64,32},{96,128},{128,96},{160,192},{192,160},{224,256},{2... | collective-permute-start | bytes 98312 | tf_op jit(solution)/shard_map/ppermute | solution.py:447
  91.9 3.1 %collective-permute-start.19 = (bf16[128,128]{1,0:T(8,128)(2,1)S(1)}, bf16[128,128]{1,0:T(8,128)(2,1)S(1)}, u32[]{:S(2)}, u32[]{:S(2)}) collective-permute-start(bf16[128,128]{1,0:T(8,128)(2,1)S(1)} %get-tuple-element.81), channel_id=1, source_target_pairs={{0,32},{32,0},{64,96},{96,64},{128,160},{160,128},{192,224},{224,1... | collective-permute-start | bytes 98312 | tf_op jit(solution)/shard_map/ppermute | solution.py:447
  95.0 0.7 copy-start.10
  95.0 0.7 copy-start.16

commit v3 on v2

--- a/solution.py
+++ b/solution.py
@@ -20,6 +20,8 @@
 F32 = jnp.float32
 BF16 = jnp.bfloat16
 GATHER_WIRE = BF16
+SCATTER_WIRE = BF16
+SCOPED = 24 * 1024 * 1024
 
 
 def halves(values):
@@ -207,10 +209,19 @@
     return jnp.sum(jnp.where(marks, 1.0, 0.0), axis=1, keepdims=True)
 
 
-def send_blocks(source_ref, blocks_ref, out_refs):
+def listed(blocks_ref, direction):
+    blocks = blocks_ref[...]
+    chosen = lax.broadcasted_iota(jnp.int32, blocks.shape, 1) == direction
+    return jnp.sum(jnp.where(chosen, blocks, 0), axis=1, keepdims=True)
+
+
+def send_blocks(values, blocks_ref, out_refs):
     for direction, out_ref in zip(place(), out_refs, strict=True):
-        start = pl.multiple_of(blocks_ref[direction] * BLOCK, BLOCK)
-        out_ref[...] = source_ref[pl.ds(start, BLOCK), :]
+        name = jnp.broadcast_to(listed(blocks_ref, direction), (BLOCK, H))
+        piece = values[:BLOCK]
+        for block in range(1, NC_DEV // BLOCK):
+            piece = jnp.where(name == block, values[block * BLOCK : (block + 1) * BLOCK], piece)
+        out_ref[...] = piece.astype(BF16)
 
 
 def live_receivers(edges_ref, live_ref):
@@ -242,8 +253,9 @@
     pre_ref[...] = node_pre
     pool_row = pool_ref[...]
     pooled = matmul(one_hot_columns(pool_row, 0, NC_DEV), output)
-    coarse_ref[...] = (pooled / pool_counts(pool_row)).astype(BF16)
-    send_blocks(coarse_ref, blocks_ref, (s0, s1, s2, s3))
+    coarse = pooled / pool_counts(pool_row)
+    coarse_ref[...] = coarse.astype(BF16)
+    send_blocks(coarse, blocks_ref, (s0, s1, s2, s3))
 
 
 def coarse_ahead(
@@ -267,7 +279,7 @@
     sums_ref[...] = edge_sums
     agg_ref[...] = agg
     pre_ref[...] = node_pre
-    send_blocks(out_ref, blocks_ref, (s0, s1, s2, s3))
+    send_blocks(output.astype(F32), blocks_ref, (s0, s1, s2, s3))
 
 
 def put_halo_grads(grad_halo, halo_ref, out_refs):
@@ -305,8 +317,10 @@
 def add_returned(grad_ref, returned, blocks_ref, total_ref):
     total_ref[...] = grad_ref[...]
     for direction, piece in zip(place(), returned, strict=True):
-        start = pl.multiple_of(blocks_ref[direction] * BLOCK, BLOCK)
-        total_ref[pl.ds(start, BLOCK), :] += piece[...].astype(F32)
+        name = jnp.broadcast_to(listed(blocks_ref, direction), (BLOCK, H))
+        values = piece[...].astype(F32)
+        for block in range(NC_DEV // BLOCK):
+            total_ref[block * BLOCK : (block + 1) * BLOCK, :] += jnp.where(name == block, values, 0.0)
 
 
 def coarse_behind(
@@ -368,21 +382,23 @@
         grads_ref,
         False,
     )
-    for index, source in enumerate((grads_ref, grads_0_ref, grads_1_ref)):
-        packed_ref[index * 5 * H : (index + 1) * 5 * H, :] = source[0 : 5 * H, :]
-        packed_ref[SMALL + index * 8 : SMALL + index * 8 + 8, :] = source[5 * H :, :]
-    packed_ref[SMALL + 24 :, :] = jnp.zeros((PACKED - SMALL - 24, H), F32)
+    sources = (grads_ref, grads_0_ref, grads_1_ref)
+    for index, source in enumerate(sources):
+        packed_ref[index * 5 * H : (index + 1) * 5 * H, :] = source[0 : 5 * H, :].astype(SCATTER_WIRE)
+    small = [source[5 * H :, :] for source in sources]
+    small.append(jnp.zeros((PACKED - SMALL - 24, H), F32))
+    packed_ref[SMALL:, :] = jnp.concatenate(small, axis=0).astype(SCATTER_WIRE)
 
 
 def sum_parts(parts_ref, out_ref):
-    values = [parts_ref[index] for index in range(parts_ref.shape[0])]
+    values = [parts_ref[index].astype(F32) for index in range(parts_ref.shape[0])]
     while len(values) > 1:
         values = [a + b for a, b in zip(values[0::2], values[1::2], strict=True)]
     out_ref[...] = values[0]
 
 
 def sum_and_spread(parts_ref, out_ref):
-    values = [parts_ref[index] for index in range(parts_ref.shape[0])]
+    values = [parts_ref[index].astype(F32) for index in range(parts_ref.shape[0])]
     while len(values) > 1:
         values = [a + b for a, b in zip(values[0::2], values[1::2], strict=True)]
     for index in range(out_ref.shape[0]):
@@ -434,7 +450,7 @@
         in_specs=[smem] * len(scalars) + [vmem] * len(arrays),
         out_specs=[vmem] * len(outs),
         scratch_shapes=[pltpu.VMEM(shape, dtype) for shape, dtype in scratch],
-        compiler_params=pltpu.CompilerParams(vmem_limit_bytes=40 * 1024 * 1024),
+        compiler_params=pltpu.CompilerParams(vmem_limit_bytes=SCOPED),
     )(*scalars, *arrays)
 
 
@@ -448,8 +464,46 @@
     return received
 
 
-def pick(blocks_ref, x_ref, s0, s1, s2, s3):
-    send_blocks(x_ref, blocks_ref, (s0, s1, s2, s3))
+def stage(*refs):
+    blocks_ref, sources = refs[0], refs[1:-2]
+    count = (len(sources) - 4) // 2
+    sources, pieces, targets = sources[:count], sources[count : count + 4], sources[count + 4 :]
+    picks_ref, semaphores = refs[-2:]
+    picking = pltpu.make_async_copy(blocks_ref, picks_ref, semaphores.at[0])
+    picking.start()
+    copies = [
+        pltpu.make_async_copy(source, target, semaphores.at[index])
+        for index, (source, target) in enumerate(zip(sources, targets, strict=True), 1)
+    ]
+    for copy in copies:
+        copy.start()
+    picking.wait()
+    for index, (direction, piece) in enumerate(zip(place(), pieces, strict=True), count + 1):
+        copy = pltpu.make_async_copy(
+            sources[0].at[rows_at(picks_ref[direction], BLOCK), :], piece, semaphores.at[index]
+        )
+        copy.start()
+        copies.append(copy)
+    for copy in copies:
+        copy.wait()
+
+
+def staged(picks, arrays):
+    hbm = pl.BlockSpec(memory_space=pltpu.HBM)
+    vmem = pl.BlockSpec(memory_space=pltpu.VMEM)
+    block = jax.ShapeDtypeStruct((BLOCK, H), BF16)
+    outs = pl.pallas_call(
+        stage,
+        out_shape=[block] * 4 + [jax.ShapeDtypeStruct(a.shape, a.dtype) for a in arrays],
+        in_specs=[hbm] * (1 + len(arrays)),
+        out_specs=[vmem] * (4 + len(arrays)),
+        scratch_shapes=[
+            pltpu.SMEM(picks.shape, jnp.int32),
+            pltpu.SemaphoreType.DMA((5 + len(arrays),)),
+        ],
+        compiler_params=pltpu.CompilerParams(vmem_limit_bytes=SCOPED),
+    )(*[pltpu.with_memory_space_constraint(a, pltpu.HBM) for a in (picks, *arrays)])
+    return outs[:4], outs[4:]
 
 
 def body(
@@ -473,7 +527,7 @@
     live = fine_live.reshape(1)
     pool = pool_map[0]
     coarse_list = coarse_edges[0, 0]
-    blocks = coarse_halo.reshape(4)
+    blocks = coarse_halo.reshape(1, 4)
     cot = cotangent[0, 0]
     bias = fine_bias.reshape(1, H)
     gain = fine_gain.reshape(1, H)
@@ -490,11 +544,18 @@
             ((edge_count, H), F32),
         ]
 
-    halos = exchange(call(pick, [fine_halo.reshape(4)], [x], [block] * 4, []))
+    sends, arrays = staged(
+        fine_halo.reshape(4),
+        [x, edges, pool, coarse_list, blocks, fine_weights, bias, gain]
+        + [coarse_weights, coarse_bias, coarse_gain, cot],
+    )
+    x, edges, pool, coarse_list, blocks, fine_weights, bias, gain = arrays[:8]
+    coarse_weights, coarse_bias, coarse_gain, cot = arrays[8:]
+    halos = exchange(sends)
     fine_out = call(
         fine_ahead,
-        [live, blocks],
-        [x, *halos, edges, pool, fine_weights, bias, gain],
+        [live],
+        [blocks, x, *halos, edges, pool, fine_weights, bias, gain],
         [((rows, H), BF16), ((NC_DEV, H), BF16)] + [block] * 4 + saved(rows, slots),
         [((rows + 4 * BLOCK, H), BF16), ((slots, H), BF16)],
     )
@@ -504,8 +565,8 @@
     halo_grads = ((4 * BLOCK, H), BF16)
     ahead = call(
         coarse_ahead,
-        [blocks],
-        [coarse_0, *halos_0, coarse_list, coarse_weights, coarse_bias, coarse_gain],
+        [],
+        [blocks, coarse_0, *halos_0, coarse_list, coarse_weights, coarse_bias, coarse_gain],
         [((NC_DEV, H), BF16)] + [block] * 4 + saved(NC_DEV, coarse_slots),
         [coarse_extended, ((coarse_slots, H), BF16)],
     )
@@ -524,8 +585,8 @@
     returned = exchange(grad_halo)
     behind = call(
         coarse_behind,
-        [blocks],
-        [grad_nodes, *returned, coarse_0, *halos_0, coarse_list]
+        [],
+        [blocks, grad_nodes, *returned, coarse_0, *halos_0, coarse_list]
         + [coarse_weights, coarse_gain, *coarse_saved],
         [((NC_DEV, H), F32)] + [block] * 4 + [grads],
         [coarse_extended, ((NC_DEV, H), F32), ((coarse_slots, 2 * H), BF16), halo_grads],
@@ -534,10 +595,10 @@
     returned = exchange(grad_halo)
     grad_pooled, packed = call(
         functools.partial(fine_behind, 1.0 / root, root),
-        [live, blocks],
-        [grad_nodes, *returned, x, *halos, edges, pool, cot, fine_weights, gain, *fine_saved]
+        [live],
+        [blocks, grad_nodes, *returned, x, *halos, edges, pool, cot, fine_weights, gain, *fine_saved]
         + [grads_0, grads_1],
-        [((NC_DEV, H), F32), ((PACKED, H), F32)],
+        [((NC_DEV, H), F32), ((PACKED, H), SCATTER_WIRE)],
         [((rows + 4 * BLOCK, H), BF16), ((NC_DEV, H), F32), ((slots, 2 * H), BF16), grads],
     )
     fine_w, coarse_w, fine_b, fine_g, coarse_b, coarse_g = reduce_all(packed)

time: 180 us -> 164 us (0.911)
  local copies, waits for them, and re-layouts: 8.79 us -> 0 us
  blocking collectives: 78.3 us -> 72.7 us
    unnamed x38 -> x0, local copies, waits for them, and re-layouts: 8.79 us -> none
    all_to_all x1, blocking collectives: 22.9 us -> 17.3 us  [reduce_all(): pieces = lax.all_to_all(packed.reshape(across, rows, H), 'gx', 0, 0)]
    pallas_call x10 -> x9, Pallas kernels: 19.5 us -> 16.3 us  [call(): pl.pallas_call(kernel, out_shape=[jax.ShapeDtypeStruct(shape, dtype) for...]
where the time goes in v3:
time: 164 us; the launch traced here: 163 us
  blocking collectives  72.7 us (44%)
  starting transfers between devices  66.2 us (40%)
  Pallas kernels  18 us (11%)
  waiting for transfers between devices  4.6 us (3%)
    ppermute x20, starting transfers between devices, exchange(): received.append(lax.ppermute(piece, axis, pairs))  66.2 us
    all_to_all x1, blocking collectives, reduce_all(): pieces = lax.all_to_all(mine.reshape(along, part, H), 'gy', 0, 0)  25.2 us
    all_to_all x1, blocking collectives, reduce_all(): pieces = lax.all_to_all(packed.reshape(across, rows, H), 'gx', 0, 0)  17.3 us
    pallas_call x9, Pallas kernels, call(): pl.pallas_call(kernel, out_shape=[jax.ShapeDtypeStruct(shape, dtype) for...  16.3 us
    all_to_all x1, blocking collectives, reduce_all(): everything = lax.all_to_all(shared, 'gx', 0, 0).reshape(PACKED, H)  16 us
    all_to_all x1, blocking collectives, reduce_all(): mine = lax.all_to_all(shared, 'gy', 0, 0).reshape(rows, H)  14.1 us
    ppermute x20, waiting for transfers between devices, exchange(): received.append(lax.ppermute(piece, axis, pairs))  4.6 us
  transfers between devices with their start and end apart: 20, of which 7 were waited for; matrix products, arithmetic and copies ran while one was open for 0% of the time, Pallas kernels for 0%

profile of v3, /device:TPU:1, one launch (start us, length us, event | category | flops | bytes accessed | tf_op | source)
XLA Modules:
  0.0 163.1 jit_solution(1496446446467547154)
XLA Ops:
  0.6 1.8 %shard_map.197 = (bf16[128,128]{1,0:T(8,128)(2,1)S(1)}, bf16[128,128]{1,0:T(8,128)(2,1)S(1)}, bf16[128,128]{1,0:T(8,128)(2,1)S(1)}, bf16[128,128]{1,0:T(8,128)(2...) custom-call(s32[4]{0:T(128)} %bitcast.31, ...), custom_call_target="tpu_custom_call" | custom-call | tf_op jit(solution)/shard_map/pallas_call | solution.py:495
  2.4 5.0 %collective-permute-start = (bf16[128,128]{1,0:T(8,128)(2,1)S(1)}, bf16[128,128]{1,0:T(8,128)(2,1)S(1)}, u32[]{:S(2)}, u32[]{:S(2)}) collective-permute-start(bf16[128,128]{1,0:T(8,128)(2,1)S(1)} %get-tuple-element.66), channel_id=1, source_target_pairs={{0,1},{1,0},{2,3},{3,2},{4,5},{5,4},{6,7},{7,6},{8,9},{9,8},{10,11... | collective-permute-start | bytes 98312 | tf_op jit(solution)/shard_map/ppermute | solution.py:463
  7.5 0.7 collective-permute-start.1
  8.1 4.0 %collective-permute-start.2 = (bf16[128,128]{1,0:T(8,128)(2,1)S(1)}, bf16[128,128]{1,0:T(8,128)(2,1)S(1)}, u32[]{:S(2)}, u32[]{:S(2)}) collective-permute-start(bf16[128,128]{1,0:T(8,128)(2,1)S(1)} %get-tuple-element.68), channel_id=1, source_target_pairs={{32,64},{64,32},{96,128},{128,96},{160,192},{192,160},{224,256},{2... | collective-permute-start | bytes 98312 | tf_op jit(solution)/shard_map/ppermute | solution.py:463
  12.1 2.3 %collective-permute-start.3 = (bf16[128,128]{1,0:T(8,128)(2,1)S(1)}, bf16[128,128]{1,0:T(8,128)(2,1)S(1)}, u32[]{:S(2)}, u32[]{:S(2)}) collective-permute-start(bf16[128,128]{1,0:T(8,128)(2,1)S(1)} %get-tuple-element.69), channel_id=1, source_target_pairs={{0,32},{32,0},{64,96},{96,64},{128,160},{160,128},{192,224},{224,1... | collective-permute-start | bytes 98312 | tf_op jit(solution)/shard_map/ppermute | solution.py:463
  15.1 0.0 collective-permute-done.h0
  15.1 0.0 collective-permute-done.1.h1
  15.1 0.2 collective-permute-done.3.h3
  15.3 2.8 %shard_map.198 = (bf16[512,128]{1,0:T(8,128)(2,1)S(1)}, bf16[256,128]{1,0:T(8,128)(2,1)S(1)}, bf16[128,128]{1,0:T(8,128)(2,1)S(1)}, bf16[128,128]{1,0:T(8,128)(2...) custom-call(s32[1]{0:T(128)} %bitcast.20.live_ref, ...), custom_call_target="tpu_custom_call" | custom-call | tf_op jit(solution)/shard_map/pallas_call | solution.py:447
  18.1 7.4 %collective-permute-start.4 = (bf16[128,128]{1,0:T(8,128)(2,1)S(1)}, bf16[128,128]{1,0:T(8,128)(2,1)S(1)}, u32[]{:S(2)}, u32[]{:S(2)}) collective-permute-start(bf16[128,128]{1,0:T(8,128)(2,1)S(1)} %get-tuple-element.76), channel_id=1, source_target_pairs={{0,1},{1,0},{2,3},{3,2},{4,5},{5,4},{6,7},{7,6},{8,9},{9,8},{10,11... | collective-permute-start | bytes 98312 | tf_op jit(solution)/shard_map/ppermute | solution.py:463
  25.5 0.7 collective-permute-start.5
  26.2 3.4 %collective-permute-start.6 = (bf16[128,128]{1,0:T(8,128)(2,1)S(1)}, bf16[128,128]{1,0:T(8,128)(2,1)S(1)}, u32[]{:S(2)}, u32[]{:S(2)}) collective-permute-start(bf16[128,128]{1,0:T(8,128)(2,1)S(1)} %get-tuple-element.78), channel_id=1, source_target_pairs={{32,64},{64,32},{96,128},{128,96},{160,192},{192,160},{224,256},{2... | collective-permute-start | bytes 98312 | tf_op jit(solution)/shard_map/ppermute | solution.py:463
  29.6 1.9 %collective-permute-start.7 = (bf16[128,128]{1,0:T(8,128)(2,1)S(1)}, bf16[128,128]{1,0:T(8,128)(2,1)S(1)}, u32[]{:S(2)}, u32[]{:S(2)}) collective-permute-start(bf16[128,128]{1,0:T(8,128)(2,1)S(1)} %get-tuple-element.79), channel_id=1, source_target_pairs={{0,32},{32,0},{64,96},{96,64},{128,160},{160,128},{192,224},{224,1... | collective-permute-start | bytes 98312 | tf_op jit(solution)/shard_map/ppermute | solution.py:463
  31.5 0.0 collective-permute-done.4.h0
  31.6 0.0 collective-permute-done.5.h1
  31.6 1.1 collective-permute-done.7.h3
  32.7 2.3 %shard_map.199 = (bf16[256,128]{1,0:T(8,128)(2,1)S(1)}, bf16[128,128]{1,0:T(8,128)(2,1)S(1)}, bf16[128,128]{1,0:T(8,128)(2,1)S(1)}, bf16[128,128]{1,0:T(8,128)(2...) custom-call(s32[1,4]{1,0:T(1,128)S(1)} %get-tuple-element.64.blocks_, ...), custom_call_target="tpu_custom_call" | custom-call | tf_op jit(solution)/shard_map/pallas_call | solution.py:447
  35.0 7.2 %collective-permute-start.8 = (bf16[128,128]{1,0:T(8,128)(2,1)S(1)}, bf16[128,128]{1,0:T(8,128)(2,1)S(1)}, u32[]{:S(2)}, u32[]{:S(2)}) collective-permute-start(bf16[128,128]{1,0:T(8,128)(2,1)S(1)} %get-tuple-element.85), channel_id=1, source_target_pairs={{0,1},{1,0},{2,3},{3,2},{4,5},{5,4},{6,7},{7,6},{8,9},{9,8},{10,11... | collective-permute-start | bytes 98312 | tf_op jit(solution)/shard_map/ppermute | solution.py:463
  42.2 0.7 collective-permute-start.9
  42.8 3.1 %collective-permute-start.10 = (bf16[128,128]{1,0:T(8,128)(2,1)S(1)}, bf16[128,128]{1,0:T(8,128)(2,1)S(1)}, u32[]{:S(2)}, u32[]{:S(2)}) collective-permute-start(bf16[128,128]{1,0:T(8,128)(2,1)S(1)} %get-tuple-element.87), channel_id=1, source_target_pairs={{32,64},{64,32},{96,128},{128,96},{160,192},{192,160},{224,256},{2... | collective-permute-start | bytes 98312 | tf_op jit(solution)/shard_map/ppermute | solution.py:463
  46.0 1.9 %collective-permute-start.11 = (bf16[128,128]{1,0:T(8,128)(2,1)S(1)}, bf16[128,128]{1,0:T(8,128)(2,1)S(1)}, u32[]{:S(2)}, u32[]{:S(2)}) collective-permute-start(bf16[128,128]{1,0:T(8,128)(2,1)S(1)} %get-tuple-element.88), channel_id=1, source_target_pairs={{0,32},{32,0},{64,96},{96,64},{128,160},{160,128},{192,224},{224,1... | collective-permute-start | bytes 98312 | tf_op jit(solution)/shard_map/ppermute | solution.py:463
  47.9 0.0 collective-permute-done.8.h0
  47.9 0.0 collective-permute-done.9.h1
  47.9 0.2 collective-permute-done.10.h2
  48.1 1.0 collective-permute-done.11.h3
  49.1 4.6 %shard_map.200 = (bf16[512,128]{1,0:T(8,128)(2,1)}, f32[256,128]{1,0:T(8,128)S(1)}, bf16[128,128]{1,0:T(8,128)(2,1)S(1)}, bf16[128,128]{1,0:T(8,128)(2,1)S(1)}, ...) custom-call(bf16[256,128]{1,0:T(8,128)(2,1)S(1)} %get-tuple-element.84.x_ref, ...), custom_call_target="tpu_custom_call" | custom-call | tf_op jit(solution)/shard_map/pallas_call | solution.py:447
  53.7 7.4 %collective-permute-start.12 = (bf16[128,128]{1,0:T(8,128)(2,1)S(1)}, bf16[128,128]{1,0:T(8,128)(2,1)S(1)}, u32[]{:S(2)}, u32[]{:S(2)}) collective-permute-start(bf16[128,128]{1,0:T(8,128)(2,1)S(1)} %get-tuple-element.93), channel_id=1, source_target_pairs={{0,1},{1,0},{2,3},{3,2},{4,5},{5,4},{6,7},{7,6},{8,9},{9,8},{10,11... | collective-permute-start | bytes 98312 | tf_op jit(solution)/shard_map/ppermute | solution.py:463
  61.2 0.7 collective-permute-start.13
  61.9 2.6 %collective-permute-start.14 = (bf16[128,128]{1,0:T(8,128)(2,1)S(1)}, bf16[128,128]{1,0:T(8,128)(2,1)S(1)}, u32[]{:S(2)}, u32[]{:S(2)}) collective-permute-start(bf16[128,128]{1,0:T(8,128)(2,1)S(1)} %get-tuple-element.95), channel_id=1, source_target_pairs={{32,64},{64,32},{96,128},{128,96},{160,192},{192,160},{224,256},{2... | collective-permute-start | bytes 98312 | tf_op jit(solution)/shard_map/ppermute | solution.py:463
  64.4 2.1 %collective-permute-start.15 = (bf16[128,128]{1,0:T(8,128)(2,1)S(1)}, bf16[128,128]{1,0:T(8,128)(2,1)S(1)}, u32[]{:S(2)}, u32[]{:S(2)}) collective-permute-start(bf16[128,128]{1,0:T(8,128)(2,1)S(1)} %get-tuple-element.96), channel_id=1, source_target_pairs={{0,32},{32,0},{64,96},{96,64},{128,160},{160,128},{192,224},{224,1... | collective-permute-start | bytes 98312 | tf_op jit(solution)/shard_map/ppermute | solution.py:463
  66.5 0.0 collective-permute-done.12.r0
  66.6 0.0 collective-permute-done.13.r1
  66.6 0.5 collective-permute-done.14.r2
  67.1 0.4 collective-permute-done.15.r3
  67.5 2.5 %shard_map.201 = (f32[256,128]{1,0:T(8,128)S(1)}, bf16[128,128]{1,0:T(8,128)(2,1)S(1)}, bf16[128,128]{1,0:T(8,128)(2,1)S(1)}, bf16[128,128]{1,0:T(8,128)(2,1)S(1...) custom-call(s32[1,4]{1,0:T(1,128)S(1)} %get-tuple-element.64.blocks_ref, ...), custom_call_target="tpu_custom_call" | custom-call | tf_op jit(solution)/shard_map/pallas_call | solution.py:447
  70.1 8.0 %collective-permute-start.16 = (bf16[128,128]{1,0:T(8,128)(2,1)S(1)}, bf16[128,128]{1,0:T(8,128)(2,1)S(1)}, u32[]{:S(2)}, u32[]{:S(2)}) collective-permute-start(bf16[128,128]{1,0:T(8,128)(2,1)S(1)} %get-tuple-element.102), channel_id=1, source_target_pairs={{0,1},{1,0},{2,3},{3,2},{4,5},{5,4},{6,7},{7,6},{8,9},{9,8},{10,11... | collective-permute-start | bytes 98312 | tf_op jit(solution)/shard_map/ppermute | solution.py:463
  78.1 0.7 collective-permute-start.17
  78.8 4.5 %collective-permute-start.18 = (bf16[128,128]{1,0:T(8,128)(2,1)S(1)}, bf16[128,128]{1,0:T(8,128)(2,1)S(1)}, u32[]{:S(2)}, u32[]{:S(2)}) collective-permute-start(bf16[128,128]{1,0:T(8,128)(2,1)S(1)} %get-tuple-element.104), channel_id=1, source_target_pairs={{32,64},{64,32},{96,128},{128,96},{160,192},{192,160},{224,256},{2... | collective-permute-start | bytes 98312 | tf_op jit(solution)/shard_map/ppermute | solution.py:463
  83.3 1.9 %collective-permute-start.19 = (bf16[128,128]{1,0:T(8,128)(2,1)S(1)}, bf16[128,128]{1,0:T(8,128)(2,1)S(1)}, u32[]{:S(2)}, u32[]{:S(2)}) collective-permute-start(bf16[128,128]{1,0:T(8,128)(2,1)S(1)} %get-tuple-element.105), channel_id=1, source_target_pairs={{0,32},{32,0},{64,96},{96,64},{128,160},{160,128},{192,224},{224,1... | collective-permute-start | bytes 98312 | tf_op jit(solution)/shard_map/ppermute | solution.py:463
  85.2 0.0 collective-permute-done.17.r1
  85.3 1.1 collective-permute-done.19.r3
  86.4 2.9 %shard_map.202 = (f32[256,128]{1,0:T(8,128)}, bf16[2048,128]{1,0:T(8,128)(2,1)S(1)}) custom-call(s32[1]{0:T(128)} %bitcast.21.live_ref, s32[1,4]{1,0:T(1,128)S(1)} %get-tuple-element.64.blocks_ref, f32[256,128]{1,0:T(8,128)S(1)} %get-tuple-element.101.grad_in_ref, bf16[128,128]{1,0:T(8,128)(2,1)S(1)} %collective-permute-done.16.r0, ...), custom_call_target="tpu_custom_call" | custom-call | tf_op jit(solution)/shard_map/pallas_call | solution.py:447
  89.3 17.3 %all_to_all.20.parts_ref = bf16[16,128,128]{2,1,0:T(8,128)(2,1)S(1)} all-to-all(bf16[16,128,128]{2,1,0:T(8,128)(2,1)S(1)} %bitcast.23), channel_id=1, replica_groups=mesh['gx'=16,'gy'=32] {'gx'}, dimensions={0} | all-to-all | bytes 1048576 | tf_op jit(solution)/shard_map/all_to_all | solution.py:428
  106.6 0.1 shard_map.203
  106.7 25.2 %all_to_all.21.parts_ref = f32[32,4,128]{2,1,0:T(4,128)S(1)} all-to-all(f32[32,4,128]{2,1,0:T(4,128)S(1)} %bitcast.24), channel_id=1, replica_groups=mesh['gx'=16,'gy'=32] {'gy'}, dimensions={0} | all-to-all | bytes 131072 | tf_op jit(solution)/shard_map/all_to_all | solution.py:430
  131.9 14.1 %all_to_all.22 = f32[32,4,128]{2,1,0:T(4,128)S(1)} all-to-all(f32[32,4,128]{2,1,0:T(4,128)S(1)} %shard_map.204), channel_id=1, replica_groups=mesh['gx'=16,'gy'=32] {'gy'}, dimensions={0} | all-to-all | bytes 131072 | tf_op jit(solution)/shard_map/all_to_all | solution.py:432
  146.1 16.0 %all_to_all.23 = bf16[16,128,128]{2,1,0:T(8,128)(2,1)S(1)} all-to-all(bf16[16,128,128]{2,1,0:T(8,128)(2,1)S(1)} %shard_map.205), channel_id=1, replica_groups=mesh['gx'=16,'gy'=32] {'gx'}, dimensions={0} | all-to-all | bytes 1048576 | tf_op jit(solution)/shard_map/all_to_all | solution.py:434
  162.1 1.0 shard_map.206
  (6 shorter events, 0.1 us)
Async XLA Ops:
  2.4 12.7 %collective-permute-start = (bf16[128,128]{1,0:T(8,128)(2,1)S(1)}, bf16[128,128]{1,0:T(8,128)(2,1)S(1)}, u32[]{:S(2)}, u32[]{:S(2)}) collective-permute-start(bf16[128,128]{1,0:T(8,128)(2,1)S(1)} %get-tuple-element.66), channel_id=1, source_target_pairs={{0,1},{1,0},{2,3},{3,2},{4,5},{5,4},{6,7},{7,6},{8,9},{9,8},{10,11... | collective-permute-start | bytes 98312 | tf_op jit(solution)/shard_map/ppermute | solution.py:463
  7.5 7.7 %collective-permute-start.1 = (bf16[128,128]{1,0:T(8,128)(2,1)S(1)}, bf16[128,128]{1,0:T(8,128)(2,1)S(1)}, u32[]{:S(2)}, u32[]{:S(2)}) collective-permute-start(bf16[128,128]{1,0:T(8,128)(2,1)S(1)} %get-tuple-element.67), channel_id=1, source_target_pairs={{1,2},{2,1},{3,4},{4,3},{5,6},{6,5},{7,8},{8,7},{9,10},{10,9},{11,... | collective-permute-start | bytes 98312 | tf_op jit(solution)/shard_map/ppermute | solution.py:463
  8.1 7.0 %collective-permute-start.2 = (bf16[128,128]{1,0:T(8,128)(2,1)S(1)}, bf16[128,128]{1,0:T(8,128)(2,1)S(1)}, u32[]{:S(2)}, u32[]{:S(2)}) collective-permute-start(bf16[128,128]{1,0:T(8,128)(2,1)S(1)} %get-tuple-element.68), channel_id=1, source_target_pairs={{32,64},{64,32},{96,128},{128,96},{160,192},{192,160},{224,256},{2... | collective-permute-start | bytes 98312 | tf_op jit(solution)/shard_map/ppermute | solution.py:463
  12.1 3.2 %collective-permute-start.3 = (bf16[128,128]{1,0:T(8,128)(2,1)S(1)}, bf16[128,128]{1,0:T(8,128)(2,1)S(1)}, u32[]{:S(2)}, u32[]{:S(2)}) collective-permute-start(bf16[128,128]{1,0:T(8,128)(2,1)S(1)} %get-tuple-element.69), channel_id=1, source_target_pairs={{0,32},{32,0},{64,96},{96,64},{128,160},{160,128},{192,224},{224,1... | collective-permute-start | bytes 98312 | tf_op jit(solution)/shard_map/ppermute | solution.py:463
  18.1 13.4 %collective-permute-start.4 = (bf16[128,128]{1,0:T(8,128)(2,1)S(1)}, bf16[128,128]{1,0:T(8,128)(2,1)S(1)}, u32[]{:S(2)}, u32[]{:S(2)}) collective-permute-start(bf16[128,128]{1,0:T(8,128)(2,1)S(1)} %get-tuple-element.76), channel_id=1, source_target_pairs={{0,1},{1,0},{2,3},{3,2},{4,5},{5,4},{6,7},{7,6},{8,9},{9,8},{10,11... | collective-permute-start | bytes 98312 | tf_op jit(solution)/shard_map/ppermute | solution.py:463
  25.5 6.1 %collective-permute-start.5 = (bf16[128,128]{1,0:T(8,128)(2,1)S(1)}, bf16[128,128]{1,0:T(8,128)(2,1)S(1)}, u32[]{:S(2)}, u32[]{:S(2)}) collective-permute-start(bf16[128,128]{1,0:T(8,128)(2,1)S(1)} %get-tuple-element.77), channel_id=1, source_target_pairs={{1,2},{2,1},{3,4},{4,3},{5,6},{6,5},{7,8},{8,7},{9,10},{10,9},{11,... | collective-permute-start | bytes 98312 | tf_op jit(solution)/shard_map/ppermute | solution.py:463
  26.2 5.4 %collective-permute-start.6 = (bf16[128,128]{1,0:T(8,128)(2,1)S(1)}, bf16[128,128]{1,0:T(8,128)(2,1)S(1)}, u32[]{:S(2)}, u32[]{:S(2)}) collective-permute-start(bf16[128,128]{1,0:T(8,128)(2,1)S(1)} %get-tuple-element.78), channel_id=1, source_target_pairs={{32,64},{64,32},{96,128},{128,96},{160,192},{192,160},{224,256},{2... | collective-permute-start | bytes 98312 | tf_op jit(solution)/shard_map/ppermute | solution.py:463
  29.6 3.1 %collective-permute-start.7 = (bf16[128,128]{1,0:T(8,128)(2,1)S(1)}, bf16[128,128]{1,0:T(8,128)(2,1)S(1)}, u32[]{:S(2)}, u32[]{:S(2)}) collective-permute-start(bf16[128,128]{1,0:T(8,128)(2,1)S(1)} %get-tuple-element.79), channel_id=1, source_target_pairs={{0,32},{32,0},{64,96},{96,64},{128,160},{160,128},{192,224},{224,1... | collective-permute-start | bytes 98312 | tf_op jit(solution)/shard_map/ppermute | solution.py:463
  35.0 12.9 %collective-permute-start.8 = (bf16[128,128]{1,0:T(8,128)(2,1)S(1)}, bf16[128,128]{1,0:T(8,128)(2,1)S(1)}, u32[]{:S(2)}, u32[]{:S(2)}) collective-permute-start(bf16[128,128]{1,0:T(8,128)(2,1)S(1)} %get-tuple-element.85), channel_id=1, source_target_pairs={{0,1},{1,0},{2,3},{3,2},{4,5},{5,4},{6,7},{7,6},{8,9},{9,8},{10,11... | collective-permute-start | bytes 98312 | tf_op jit(solution)/shard_map/ppermute | solution.py:463
  42.2 5.7 %collective-permute-start.9 = (bf16[128,128]{1,0:T(8,128)(2,1)S(1)}, bf16[128,128]{1,0:T(8,128)(2,1)S(1)}, u32[]{:S(2)}, u32[]{:S(2)}) collective-permute-start(bf16[128,128]{1,0:T(8,128)(2,1)S(1)} %get-tuple-element.86), channel_id=1, source_target_pairs={{1,2},{2,1},{3,4},{4,3},{5,6},{6,5},{7,8},{8,7},{9,10},{10,9},{11,... | collective-permute-start | bytes 98312 | tf_op jit(solution)/shard_map/ppermute | solution.py:463
  42.8 5.2 %collective-permute-start.10 = (bf16[128,128]{1,0:T(8,128)(2,1)S(1)}, bf16[128,128]{1,0:T(8,128)(2,1)S(1)}, u32[]{:S(2)}, u32[]{:S(2)}) collective-permute-start(bf16[128,128]{1,0:T(8,128)(2,1)S(1)} %get-tuple-element.87), channel_id=1, source_target_pairs={{32,64},{64,32},{96,128},{128,96},{160,192},{192,160},{224,256},{2... | collective-permute-start | bytes 98312 | tf_op jit(solution)/shard_map/ppermute | solution.py:463
  46.0 3.1 %collective-permute-start.11 = (bf16[128,128]{1,0:T(8,128)(2,1)S(1)}, bf16[128,128]{1,0:T(8,128)(2,1)S(1)}, u32[]{:S(2)}, u32[]{:S(2)}) collective-permute-start(bf16[128,128]{1,0:T(8,128)(2,1)S(1)} %get-tuple-element.88), channel_id=1, source_target_pairs={{0,32},{32,0},{64,96},{96,64},{128,160},{160,128},{192,224},{224,1... | collective-permute-start | bytes 98312 | tf_op jit(solution)/shard_map/ppermute | solution.py:463
  53.7 12.8 %collective-permute-start.12 = (bf16[128,128]{1,0:T(8,128)(2,1)S(1)}, bf16[128,128]{1,0:T(8,128)(2,1)S(1)}, u32[]{:S(2)}, u32[]{:S(2)}) collective-permute-start(bf16[128,128]{1,0:T(8,128)(2,1)S(1)} %get-tuple-element.93), channel_id=1, source_target_pairs={{0,1},{1,0},{2,3},{3,2},{4,5},{5,4},{6,7},{7,6},{8,9},{9,8},{10,11... | collective-permute-start | bytes 98312 | tf_op jit(solution)/shard_map/ppermute | solution.py:463
  61.2 5.4 %collective-permute-start.13 = (bf16[128,128]{1,0:T(8,128)(2,1)S(1)}, bf16[128,128]{1,0:T(8,128)(2,1)S(1)}, u32[]{:S(2)}, u32[]{:S(2)}) collective-permute-start(bf16[128,128]{1,0:T(8,128)(2,1)S(1)} %get-tuple-element.94), channel_id=1, source_target_pairs={{1,2},{2,1},{3,4},{4,3},{5,6},{6,5},{7,8},{8,7},{9,10},{10,9},{11,... | collective-permute-start | bytes 98312 | tf_op jit(solution)/shard_map/ppermute | solution.py:463
  61.9 5.2 %collective-permute-start.14 = (bf16[128,128]{1,0:T(8,128)(2,1)S(1)}, bf16[128,128]{1,0:T(8,128)(2,1)S(1)}, u32[]{:S(2)}, u32[]{:S(2)}) collective-permute-start(bf16[128,128]{1,0:T(8,128)(2,1)S(1)} %get-tuple-element.95), channel_id=1, source_target_pairs={{32,64},{64,32},{96,128},{128,96},{160,192},{192,160},{224,256},{2... | collective-permute-start | bytes 98312 | tf_op jit(solution)/shard_map/ppermute | solution.py:463
  64.4 3.1 %collective-permute-start.15 = (bf16[128,128]{1,0:T(8,128)(2,1)S(1)}, bf16[128,128]{1,0:T(8,128)(2,1)S(1)}, u32[]{:S(2)}, u32[]{:S(2)}) collective-permute-start(bf16[128,128]{1,0:T(8,128)(2,1)S(1)} %get-tuple-element.96), channel_id=1, source_target_pairs={{0,32},{32,0},{64,96},{96,64},{128,160},{160,128},{192,224},{224,1... | collective-permute-start | bytes 98312 | tf_op jit(solution)/shard_map/ppermute | solution.py:463
  70.1 15.2 %collective-permute-start.16 = (bf16[128,128]{1,0:T(8,128)(2,1)S(1)}, bf16[128,128]{1,0:T(8,128)(2,1)S(1)}, u32[]{:S(2)}, u32[]{:S(2)}) collective-permute-start(bf16[128,128]{1,0:T(8,128)(2,1)S(1)} %get-tuple-element.102), channel_id=1, source_target_pairs={{0,1},{1,0},{2,3},{3,2},{4,5},{5,4},{6,7},{7,6},{8,9},{9,8},{10,11... | collective-permute-start | bytes 98312 | tf_op jit(solution)/shard_map/ppermute | solution.py:463
  78.1 7.1 %collective-permute-start.17 = (bf16[128,128]{1,0:T(8,128)(2,1)S(1)}, bf16[128,128]{1,0:T(8,128)(2,1)S(1)}, u32[]{:S(2)}, u32[]{:S(2)}) collective-permute-start(bf16[128,128]{1,0:T(8,128)(2,1)S(1)} %get-tuple-element.103), channel_id=1, source_target_pairs={{1,2},{2,1},{3,4},{4,3},{5,6},{6,5},{7,8},{8,7},{9,10},{10,9},{11,... | collective-permute-start | bytes 98312 | tf_op jit(solution)/shard_map/ppermute | solution.py:463
  78.8 6.5 %collective-permute-start.18 = (bf16[128,128]{1,0:T(8,128)(2,1)S(1)}, bf16[128,128]{1,0:T(8,128)(2,1)S(1)}, u32[]{:S(2)}, u32[]{:S(2)}) collective-permute-start(bf16[128,128]{1,0:T(8,128)(2,1)S(1)} %get-tuple-element.104), channel_id=1, source_target_pairs={{32,64},{64,32},{96,128},{128,96},{160,192},{192,160},{224,256},{2... | collective-permute-start | bytes 98312 | tf_op jit(solution)/shard_map/ppermute | solution.py:463
  83.3 3.1 %collective-permute-start.19 = (bf16[128,128]{1,0:T(8,128)(2,1)S(1)}, bf16[128,128]{1,0:T(8,128)(2,1)S(1)}, u32[]{:S(2)}, u32[]{:S(2)}) collective-permute-start(bf16[128,128]{1,0:T(8,128)(2,1)S(1)} %get-tuple-element.105), channel_id=1, source_target_pairs={{0,32},{32,0},{64,96},{96,64},{128,160},{160,128},{192,224},{224,1... | collective-permute-start | bytes 98312 | tf_op jit(solution)/shard_map/ppermute | solution.py:463

commit v4 on v3

--- a/solution.py
+++ b/solution.py
@@ -61,19 +61,25 @@
 def one_hot_rows(row, width):
     spread = column_of(row)
     spread = spread - lax.broadcasted_iota(jnp.int32, spread.shape, 1)
-    tiles = [jnp.where(spread == start, 1.0, 0.0).astype(BF16) for start in range(0, width, 128)]
+    spread = spread.astype(jnp.int16)
+    one, zero = jnp.ones(spread.shape, BF16), jnp.zeros(spread.shape, BF16)
+    tiles = [jnp.where(spread == start, one, zero) for start in range(0, width, 128)]
     return jnp.concatenate(tiles, axis=1)
 
 
 def one_hot_columns(row, first, count):
     shape = (count, row.shape[1])
-    marks = lax.broadcasted_iota(jnp.int32, shape, 0) + first == jnp.broadcast_to(row, shape)
-    return jnp.where(marks, 1.0, 0.0).astype(BF16)
+    wanted = jnp.broadcast_to(row - first, (128, row.shape[1]))
+    spread = (wanted - lax.broadcasted_iota(jnp.int32, wanted.shape, 0)).astype(jnp.int16)
+    one, zero = jnp.ones(spread.shape, BF16), jnp.zeros(spread.shape, BF16)
+    return jnp.concatenate(
+        [jnp.where(spread == start, one, zero) for start in range(0, count, 128)], axis=0
+    )
 
 
 def place():
     across, along = lax.axis_index("gx") % 2, lax.axis_index("gy") % 2
-    return (3 - along, 2 + along, across, 1 - across)
+    return (2 + along, across, 3 - along, 1 - across)
 
 
 def rows_at(index, count):
@@ -456,7 +462,7 @@
 
 def exchange(pieces):
     received = []
-    for piece, (axis, first) in zip(pieces, (("gy", 0), ("gy", 1), ("gx", 1), ("gx", 0)), strict=True):
+    for piece, (axis, first) in zip(pieces, (("gy", 1), ("gx", 1), ("gy", 0), ("gx", 0)), strict=True):
         pairs = []
         for i in range(first, lax.axis_size(axis) - 1, 2):
             pairs += [(i, i + 1), (i + 1, i)]
@@ -478,13 +484,10 @@
     for copy in copies:
         copy.start()
     picking.wait()
-    for index, (direction, piece) in enumerate(zip(place(), pieces, strict=True), count + 1):
-        copy = pltpu.make_async_copy(
-            sources[0].at[rows_at(picks_ref[direction], BLOCK), :], piece, semaphores.at[index]
-        )
-        copy.start()
-        copies.append(copy)
-    for copy in copies:
+    copies[0].wait()
+    for direction, piece in zip(place(), pieces, strict=True):
+        piece[...] = targets[0][rows_at(picks_ref[direction], BLOCK), :]
+    for copy in copies[1:]:
         copy.wait()
 
 
@@ -499,7 +502,7 @@
         out_specs=[vmem] * (4 + len(arrays)),
         scratch_shapes=[
             pltpu.SMEM(picks.shape, jnp.int32),
-            pltpu.SemaphoreType.DMA((5 + len(arrays),)),
+            pltpu.SemaphoreType.DMA((1 + len(arrays),)),
         ],
         compiler_params=pltpu.CompilerParams(vmem_limit_bytes=SCOPED),
     )(*[pltpu.with_memory_space_constraint(a, pltpu.HBM) for a in (picks, *arrays)])

time: 164 us -> 162 us (0.988)
  blocking collectives: 72.7 us -> 67.8 us
  starting transfers between devices: 66.2 us -> 69.3 us
    all_to_all x1, blocking collectives: 25.2 us -> 22.1 us  [reduce_all(): pieces = lax.all_to_all(mine.reshape(along, part, H), 'gy', 0, 0)]
    ppermute x20, starting transfers between devices: 66.2 us -> 69.3 us  [exchange(): received.append(lax.ppermute(piece, axis, pairs))]
    all_to_all x1, blocking collectives: 17.3 us -> 15.6 us  [reduce_all(): pieces = lax.all_to_all(packed.reshape(across, rows, H), 'gx', 0, 0)]
  transfers between devices with their start and end apart: 20 -> 20, of which waited for: 7 -> 5; matrix products, arithmetic and copies ran while one was open for 0% -> 0% of each run, Pallas kernels for 0% -> 0%
where the time goes in v4:
time: 162 us; the launch traced here: 161 us
  starting transfers between devices  69.3 us (43%)
  blocking collectives  67.8 us (42%)
  Pallas kernels  17.5 us (11%)
  waiting for transfers between devices  4.92 us (3%)
    ppermute x20, starting transfers between devices, exchange(): received.append(lax.ppermute(piece, axis, pairs))  69.3 us
    all_to_all x1, blocking collectives, reduce_all(): pieces = lax.all_to_all(mine.reshape(along, part, H), 'gy', 0, 0)  22.1 us
    pallas_call x9, Pallas kernels, call(): pl.pallas_call(kernel, out_shape=[jax.ShapeDtypeStruct(shape, dtype) for...  16.2 us
    all_to_all x1, blocking collectives, reduce_all(): everything = lax.all_to_all(shared, 'gx', 0, 0).reshape(PACKED, H)  16 us
    all_to_all x1, blocking collectives, reduce_all(): pieces = lax.all_to_all(packed.reshape(across, rows, H), 'gx', 0, 0)  15.6 us
    all_to_all x1, blocking collectives, reduce_all(): mine = lax.all_to_all(shared, 'gy', 0, 0).reshape(rows, H)  14.1 us
    ppermute x20, waiting for transfers between devices, exchange(): received.append(lax.ppermute(piece, axis, pairs))  4.92 us
  transfers between devices with their start and end apart: 20, of which 5 were waited for; matrix products, arithmetic and copies ran while one was open for 0% of the time, Pallas kernels for 0%

profile of v4, /device:TPU:1, one launch (start us, length us, event | category | flops | bytes accessed | tf_op | source)
XLA Modules:
  0.0 161.2 jit_solution(4096778848682295616)
XLA Ops:
  0.6 1.4 shard_map.197
  2.0 0.7 collective-permute-start
  2.7 4.5 %collective-permute-start.1 = (bf16[128,128]{1,0:T(8,128)(2,1)S(1)}, bf16[128,128]{1,0:T(8,128)(2,1)S(1)}, u32[]{:S(2)}, u32[]{:S(2)}) collective-permute-start(bf16[128,128]{1,0:T(8,128)(2,1)S(1)} %get-tuple-element.67), channel_id=1, source_target_pairs={{32,64},{64,32},{96,128},{128,96},{160,192},{192,160},{224,256},{2... | collective-permute-start | bytes 98312 | tf_op jit(solution)/shard_map/ppermute | solution.py:469
  7.2 9.3 %collective-permute-start.2 = (bf16[128,128]{1,0:T(8,128)(2,1)S(1)}, bf16[128,128]{1,0:T(8,128)(2,1)S(1)}, u32[]{:S(2)}, u32[]{:S(2)}) collective-permute-start(bf16[128,128]{1,0:T(8,128)(2,1)S(1)} %get-tuple-element.68), channel_id=1, source_target_pairs={{0,1},{1,0},{2,3},{3,2},{4,5},{5,4},{6,7},{7,6},{8,9},{9,8},{10,11... | collective-permute-start | bytes 98312 | tf_op jit(solution)/shard_map/ppermute | solution.py:469
  16.5 1.9 %collective-permute-start.3 = (bf16[128,128]{1,0:T(8,128)(2,1)S(1)}, bf16[128,128]{1,0:T(8,128)(2,1)S(1)}, u32[]{:S(2)}, u32[]{:S(2)}) collective-permute-start(bf16[128,128]{1,0:T(8,128)(2,1)S(1)} %get-tuple-element.69), channel_id=1, source_target_pairs={{0,32},{32,0},{64,96},{96,64},{128,160},{160,128},{192,224},{224,1... | collective-permute-start | bytes 98312 | tf_op jit(solution)/shard_map/ppermute | solution.py:469
  19.1 0.0 collective-permute-done.h0
  19.1 0.0 collective-permute-done.1.h1
  19.1 0.0 collective-permute-done.2.h2
  19.1 0.5 collective-permute-done.3.h3
  19.6 2.7 %shard_map.198 = (bf16[512,128]{1,0:T(8,128)(2,1)S(1)}, bf16[256,128]{1,0:T(8,128)(2,1)S(1)}, bf16[128,128]{1,0:T(8,128)(2,1)S(1)}, bf16[128,128]{1,0:T(8,128)(2...) custom-call(s32[1]{0:T(128)} %bitcast.20.live_ref, ...), custom_call_target="tpu_custom_call" | custom-call | tf_op jit(solution)/shard_map/pallas_call | solution.py:453
  22.3 0.7 collective-permute-start.4
  23.0 3.2 %collective-permute-start.5 = (bf16[128,128]{1,0:T(8,128)(2,1)S(1)}, bf16[128,128]{1,0:T(8,128)(2,1)S(1)}, u32[]{:S(2)}, u32[]{:S(2)}) collective-permute-start(bf16[128,128]{1,0:T(8,128)(2,1)S(1)} %get-tuple-element.77), channel_id=1, source_target_pairs={{32,64},{64,32},{96,128},{128,96},{160,192},{192,160},{224,256},{2... | collective-permute-start | bytes 98312 | tf_op jit(solution)/shard_map/ppermute | solution.py:469
  26.2 5.4 %collective-permute-start.6 = (bf16[128,128]{1,0:T(8,128)(2,1)S(1)}, bf16[128,128]{1,0:T(8,128)(2,1)S(1)}, u32[]{:S(2)}, u32[]{:S(2)}) collective-permute-start(bf16[128,128]{1,0:T(8,128)(2,1)S(1)} %get-tuple-element.78), channel_id=1, source_target_pairs={{0,1},{1,0},{2,3},{3,2},{4,5},{5,4},{6,7},{7,6},{8,9},{9,8},{10,11... | collective-permute-start | bytes 98312 | tf_op jit(solution)/shard_map/ppermute | solution.py:469
  31.5 1.9 %collective-permute-start.7 = (bf16[128,128]{1,0:T(8,128)(2,1)S(1)}, bf16[128,128]{1,0:T(8,128)(2,1)S(1)}, u32[]{:S(2)}, u32[]{:S(2)}) collective-permute-start(bf16[128,128]{1,0:T(8,128)(2,1)S(1)} %get-tuple-element.79), channel_id=1, source_target_pairs={{0,32},{32,0},{64,96},{96,64},{128,160},{160,128},{192,224},{224,1... | collective-permute-start | bytes 98312 | tf_op jit(solution)/shard_map/ppermute | solution.py:469
  33.4 0.0 collective-permute-done.4.h0
  33.5 0.0 collective-permute-done.5.h1
  33.5 0.0 collective-permute-done.6.h2
  33.5 1.1 collective-permute-done.7.h3
  34.6 2.2 %shard_map.199 = (bf16[256,128]{1,0:T(8,128)(2,1)S(1)}, bf16[128,128]{1,0:T(8,128)(2,1)S(1)}, bf16[128,128]{1,0:T(8,128)(2,1)S(1)}, bf16[128,128]{1,0:T(8,128)(2...) custom-call(s32[1,4]{1,0:T(1,128)S(1)} %get-tuple-element.64.blocks_, ...), custom_call_target="tpu_custom_call" | custom-call | tf_op jit(solution)/shard_map/pallas_call | solution.py:453
  36.8 0.7 collective-permute-start.8
  37.5 2.9 %collective-permute-start.9 = (bf16[128,128]{1,0:T(8,128)(2,1)S(1)}, bf16[128,128]{1,0:T(8,128)(2,1)S(1)}, u32[]{:S(2)}, u32[]{:S(2)}) collective-permute-start(bf16[128,128]{1,0:T(8,128)(2,1)S(1)} %get-tuple-element.86), channel_id=1, source_target_pairs={{32,64},{64,32},{96,128},{128,96},{160,192},{192,160},{224,256},{2... | collective-permute-start | bytes 98312 | tf_op jit(solution)/shard_map/ppermute | solution.py:469
  40.4 9.3 %collective-permute-start.10 = (bf16[128,128]{1,0:T(8,128)(2,1)S(1)}, bf16[128,128]{1,0:T(8,128)(2,1)S(1)}, u32[]{:S(2)}, u32[]{:S(2)}) collective-permute-start(bf16[128,128]{1,0:T(8,128)(2,1)S(1)} %get-tuple-element.87), channel_id=1, source_target_pairs={{0,1},{1,0},{2,3},{3,2},{4,5},{5,4},{6,7},{7,6},{8,9},{9,8},{10,11... | collective-permute-start | bytes 98312 | tf_op jit(solution)/shard_map/ppermute | solution.py:469
  49.6 1.9 %collective-permute-start.11 = (bf16[128,128]{1,0:T(8,128)(2,1)S(1)}, bf16[128,128]{1,0:T(8,128)(2,1)S(1)}, u32[]{:S(2)}, u32[]{:S(2)}) collective-permute-start(bf16[128,128]{1,0:T(8,128)(2,1)S(1)} %get-tuple-element.88), channel_id=1, source_target_pairs={{0,32},{32,0},{64,96},{96,64},{128,160},{160,128},{192,224},{224,1... | collective-permute-start | bytes 98312 | tf_op jit(solution)/shard_map/ppermute | solution.py:469
  51.6 0.0 collective-permute-done.10.h2
  51.6 1.1 collective-permute-done.11.h3
  52.7 4.4 %shard_map.200 = (bf16[512,128]{1,0:T(8,128)(2,1)}, f32[256,128]{1,0:T(8,128)S(1)}, bf16[128,128]{1,0:T(8,128)(2,1)S(1)}, bf16[128,128]{1,0:T(8,128)(2,1)S(1)}, ...) custom-call(bf16[256,128]{1,0:T(8,128)(2,1)S(1)} %get-tuple-element.84.x_ref, ...), custom_call_target="tpu_custom_call" | custom-call | tf_op jit(solution)/shard_map/pallas_call | solution.py:453
  57.2 0.7 collective-permute-start.12
  57.9 2.7 %collective-permute-start.13 = (bf16[128,128]{1,0:T(8,128)(2,1)S(1)}, bf16[128,128]{1,0:T(8,128)(2,1)S(1)}, u32[]{:S(2)}, u32[]{:S(2)}) collective-permute-start(bf16[128,128]{1,0:T(8,128)(2,1)S(1)} %get-tuple-element.94), channel_id=1, source_target_pairs={{32,64},{64,32},{96,128},{128,96},{160,192},{192,160},{224,256},{2... | collective-permute-start | bytes 98312 | tf_op jit(solution)/shard_map/ppermute | solution.py:469
  60.6 5.8 %collective-permute-start.14 = (bf16[128,128]{1,0:T(8,128)(2,1)S(1)}, bf16[128,128]{1,0:T(8,128)(2,1)S(1)}, u32[]{:S(2)}, u32[]{:S(2)}) collective-permute-start(bf16[128,128]{1,0:T(8,128)(2,1)S(1)} %get-tuple-element.95), channel_id=1, source_target_pairs={{0,1},{1,0},{2,3},{3,2},{4,5},{5,4},{6,7},{7,6},{8,9},{9,8},{10,11... | collective-permute-start | bytes 98312 | tf_op jit(solution)/shard_map/ppermute | solution.py:469
  66.4 1.9 %collective-permute-start.15 = (bf16[128,128]{1,0:T(8,128)(2,1)S(1)}, bf16[128,128]{1,0:T(8,128)(2,1)S(1)}, u32[]{:S(2)}, u32[]{:S(2)}) collective-permute-start(bf16[128,128]{1,0:T(8,128)(2,1)S(1)} %get-tuple-element.96), channel_id=1, source_target_pairs={{0,32},{32,0},{64,96},{96,64},{128,160},{160,128},{192,224},{224,1... | collective-permute-start | bytes 98312 | tf_op jit(solution)/shard_map/ppermute | solution.py:469
  68.3 0.0 collective-permute-done.13.r1
  68.4 0.0 collective-permute-done.14.r2
  68.4 1.1 collective-permute-done.15.r3
  69.5 2.5 %shard_map.201 = (f32[256,128]{1,0:T(8,128)S(1)}, bf16[128,128]{1,0:T(8,128)(2,1)S(1)}, bf16[128,128]{1,0:T(8,128)(2,1)S(1)}, bf16[128,128]{1,0:T(8,128)(2,1)S(1...) custom-call(s32[1,4]{1,0:T(1,128)S(1)} %get-tuple-element.64.blocks_ref, ...), custom_call_target="tpu_custom_call" | custom-call | tf_op jit(solution)/shard_map/pallas_call | solution.py:453
  72.0 0.7 collective-permute-start.16
  72.7 4.0 %collective-permute-start.17 = (bf16[128,128]{1,0:T(8,128)(2,1)S(1)}, bf16[128,128]{1,0:T(8,128)(2,1)S(1)}, u32[]{:S(2)}, u32[]{:S(2)}) collective-permute-start(bf16[128,128]{1,0:T(8,128)(2,1)S(1)} %get-tuple-element.103), channel_id=1, source_target_pairs={{32,64},{64,32},{96,128},{128,96},{160,192},{192,160},{224,256},{2... | collective-permute-start | bytes 98312 | tf_op jit(solution)/shard_map/ppermute | solution.py:469
  76.7 9.3 %collective-permute-start.18 = (bf16[128,128]{1,0:T(8,128)(2,1)S(1)}, bf16[128,128]{1,0:T(8,128)(2,1)S(1)}, u32[]{:S(2)}, u32[]{:S(2)}) collective-permute-start(bf16[128,128]{1,0:T(8,128)(2,1)S(1)} %get-tuple-element.104), channel_id=1, source_target_pairs={{0,1},{1,0},{2,3},{3,2},{4,5},{5,4},{6,7},{7,6},{8,9},{9,8},{10,11... | collective-permute-start | bytes 98312 | tf_op jit(solution)/shard_map/ppermute | solution.py:469
  86.0 2.1 %collective-permute-start.19 = (bf16[128,128]{1,0:T(8,128)(2,1)S(1)}, bf16[128,128]{1,0:T(8,128)(2,1)S(1)}, u32[]{:S(2)}, u32[]{:S(2)}) collective-permute-start(bf16[128,128]{1,0:T(8,128)(2,1)S(1)} %get-tuple-element.105), channel_id=1, source_target_pairs={{0,32},{32,0},{64,96},{96,64},{128,160},{160,128},{192,224},{224,1... | collective-permute-start | bytes 98312 | tf_op jit(solution)/shard_map/ppermute | solution.py:469
  88.1 0.0 collective-permute-done.17.r1
  88.1 0.0 collective-permute-done.18.r2
  88.1 1.0 collective-permute-done.19.r3
  89.1 3.2 %shard_map.202 = (f32[256,128]{1,0:T(8,128)}, bf16[2048,128]{1,0:T(8,128)(2,1)S(1)}) custom-call(s32[1]{0:T(128)} %bitcast.21.live_ref, s32[1,4]{1,0:T(1,128)S(1)} %get-tuple-element.64.blocks_ref, f32[256,128]{1,0:T(8,128)S(1)} %get-tuple-element.101.grad_in_ref, bf16[128,128]{1,0:T(8,128)(2,1)S(1)} %collective-permute-done.16.r0, ...), custom_call_target="tpu_custom_call" | custom-call | tf_op jit(solution)/shard_map/pallas_call | solution.py:453
  92.2 15.6 %all_to_all.20.parts_ref = bf16[16,128,128]{2,1,0:T(8,128)(2,1)S(1)} all-to-all(bf16[16,128,128]{2,1,0:T(8,128)(2,1)S(1)} %bitcast.23), channel_id=1, replica_groups=mesh['gx'=16,'gy'=32] {'gx'}, dimensions={0} | all-to-all | bytes 1048576 | tf_op jit(solution)/shard_map/all_to_all | solution.py:434
  107.8 0.1 shard_map.203
  107.9 22.1 %all_to_all.21.parts_ref = f32[32,4,128]{2,1,0:T(4,128)S(1)} all-to-all(f32[32,4,128]{2,1,0:T(4,128)S(1)} %bitcast.24), channel_id=1, replica_groups=mesh['gx'=16,'gy'=32] {'gy'}, dimensions={0} | all-to-all | bytes 131072 | tf_op jit(solution)/shard_map/all_to_all | solution.py:436
  130.0 14.1 %all_to_all.22 = f32[32,4,128]{2,1,0:T(4,128)S(1)} all-to-all(f32[32,4,128]{2,1,0:T(4,128)S(1)} %shard_map.204), channel_id=1, replica_groups=mesh['gx'=16,'gy'=32] {'gy'}, dimensions={0} | all-to-all | bytes 131072 | tf_op jit(solution)/shard_map/all_to_all | solution.py:438
  144.2 16.0 %all_to_all.23 = bf16[16,128,128]{2,1,0:T(8,128)(2,1)S(1)} all-to-all(bf16[16,128,128]{2,1,0:T(8,128)(2,1)S(1)} %shard_map.205), channel_id=1, replica_groups=mesh['gx'=16,'gy'=32] {'gx'}, dimensions={0} | all-to-all | bytes 1048576 | tf_op jit(solution)/shard_map/all_to_all | solution.py:440
  160.2 1.0 shard_map.206
  (6 shorter events, 0.1 us)
Async XLA Ops:
  2.0 17.0 %collective-permute-start = (bf16[128,128]{1,0:T(8,128)(2,1)S(1)}, bf16[128,128]{1,0:T(8,128)(2,1)S(1)}, u32[]{:S(2)}, u32[]{:S(2)}) collective-permute-start(bf16[128,128]{1,0:T(8,128)(2,1)S(1)} %get-tuple-element.66), channel_id=1, source_target_pairs={{1,2},{2,1},{3,4},{4,3},{5,6},{6,5},{7,8},{8,7},{9,10},{10,9},{11,... | collective-permute-start | bytes 98312 | tf_op jit(solution)/shard_map/ppermute | solution.py:469
  2.7 16.4 %collective-permute-start.1 = (bf16[128,128]{1,0:T(8,128)(2,1)S(1)}, bf16[128,128]{1,0:T(8,128)(2,1)S(1)}, u32[]{:S(2)}, u32[]{:S(2)}) collective-permute-start(bf16[128,128]{1,0:T(8,128)(2,1)S(1)} %get-tuple-element.67), channel_id=1, source_target_pairs={{32,64},{64,32},{96,128},{128,96},{160,192},{192,160},{224,256},{2... | collective-permute-start | bytes 98312 | tf_op jit(solution)/shard_map/ppermute | solution.py:469
  7.2 11.9 %collective-permute-start.2 = (bf16[128,128]{1,0:T(8,128)(2,1)S(1)}, bf16[128,128]{1,0:T(8,128)(2,1)S(1)}, u32[]{:S(2)}, u32[]{:S(2)}) collective-permute-start(bf16[128,128]{1,0:T(8,128)(2,1)S(1)} %get-tuple-element.68), channel_id=1, source_target_pairs={{0,1},{1,0},{2,3},{3,2},{4,5},{5,4},{6,7},{7,6},{8,9},{9,8},{10,11... | collective-permute-start | bytes 98312 | tf_op jit(solution)/shard_map/ppermute | solution.py:469
  16.5 3.1 %collective-permute-start.3 = (bf16[128,128]{1,0:T(8,128)(2,1)S(1)}, bf16[128,128]{1,0:T(8,128)(2,1)S(1)}, u32[]{:S(2)}, u32[]{:S(2)}) collective-permute-start(bf16[128,128]{1,0:T(8,128)(2,1)S(1)} %get-tuple-element.69), channel_id=1, source_target_pairs={{0,32},{32,0},{64,96},{96,64},{128,160},{160,128},{192,224},{224,1... | collective-permute-start | bytes 98312 | tf_op jit(solution)/shard_map/ppermute | solution.py:469
  22.3 11.1 %collective-permute-start.4 = (bf16[128,128]{1,0:T(8,128)(2,1)S(1)}, bf16[128,128]{1,0:T(8,128)(2,1)S(1)}, u32[]{:S(2)}, u32[]{:S(2)}) collective-permute-start(bf16[128,128]{1,0:T(8,128)(2,1)S(1)} %get-tuple-element.76), channel_id=1, source_target_pairs={{1,2},{2,1},{3,4},{4,3},{5,6},{6,5},{7,8},{8,7},{9,10},{10,9},{11,... | collective-permute-start | bytes 98312 | tf_op jit(solution)/shard_map/ppermute | solution.py:469
  23.0 10.5 %collective-permute-start.5 = (bf16[128,128]{1,0:T(8,128)(2,1)S(1)}, bf16[128,128]{1,0:T(8,128)(2,1)S(1)}, u32[]{:S(2)}, u32[]{:S(2)}) collective-permute-start(bf16[128,128]{1,0:T(8,128)(2,1)S(1)} %get-tuple-element.77), channel_id=1, source_target_pairs={{32,64},{64,32},{96,128},{128,96},{160,192},{192,160},{224,256},{2... | collective-permute-start | bytes 98312 | tf_op jit(solution)/shard_map/ppermute | solution.py:469
  26.2 7.3 %collective-permute-start.6 = (bf16[128,128]{1,0:T(8,128)(2,1)S(1)}, bf16[128,128]{1,0:T(8,128)(2,1)S(1)}, u32[]{:S(2)}, u32[]{:S(2)}) collective-permute-start(bf16[128,128]{1,0:T(8,128)(2,1)S(1)} %get-tuple-element.78), channel_id=1, source_target_pairs={{0,1},{1,0},{2,3},{3,2},{4,5},{5,4},{6,7},{7,6},{8,9},{9,8},{10,11... | collective-permute-start | bytes 98312 | tf_op jit(solution)/shard_map/ppermute | solution.py:469
  31.5 3.1 %collective-permute-start.7 = (bf16[128,128]{1,0:T(8,128)(2,1)S(1)}, bf16[128,128]{1,0:T(8,128)(2,1)S(1)}, u32[]{:S(2)}, u32[]{:S(2)}) collective-permute-start(bf16[128,128]{1,0:T(8,128)(2,1)S(1)} %get-tuple-element.79), channel_id=1, source_target_pairs={{0,32},{32,0},{64,96},{96,64},{128,160},{160,128},{192,224},{224,1... | collective-permute-start | bytes 98312 | tf_op jit(solution)/shard_map/ppermute | solution.py:469
  36.8 14.8 %collective-permute-start.8 = (bf16[128,128]{1,0:T(8,128)(2,1)S(1)}, bf16[128,128]{1,0:T(8,128)(2,1)S(1)}, u32[]{:S(2)}, u32[]{:S(2)}) collective-permute-start(bf16[128,128]{1,0:T(8,128)(2,1)S(1)} %get-tuple-element.85), channel_id=1, source_target_pairs={{1,2},{2,1},{3,4},{4,3},{5,6},{6,5},{7,8},{8,7},{9,10},{10,9},{11,... | collective-permute-start | bytes 98312 | tf_op jit(solution)/shard_map/ppermute | solution.py:469
  37.5 14.1 %collective-permute-start.9 = (bf16[128,128]{1,0:T(8,128)(2,1)S(1)}, bf16[128,128]{1,0:T(8,128)(2,1)S(1)}, u32[]{:S(2)}, u32[]{:S(2)}) collective-permute-start(bf16[128,128]{1,0:T(8,128)(2,1)S(1)} %get-tuple-element.86), channel_id=1, source_target_pairs={{32,64},{64,32},{96,128},{128,96},{160,192},{192,160},{224,256},{2... | collective-permute-start | bytes 98312 | tf_op jit(solution)/shard_map/ppermute | solution.py:469
  40.4 11.2 %collective-permute-start.10 = (bf16[128,128]{1,0:T(8,128)(2,1)S(1)}, bf16[128,128]{1,0:T(8,128)(2,1)S(1)}, u32[]{:S(2)}, u32[]{:S(2)}) collective-permute-start(bf16[128,128]{1,0:T(8,128)(2,1)S(1)} %get-tuple-element.87), channel_id=1, source_target_pairs={{0,1},{1,0},{2,3},{3,2},{4,5},{5,4},{6,7},{7,6},{8,9},{9,8},{10,11... | collective-permute-start | bytes 98312 | tf_op jit(solution)/shard_map/ppermute | solution.py:469
  49.6 3.1 %collective-permute-start.11 = (bf16[128,128]{1,0:T(8,128)(2,1)S(1)}, bf16[128,128]{1,0:T(8,128)(2,1)S(1)}, u32[]{:S(2)}, u32[]{:S(2)}) collective-permute-start(bf16[128,128]{1,0:T(8,128)(2,1)S(1)} %get-tuple-element.88), channel_id=1, source_target_pairs={{0,32},{32,0},{64,96},{96,64},{128,160},{160,128},{192,224},{224,1... | collective-permute-start | bytes 98312 | tf_op jit(solution)/shard_map/ppermute | solution.py:469
  57.2 11.1 %collective-permute-start.12 = (bf16[128,128]{1,0:T(8,128)(2,1)S(1)}, bf16[128,128]{1,0:T(8,128)(2,1)S(1)}, u32[]{:S(2)}, u32[]{:S(2)}) collective-permute-start(bf16[128,128]{1,0:T(8,128)(2,1)S(1)} %get-tuple-element.93), channel_id=1, source_target_pairs={{1,2},{2,1},{3,4},{4,3},{5,6},{6,5},{7,8},{8,7},{9,10},{10,9},{11,... | collective-permute-start | bytes 98312 | tf_op jit(solution)/shard_map/ppermute | solution.py:469
  57.9 10.5 %collective-permute-start.13 = (bf16[128,128]{1,0:T(8,128)(2,1)S(1)}, bf16[128,128]{1,0:T(8,128)(2,1)S(1)}, u32[]{:S(2)}, u32[]{:S(2)}) collective-permute-start(bf16[128,128]{1,0:T(8,128)(2,1)S(1)} %get-tuple-element.94), channel_id=1, source_target_pairs={{32,64},{64,32},{96,128},{128,96},{160,192},{192,160},{224,256},{2... | collective-permute-start | bytes 98312 | tf_op jit(solution)/shard_map/ppermute | solution.py:469
  60.6 7.8 %collective-permute-start.14 = (bf16[128,128]{1,0:T(8,128)(2,1)S(1)}, bf16[128,128]{1,0:T(8,128)(2,1)S(1)}, u32[]{:S(2)}, u32[]{:S(2)}) collective-permute-start(bf16[128,128]{1,0:T(8,128)(2,1)S(1)} %get-tuple-element.95), channel_id=1, source_target_pairs={{0,1},{1,0},{2,3},{3,2},{4,5},{5,4},{6,7},{7,6},{8,9},{9,8},{10,11... | collective-permute-start | bytes 98312 | tf_op jit(solution)/shard_map/ppermute | solution.py:469
  66.4 3.1 %collective-permute-start.15 = (bf16[128,128]{1,0:T(8,128)(2,1)S(1)}, bf16[128,128]{1,0:T(8,128)(2,1)S(1)}, u32[]{:S(2)}, u32[]{:S(2)}) collective-permute-start(bf16[128,128]{1,0:T(8,128)(2,1)S(1)} %get-tuple-element.96), channel_id=1, source_target_pairs={{0,32},{32,0},{64,96},{96,64},{128,160},{160,128},{192,224},{224,1... | collective-permute-start | bytes 98312 | tf_op jit(solution)/shard_map/ppermute | solution.py:469
  72.0 16.1 %collective-permute-start.16 = (bf16[128,128]{1,0:T(8,128)(2,1)S(1)}, bf16[128,128]{1,0:T(8,128)(2,1)S(1)}, u32[]{:S(2)}, u32[]{:S(2)}) collective-permute-start(bf16[128,128]{1,0:T(8,128)(2,1)S(1)} %get-tuple-element.102), channel_id=1, source_target_pairs={{1,2},{2,1},{3,4},{4,3},{5,6},{6,5},{7,8},{8,7},{9,10},{10,9},{11,... | collective-permute-start | bytes 98312 | tf_op jit(solution)/shard_map/ppermute | solution.py:469
  72.7 15.4 %collective-permute-start.17 = (bf16[128,128]{1,0:T(8,128)(2,1)S(1)}, bf16[128,128]{1,0:T(8,128)(2,1)S(1)}, u32[]{:S(2)}, u32[]{:S(2)}) collective-permute-start(bf16[128,128]{1,0:T(8,128)(2,1)S(1)} %get-tuple-element.103), channel_id=1, source_target_pairs={{32,64},{64,32},{96,128},{128,96},{160,192},{192,160},{224,256},{2... | collective-permute-start | bytes 98312 | tf_op jit(solution)/shard_map/ppermute | solution.py:469
  76.7 11.4 %collective-permute-start.18 = (bf16[128,128]{1,0:T(8,128)(2,1)S(1)}, bf16[128,128]{1,0:T(8,128)(2,1)S(1)}, u32[]{:S(2)}, u32[]{:S(2)}) collective-permute-start(bf16[128,128]{1,0:T(8,128)(2,1)S(1)} %get-tuple-element.104), channel_id=1, source_target_pairs={{0,1},{1,0},{2,3},{3,2},{4,5},{5,4},{6,7},{7,6},{8,9},{9,8},{10,11... | collective-permute-start | bytes 98312 | tf_op jit(solution)/shard_map/ppermute | solution.py:469
  86.0 3.1 %collective-permute-start.19 = (bf16[128,128]{1,0:T(8,128)(2,1)S(1)}, bf16[128,128]{1,0:T(8,128)(2,1)S(1)}, u32[]{:S(2)}, u32[]{:S(2)}) collective-permute-start(bf16[128,128]{1,0:T(8,128)(2,1)S(1)} %get-tuple-element.105), channel_id=1, source_target_pairs={{0,32},{32,0},{64,96},{96,64},{128,160},{160,128},{192,224},{224,1... | collective-permute-start | bytes 98312 | tf_op jit(solution)/shard_map/ppermute | solution.py:469

commit v5 on v4

--- a/solution.py
+++ b/solution.py
@@ -22,6 +22,7 @@
 GATHER_WIRE = BF16
 SCATTER_WIRE = BF16
 SCOPED = 24 * 1024 * 1024
+COST = pl.CostEstimate(flops=1 << 29, bytes_accessed=1 << 20, transcendentals=0)
 
 
 def halves(values):
@@ -100,22 +101,28 @@
     return centred * scale, scale
 
 
-def forward_step(x, extended, senders, receivers, weights, bias, gain, hidden_ref, slope_ref):
+def own_part(step, x_ref, edges_ref, w_ref, own_ref):
+    weights = w_ref if step is None else w_ref.at[step]
+    x = x_ref[...]
+    rows = x.shape[0]
+    projected = jnp.concatenate(
+        [halves(matmul(x, weights[0])), halves(matmul(x, weights[1]))], axis=0
+    )
+    for first in range(0, own_ref.shape[0], CHUNK):
+        ends = [edges_ref[end : end + 1, first : first + CHUNK] for end in range(2)]
+        marks = jnp.concatenate([one_hot_rows(end, rows) for end in ends], axis=1)
+        own_ref[first : first + CHUNK, :] = joined(matmul(marks, projected))
+
+
+def forward_step(x, extended, senders, receivers, weights, bias, gain, own_ref, hidden_ref, slope_ref):
     rows = x.shape[0]
     slots = senders.shape[1]
-    width = extended.shape[0]
-    projected = jnp.concatenate(
-        [halves(matmul(extended, weights[0])), halves(matmul(x, weights[1]))], axis=0
-    )
+    width = extended.shape[0] - rows
+    projected = halves(matmul(extended[rows:], weights[0]))
     for first in range(0, slots, CHUNK):
-        marks = jnp.concatenate(
-            [
-                one_hot_rows(senders[:, first : first + CHUNK], width),
-                one_hot_rows(receivers[:, first : first + CHUNK], rows),
-            ],
-            axis=1,
-        )
-        pre_act = joined(matmul(marks, projected)) + bias
+        marks = one_hot_rows(senders[:, first : first + CHUNK] - rows, width)
+        own = own_ref[first : first + CHUNK, :]
+        pre_act = joined(matmul(marks, projected)) + own + bias
         sigmoid = jax.nn.sigmoid(pre_act)
         hidden_ref[first : first + CHUNK, :] = (pre_act * sigmoid).astype(BF16)
         slope_ref[first : first + CHUNK, :] = sigmoid * (1.0 + pre_act * (1.0 - sigmoid))
@@ -237,7 +244,7 @@
 
 
 def fine_ahead(
-    live_ref, blocks_ref, x_ref, h0, h1, h2, h3, edges_ref, pool_ref, w_ref, bias_ref, gain_ref,
+    live_ref, blocks_ref, x_ref, h0, h1, h2, h3, edges_ref, pool_ref, w_ref, bias_ref, gain_ref, own_ref,
     mid_ref, coarse_ref, s0, s1, s2, s3, sums_ref, agg_ref, pre_ref, slope_ref,
     extended_ref, hidden_ref,
 ):
@@ -250,6 +257,7 @@
         w_ref,
         bias_ref[...],
         gain_ref[...],
+        own_ref,
         hidden_ref,
         slope_ref,
     )
@@ -265,7 +273,7 @@
 
 
 def coarse_ahead(
-    blocks_ref, x_ref, h0, h1, h2, h3, edges_ref, w_ref, bias_ref, gain_ref,
+    blocks_ref, x_ref, h0, h1, h2, h3, edges_ref, w_ref, bias_ref, gain_ref, own_ref,
     out_ref, s0, s1, s2, s3, sums_ref, agg_ref, pre_ref, slope_ref,
     extended_ref, hidden_ref,
 ):
@@ -278,6 +286,7 @@
         w_ref.at[0],
         bias_ref[0:1, :],
         gain_ref[0:1, :],
+        own_ref,
         hidden_ref,
         slope_ref,
     )
@@ -296,6 +305,7 @@
 
 def coarse_turn(
     loss_scale, x_ref, h0, h1, h2, h3, edges_ref, w_ref, bias_ref, gain_ref, pool_ref, mid_ref, cot_ref,
+    own_ref,
     out_ref, grad_ref, g0, g1, g2, g3, grads_ref,
     extended_ref, hidden_ref, slope_ref, act_ref, halo_ref,
 ):
@@ -306,7 +316,7 @@
     gain = gain_ref[1:2, :]
     weights = w_ref.at[1]
     output, edge_sums, agg, node_pre = forward_step(
-        x, extended, senders, receivers, weights, bias_ref[1:2, :], gain, hidden_ref, slope_ref
+        x, extended, senders, receivers, weights, bias_ref[1:2, :], gain, own_ref, hidden_ref, slope_ref
     )
     pool_row = pool_ref[...]
     lifted = matmul(one_hot_rows(pool_row, NC_DEV), output)
@@ -457,6 +467,7 @@
         out_specs=[vmem] * len(outs),
         scratch_shapes=[pltpu.VMEM(shape, dtype) for shape, dtype in scratch],
         compiler_params=pltpu.CompilerParams(vmem_limit_bytes=SCOPED),
+        cost_estimate=COST,
     )(*scalars, *arrays)
 
 
@@ -555,31 +566,41 @@
     x, edges, pool, coarse_list, blocks, fine_weights, bias, gain = arrays[:8]
     coarse_weights, coarse_bias, coarse_gain, cot = arrays[8:]
     halos = exchange(sends)
+
+    def own_of(step, values, edge_list, weights):
+        outs = [((edge_list.shape[1], H), F32)]
+        return list(call(functools.partial(own_part, step), [], [values, edge_list, weights], outs, []))
+
+    own = own_of(None, x, edges, fine_weights)
     fine_out = call(
         fine_ahead,
         [live],
-        [blocks, x, *halos, edges, pool, fine_weights, bias, gain],
+        [blocks, x, *halos, edges, pool, fine_weights, bias, gain, *own],
         [((rows, H), BF16), ((NC_DEV, H), BF16)] + [block] * 4 + saved(rows, slots),
         [((rows + 4 * BLOCK, H), BF16), ((slots, H), BF16)],
     )
     mid, coarse_0, sends, fine_saved = fine_out[0], fine_out[1], fine_out[2:6], fine_out[6:]
     halos_0 = exchange(sends)
+    own = own_of(0, coarse_0, coarse_list, coarse_weights)
     coarse_extended = ((NC_DEV + 4 * BLOCK, H), BF16)
     halo_grads = ((4 * BLOCK, H), BF16)
     ahead = call(
         coarse_ahead,
         [],
-        [blocks, coarse_0, *halos_0, coarse_list, coarse_weights, coarse_bias, coarse_gain],
+        [blocks, coarse_0, *halos_0, coarse_list, coarse_weights, coarse_bias, coarse_gain]
+        + own,
         [((NC_DEV, H), BF16)] + [block] * 4 + saved(NC_DEV, coarse_slots),
         [coarse_extended, ((coarse_slots, H), BF16)],
     )
     coarse_1, sends, coarse_saved = ahead[0], ahead[1:5], ahead[5:]
     halos_1 = exchange(sends)
+    own = own_of(1, coarse_1, coarse_list, coarse_weights)
     grads = ((GRAD_ROWS, H), F32)
     turned = call(
         functools.partial(coarse_turn, 1.0 / root),
         [],
-        [coarse_1, *halos_1, coarse_list, coarse_weights, coarse_bias, coarse_gain, pool, mid, cot],
+        [coarse_1, *halos_1, coarse_list, coarse_weights, coarse_bias, coarse_gain, pool, mid, cot]
+        + own,
         [((rows, H), BF16), ((NC_DEV, H), F32)] + [block] * 4 + [grads],
         [coarse_extended, ((coarse_slots, H), BF16), ((coarse_slots, H), F32)]
         + [((coarse_slots, 2 * H), BF16), halo_grads],

time: 162 us -> 161 us (level)
  waiting for transfers between devices: 4.92 us -> 2.66 us
    ppermute x20, waiting for transfers between devices: 4.92 us -> 2.66 us  [exchange(): received.append(lax.ppermute(piece, axis, pairs))]
    pallas_call x9 -> x12, Pallas kernels: 16.2 us -> 17.7 us  [call(): pl.pallas_call(kernel, out_shape=[jax.ShapeDtypeStruct(shape, dtype) for...]
  transfers between devices with their start and end apart: 20 -> 20, of which waited for: 5 -> 4; matrix products, arithmetic and copies ran while one was open for 0% -> 0% of each run, Pallas kernels for 0% -> 2%
where the time goes in v5:
time: 161 us
  starting transfers between devices  69.5 us (43%)
  blocking collectives  67.7 us (42%)
  Pallas kernels  19.1 us (12%)
  waiting for transfers between devices  2.66 us (2%)
  between operations  1.63 us (1%)
    ppermute x20, starting transfers between devices, exchange(): received.append(lax.ppermute(piece, axis, pairs))  69.5 us
    all_to_all x1, blocking collectives, reduce_all(): pieces = lax.all_to_all(mine.reshape(along, part, H), 'gy', 0, 0)  22.2 us
    pallas_call x12, Pallas kernels, call(): pl.pallas_call(kernel, out_shape=[jax.ShapeDtypeStruct(shape, dtype) for...  17.7 us
    all_to_all x1, blocking collectives, reduce_all(): everything = lax.all_to_all(shared, 'gx', 0, 0).reshape(PACKED, H)  16 us
    all_to_all x1, blocking collectives, reduce_all(): pieces = lax.all_to_all(packed.reshape(across, rows, H), 'gx', 0, 0)  15.4 us
    all_to_all x1, blocking collectives, reduce_all(): mine = lax.all_to_all(shared, 'gy', 0, 0).reshape(rows, H)  14.1 us
  transfers between devices with their start and end apart: 20, of which 4 were waited for; matrix products, arithmetic and copies ran while one was open for 0% of the time, Pallas kernels for 2%

profile of v5, /device:TPU:1, one launch (start us, length us, event | category | flops | bytes accessed | tf_op | source)
XLA Modules:
  0.0 160.5 jit_solution(8065201397931072876)
XLA Ops:
  0.6 1.4 shard_map.197
  2.0 0.7 collective-permute-start
  2.7 4.5 %collective-permute-start.1 = (bf16[128,128]{1,0:T(8,128)(2,1)S(1)}, bf16[128,128]{1,0:T(8,128)(2,1)S(1)}, u32[]{:S(2)}, u32[]{:S(2)}) collective-permute-start(bf16[128,128]{1,0:T(8,128)(2,1)S(1)} %get-tuple-element.67), channel_id=1, source_target_pairs={{32,64},{64,32},{96,128},{128,96},{160,192},{192,160},{224,256},{2... | collective-permute-start | bytes 98312 | tf_op jit(solution)/shard_map/ppermute | solution.py:480
  7.2 9.3 %collective-permute-start.2 = (bf16[128,128]{1,0:T(8,128)(2,1)S(1)}, bf16[128,128]{1,0:T(8,128)(2,1)S(1)}, u32[]{:S(2)}, u32[]{:S(2)}) collective-permute-start(bf16[128,128]{1,0:T(8,128)(2,1)S(1)} %get-tuple-element.68), channel_id=1, source_target_pairs={{0,1},{1,0},{2,3},{3,2},{4,5},{5,4},{6,7},{7,6},{8,9},{9,8},{10,11... | collective-permute-start | bytes 98312 | tf_op jit(solution)/shard_map/ppermute | solution.py:480
  16.5 1.9 %collective-permute-start.3 = (bf16[128,128]{1,0:T(8,128)(2,1)S(1)}, bf16[128,128]{1,0:T(8,128)(2,1)S(1)}, u32[]{:S(2)}, u32[]{:S(2)}) collective-permute-start(bf16[128,128]{1,0:T(8,128)(2,1)S(1)} %get-tuple-element.69), channel_id=1, source_target_pairs={{0,32},{32,0},{64,96},{96,64},{128,160},{160,128},{192,224},{224,1... | collective-permute-start | bytes 98312 | tf_op jit(solution)/shard_map/ppermute | solution.py:480
  19.1 1.1 shard_map.198.own_ref
  20.2 0.0 collective-permute-done.h0
  20.2 0.0 collective-permute-done.2.h2
  20.2 0.0 collective-permute-done.3.h3
  20.3 1.9 %shard_map.199 = (bf16[512,128]{1,0:T(8,128)(2,1)S(1)}, bf16[256,128]{1,0:T(8,128)(2,1)S(1)}, bf16[128,128]{1,0:T(8,128)(2,1)S(1)}, bf16[128,128]{1,0:T(8,128)(2...) custom-call(s32[1]{0:T(128)} %bitcast.20.live_ref, ...), custom_call_target="tpu_custom_call" | custom-call | flops 536870912 | bytes 1048576 | tf_op jit(solution)/shard_map/pallas_call | solution.py:463
  22.2 0.7 collective-permute-start.4
  22.9 3.5 %collective-permute-start.5 = (bf16[128,128]{1,0:T(8,128)(2,1)S(1)}, bf16[128,128]{1,0:T(8,128)(2,1)S(1)}, u32[]{:S(2)}, u32[]{:S(2)}) collective-permute-start(bf16[128,128]{1,0:T(8,128)(2,1)S(1)} %get-tuple-element.77), channel_id=1, source_target_pairs={{32,64},{64,32},{96,128},{128,96},{160,192},{192,160},{224,256},{2... | collective-permute-start | bytes 98312 | tf_op jit(solution)/shard_map/ppermute | solution.py:480
  26.4 5.3 %collective-permute-start.6 = (bf16[128,128]{1,0:T(8,128)(2,1)S(1)}, bf16[128,128]{1,0:T(8,128)(2,1)S(1)}, u32[]{:S(2)}, u32[]{:S(2)}) collective-permute-start(bf16[128,128]{1,0:T(8,128)(2,1)S(1)} %get-tuple-element.78), channel_id=1, source_target_pairs={{0,1},{1,0},{2,3},{3,2},{4,5},{5,4},{6,7},{7,6},{8,9},{9,8},{10,11... | collective-permute-start | bytes 98312 | tf_op jit(solution)/shard_map/ppermute | solution.py:480
  31.7 1.9 %collective-permute-start.7 = (bf16[128,128]{1,0:T(8,128)(2,1)S(1)}, bf16[128,128]{1,0:T(8,128)(2,1)S(1)}, u32[]{:S(2)}, u32[]{:S(2)}) collective-permute-start(bf16[128,128]{1,0:T(8,128)(2,1)S(1)} %get-tuple-element.79), channel_id=1, source_target_pairs={{0,32},{32,0},{64,96},{96,64},{128,160},{160,128},{192,224},{224,1... | collective-permute-start | bytes 98312 | tf_op jit(solution)/shard_map/ppermute | solution.py:480
  33.7 0.9 shard_map.200.own_ref
  34.6 0.0 collective-permute-done.5.h1
  34.6 0.0 collective-permute-done.6.h2
  34.6 0.3 collective-permute-done.7.h3
  34.8 1.7 %shard_map.201 = (bf16[256,128]{1,0:T(8,128)(2,1)S(1)}, bf16[128,128]{1,0:T(8,128)(2,1)S(1)}, bf16[128,128]{1,0:T(8,128)(2,1)S(1)}, bf16[128,128]{1,0:T(8,128)(2...) custom-call(s32[1,4]{1,0:T(1,128)S(1)} %get-tuple-element.64.blocks_, ...), custom_call_target="tpu_custom_call" | custom-call | flops 536870912 | bytes 1048576 | tf_op jit(solution)/shard_map/pallas_call | solution.py:463
  36.5 0.7 collective-permute-start.8
  37.2 3.0 %collective-permute-start.9 = (bf16[128,128]{1,0:T(8,128)(2,1)S(1)}, bf16[128,128]{1,0:T(8,128)(2,1)S(1)}, u32[]{:S(2)}, u32[]{:S(2)}) collective-permute-start(bf16[128,128]{1,0:T(8,128)(2,1)S(1)} %get-tuple-element.86), channel_id=1, source_target_pairs={{32,64},{64,32},{96,128},{128,96},{160,192},{192,160},{224,256},{2... | collective-permute-start | bytes 98312 | tf_op jit(solution)/shard_map/ppermute | solution.py:480
  40.2 9.3 %collective-permute-start.10 = (bf16[128,128]{1,0:T(8,128)(2,1)S(1)}, bf16[128,128]{1,0:T(8,128)(2,1)S(1)}, u32[]{:S(2)}, u32[]{:S(2)}) collective-permute-start(bf16[128,128]{1,0:T(8,128)(2,1)S(1)} %get-tuple-element.87), channel_id=1, source_target_pairs={{0,1},{1,0},{2,3},{3,2},{4,5},{5,4},{6,7},{7,6},{8,9},{9,8},{10,11... | collective-permute-start | bytes 98312 | tf_op jit(solution)/shard_map/ppermute | solution.py:480
  49.5 1.9 %collective-permute-start.11 = (bf16[128,128]{1,0:T(8,128)(2,1)S(1)}, bf16[128,128]{1,0:T(8,128)(2,1)S(1)}, u32[]{:S(2)}, u32[]{:S(2)}) collective-permute-start(bf16[128,128]{1,0:T(8,128)(2,1)S(1)} %get-tuple-element.88), channel_id=1, source_target_pairs={{0,32},{32,0},{64,96},{96,64},{128,160},{160,128},{192,224},{224,1... | collective-permute-start | bytes 98312 | tf_op jit(solution)/shard_map/ppermute | solution.py:480
  51.4 0.9 shard_map.202.own_ref
  52.3 0.0 collective-permute-done.10.h2
  52.3 0.3 collective-permute-done.11.h3
  52.6 4.3 %shard_map.203 = (bf16[512,128]{1,0:T(8,128)(2,1)}, f32[256,128]{1,0:T(8,128)S(1)}, bf16[128,128]{1,0:T(8,128)(2,1)S(1)}, bf16[128,128]{1,0:T(8,128)(2,1)S(1)}, ...) custom-call(bf16[256,128]{1,0:T(8,128)(2,1)S(1)} %get-tuple-element.84.x_ref, ...), custom_call_target="tpu_custom_call" | custom-call | flops 536870912 | bytes 1048576 | tf_op jit(solution)/shard_map/pallas_call | solution.py:463
  56.9 0.7 collective-permute-start.12
  57.6 2.6 %collective-permute-start.13 = (bf16[128,128]{1,0:T(8,128)(2,1)S(1)}, bf16[128,128]{1,0:T(8,128)(2,1)S(1)}, u32[]{:S(2)}, u32[]{:S(2)}) collective-permute-start(bf16[128,128]{1,0:T(8,128)(2,1)S(1)} %get-tuple-element.94), channel_id=1, source_target_pairs={{32,64},{64,32},{96,128},{128,96},{160,192},{192,160},{224,256},{2... | collective-permute-start | bytes 98312 | tf_op jit(solution)/shard_map/ppermute | solution.py:480
  60.2 6.0 %collective-permute-start.14 = (bf16[128,128]{1,0:T(8,128)(2,1)S(1)}, bf16[128,128]{1,0:T(8,128)(2,1)S(1)}, u32[]{:S(2)}, u32[]{:S(2)}) collective-permute-start(bf16[128,128]{1,0:T(8,128)(2,1)S(1)} %get-tuple-element.95), channel_id=1, source_target_pairs={{0,1},{1,0},{2,3},{3,2},{4,5},{5,4},{6,7},{7,6},{8,9},{9,8},{10,11... | collective-permute-start | bytes 98312 | tf_op jit(solution)/shard_map/ppermute | solution.py:480
  66.2 2.1 %collective-permute-start.15 = (bf16[128,128]{1,0:T(8,128)(2,1)S(1)}, bf16[128,128]{1,0:T(8,128)(2,1)S(1)}, u32[]{:S(2)}, u32[]{:S(2)}) collective-permute-start(bf16[128,128]{1,0:T(8,128)(2,1)S(1)} %get-tuple-element.96), channel_id=1, source_target_pairs={{0,32},{32,0},{64,96},{96,64},{128,160},{160,128},{192,224},{224,1... | collective-permute-start | bytes 98312 | tf_op jit(solution)/shard_map/ppermute | solution.py:480
  68.3 0.0 collective-permute-done.12.r0
  68.3 0.0 collective-permute-done.13.r1
  68.3 1.0 collective-permute-done.15.r3
  69.3 2.5 %shard_map.204 = (f32[256,128]{1,0:T(8,128)S(1)}, bf16[128,128]{1,0:T(8,128)(2,1)S(1)}, bf16[128,128]{1,0:T(8,128)(2,1)S(1)}, bf16[128,128]{1,0:T(8,128)(2,1)S(1...) custom-call(s32[1,4]{1,0:T(1,128)S(1)} %get-tuple-element.64.blocks_ref, ...), custom_call_target="tpu_custom_call" | custom-call | flops 536870912 | bytes 1048576 | tf_op jit(solution)/shard_map/pallas_call | solution.py:463
  71.8 0.7 collective-permute-start.16
  72.5 3.7 %collective-permute-start.17 = (bf16[128,128]{1,0:T(8,128)(2,1)S(1)}, bf16[128,128]{1,0:T(8,128)(2,1)S(1)}, u32[]{:S(2)}, u32[]{:S(2)}) collective-permute-start(bf16[128,128]{1,0:T(8,128)(2,1)S(1)} %get-tuple-element.103), channel_id=1, source_target_pairs={{32,64},{64,32},{96,128},{128,96},{160,192},{192,160},{224,256},{2... | collective-permute-start | bytes 98312 | tf_op jit(solution)/shard_map/ppermute | solution.py:480
  76.1 9.3 %collective-permute-start.18 = (bf16[128,128]{1,0:T(8,128)(2,1)S(1)}, bf16[128,128]{1,0:T(8,128)(2,1)S(1)}, u32[]{:S(2)}, u32[]{:S(2)}) collective-permute-start(bf16[128,128]{1,0:T(8,128)(2,1)S(1)} %get-tuple-element.104), channel_id=1, source_target_pairs={{0,1},{1,0},{2,3},{3,2},{4,5},{5,4},{6,7},{7,6},{8,9},{9,8},{10,11... | collective-permute-start | bytes 98312 | tf_op jit(solution)/shard_map/ppermute | solution.py:480
  85.4 1.9 %collective-permute-start.19 = (bf16[128,128]{1,0:T(8,128)(2,1)S(1)}, bf16[128,128]{1,0:T(8,128)(2,1)S(1)}, u32[]{:S(2)}, u32[]{:S(2)}) collective-permute-start(bf16[128,128]{1,0:T(8,128)(2,1)S(1)} %get-tuple-element.105), channel_id=1, source_target_pairs={{0,32},{32,0},{64,96},{96,64},{128,160},{160,128},{192,224},{224,1... | collective-permute-start | bytes 98312 | tf_op jit(solution)/shard_map/ppermute | solution.py:480
  87.3 0.0 collective-permute-done.16.r0
  87.4 1.1 collective-permute-done.19.r3
  88.5 3.2 %shard_map.205 = (f32[256,128]{1,0:T(8,128)}, bf16[2048,128]{1,0:T(8,128)(2,1)S(1)}) custom-call(s32[1]{0:T(128)} %bitcast.21.live_ref, s32[1,4]{1,0:T(1,128)S(1)} %get-tuple-element.64.blocks_ref, f32[256,128]{1,0:T(8,128)S(1)} %get-tuple-element.101.grad_in_ref, bf16[128,128]{1,0:T(8,128)(2,1)S(1)} %collective-permute-done.16.r0, ...), custom_call_target="tpu_custom_call" | custom-call | flops 536870912 | bytes 1048576 | tf_op jit(solution)/shard_map/pallas_call | solution.py:463
  91.7 15.4 %all_to_all.20.parts_ref = bf16[16,128,128]{2,1,0:T(8,128)(2,1)S(1)} all-to-all(bf16[16,128,128]{2,1,0:T(8,128)(2,1)S(1)} %bitcast.22), channel_id=1, replica_groups=mesh['gx'=16,'gy'=32] {'gx'}, dimensions={0} | all-to-all | bytes 1048576 | tf_op jit(solution)/shard_map/all_to_all | solution.py:444
  107.1 0.1 shard_map.206
  107.2 22.2 %all_to_all.21.parts_ref = f32[32,4,128]{2,1,0:T(4,128)S(1)} all-to-all(f32[32,4,128]{2,1,0:T(4,128)S(1)} %bitcast.24), channel_id=1, replica_groups=mesh['gx'=16,'gy'=32] {'gy'}, dimensions={0} | all-to-all | bytes 131072 | tf_op jit(solution)/shard_map/all_to_all | solution.py:446
  129.4 14.1 %all_to_all.22 = f32[32,4,128]{2,1,0:T(4,128)S(1)} all-to-all(f32[32,4,128]{2,1,0:T(4,128)S(1)} %shard_map.207), channel_id=1, replica_groups=mesh['gx'=16,'gy'=32] {'gy'}, dimensions={0} | all-to-all | bytes 131072 | tf_op jit(solution)/shard_map/all_to_all | solution.py:448
  143.5 16.0 %all_to_all.23 = bf16[16,128,128]{2,1,0:T(8,128)(2,1)S(1)} all-to-all(bf16[16,128,128]{2,1,0:T(8,128)(2,1)S(1)} %shard_map.208), channel_id=1, replica_groups=mesh['gx'=16,'gy'=32] {'gx'}, dimensions={0} | all-to-all | bytes 1048576 | tf_op jit(solution)/shard_map/all_to_all | solution.py:450
  159.5 1.0 shard_map.209
  (9 shorter events, 0.1 us)
Async XLA Ops:
  2.0 18.2 %collective-permute-start = (bf16[128,128]{1,0:T(8,128)(2,1)S(1)}, bf16[128,128]{1,0:T(8,128)(2,1)S(1)}, u32[]{:S(2)}, u32[]{:S(2)}) collective-permute-start(bf16[128,128]{1,0:T(8,128)(2,1)S(1)} %get-tuple-element.66), channel_id=1, source_target_pairs={{1,2},{2,1},{3,4},{4,3},{5,6},{6,5},{7,8},{8,7},{9,10},{10,9},{11,... | collective-permute-start | bytes 98312 | tf_op jit(solution)/shard_map/ppermute | solution.py:480
  2.7 17.5 %collective-permute-start.1 = (bf16[128,128]{1,0:T(8,128)(2,1)S(1)}, bf16[128,128]{1,0:T(8,128)(2,1)S(1)}, u32[]{:S(2)}, u32[]{:S(2)}) collective-permute-start(bf16[128,128]{1,0:T(8,128)(2,1)S(1)} %get-tuple-element.67), channel_id=1, source_target_pairs={{32,64},{64,32},{96,128},{128,96},{160,192},{192,160},{224,256},{2... | collective-permute-start | bytes 98312 | tf_op jit(solution)/shard_map/ppermute | solution.py:480
  7.2 13.0 %collective-permute-start.2 = (bf16[128,128]{1,0:T(8,128)(2,1)S(1)}, bf16[128,128]{1,0:T(8,128)(2,1)S(1)}, u32[]{:S(2)}, u32[]{:S(2)}) collective-permute-start(bf16[128,128]{1,0:T(8,128)(2,1)S(1)} %get-tuple-element.68), channel_id=1, source_target_pairs={{0,1},{1,0},{2,3},{3,2},{4,5},{5,4},{6,7},{7,6},{8,9},{9,8},{10,11... | collective-permute-start | bytes 98312 | tf_op jit(solution)/shard_map/ppermute | solution.py:480
  16.5 3.8 %collective-permute-start.3 = (bf16[128,128]{1,0:T(8,128)(2,1)S(1)}, bf16[128,128]{1,0:T(8,128)(2,1)S(1)}, u32[]{:S(2)}, u32[]{:S(2)}) collective-permute-start(bf16[128,128]{1,0:T(8,128)(2,1)S(1)} %get-tuple-element.69), channel_id=1, source_target_pairs={{0,32},{32,0},{64,96},{96,64},{128,160},{160,128},{192,224},{224,1... | collective-permute-start | bytes 98312 | tf_op jit(solution)/shard_map/ppermute | solution.py:480
  22.2 12.4 %collective-permute-start.4 = (bf16[128,128]{1,0:T(8,128)(2,1)S(1)}, bf16[128,128]{1,0:T(8,128)(2,1)S(1)}, u32[]{:S(2)}, u32[]{:S(2)}) collective-permute-start(bf16[128,128]{1,0:T(8,128)(2,1)S(1)} %get-tuple-element.76), channel_id=1, source_target_pairs={{1,2},{2,1},{3,4},{4,3},{5,6},{6,5},{7,8},{8,7},{9,10},{10,9},{11,... | collective-permute-start | bytes 98312 | tf_op jit(solution)/shard_map/ppermute | solution.py:480
  22.9 11.7 %collective-permute-start.5 = (bf16[128,128]{1,0:T(8,128)(2,1)S(1)}, bf16[128,128]{1,0:T(8,128)(2,1)S(1)}, u32[]{:S(2)}, u32[]{:S(2)}) collective-permute-start(bf16[128,128]{1,0:T(8,128)(2,1)S(1)} %get-tuple-element.77), channel_id=1, source_target_pairs={{32,64},{64,32},{96,128},{128,96},{160,192},{192,160},{224,256},{2... | collective-permute-start | bytes 98312 | tf_op jit(solution)/shard_map/ppermute | solution.py:480
  26.4 8.2 %collective-permute-start.6 = (bf16[128,128]{1,0:T(8,128)(2,1)S(1)}, bf16[128,128]{1,0:T(8,128)(2,1)S(1)}, u32[]{:S(2)}, u32[]{:S(2)}) collective-permute-start(bf16[128,128]{1,0:T(8,128)(2,1)S(1)} %get-tuple-element.78), channel_id=1, source_target_pairs={{0,1},{1,0},{2,3},{3,2},{4,5},{5,4},{6,7},{7,6},{8,9},{9,8},{10,11... | collective-permute-start | bytes 98312 | tf_op jit(solution)/shard_map/ppermute | solution.py:480
  31.7 3.1 %collective-permute-start.7 = (bf16[128,128]{1,0:T(8,128)(2,1)S(1)}, bf16[128,128]{1,0:T(8,128)(2,1)S(1)}, u32[]{:S(2)}, u32[]{:S(2)}) collective-permute-start(bf16[128,128]{1,0:T(8,128)(2,1)S(1)} %get-tuple-element.79), channel_id=1, source_target_pairs={{0,32},{32,0},{64,96},{96,64},{128,160},{160,128},{192,224},{224,1... | collective-permute-start | bytes 98312 | tf_op jit(solution)/shard_map/ppermute | solution.py:480
  36.5 15.7 %collective-permute-start.8 = (bf16[128,128]{1,0:T(8,128)(2,1)S(1)}, bf16[128,128]{1,0:T(8,128)(2,1)S(1)}, u32[]{:S(2)}, u32[]{:S(2)}) collective-permute-start(bf16[128,128]{1,0:T(8,128)(2,1)S(1)} %get-tuple-element.85), channel_id=1, source_target_pairs={{1,2},{2,1},{3,4},{4,3},{5,6},{6,5},{7,8},{8,7},{9,10},{10,9},{11,... | collective-permute-start | bytes 98312 | tf_op jit(solution)/shard_map/ppermute | solution.py:480
  37.2 15.1 %collective-permute-start.9 = (bf16[128,128]{1,0:T(8,128)(2,1)S(1)}, bf16[128,128]{1,0:T(8,128)(2,1)S(1)}, u32[]{:S(2)}, u32[]{:S(2)}) collective-permute-start(bf16[128,128]{1,0:T(8,128)(2,1)S(1)} %get-tuple-element.86), channel_id=1, source_target_pairs={{32,64},{64,32},{96,128},{128,96},{160,192},{192,160},{224,256},{2... | collective-permute-start | bytes 98312 | tf_op jit(solution)/shard_map/ppermute | solution.py:480
  40.2 12.1 %collective-permute-start.10 = (bf16[128,128]{1,0:T(8,128)(2,1)S(1)}, bf16[128,128]{1,0:T(8,128)(2,1)S(1)}, u32[]{:S(2)}, u32[]{:S(2)}) collective-permute-start(bf16[128,128]{1,0:T(8,128)(2,1)S(1)} %get-tuple-element.87), channel_id=1, source_target_pairs={{0,1},{1,0},{2,3},{3,2},{4,5},{5,4},{6,7},{7,6},{8,9},{9,8},{10,11... | collective-permute-start | bytes 98312 | tf_op jit(solution)/shard_map/ppermute | solution.py:480
  49.5 3.1 %collective-permute-start.11 = (bf16[128,128]{1,0:T(8,128)(2,1)S(1)}, bf16[128,128]{1,0:T(8,128)(2,1)S(1)}, u32[]{:S(2)}, u32[]{:S(2)}) collective-permute-start(bf16[128,128]{1,0:T(8,128)(2,1)S(1)} %get-tuple-element.88), channel_id=1, source_target_pairs={{0,32},{32,0},{64,96},{96,64},{128,160},{160,128},{192,224},{224,1... | collective-permute-start | bytes 98312 | tf_op jit(solution)/shard_map/ppermute | solution.py:480
  56.9 11.4 %collective-permute-start.12 = (bf16[128,128]{1,0:T(8,128)(2,1)S(1)}, bf16[128,128]{1,0:T(8,128)(2,1)S(1)}, u32[]{:S(2)}, u32[]{:S(2)}) collective-permute-start(bf16[128,128]{1,0:T(8,128)(2,1)S(1)} %get-tuple-element.93), channel_id=1, source_target_pairs={{1,2},{2,1},{3,4},{4,3},{5,6},{6,5},{7,8},{8,7},{9,10},{10,9},{11,... | collective-permute-start | bytes 98312 | tf_op jit(solution)/shard_map/ppermute | solution.py:480
  57.6 10.7 %collective-permute-start.13 = (bf16[128,128]{1,0:T(8,128)(2,1)S(1)}, bf16[128,128]{1,0:T(8,128)(2,1)S(1)}, u32[]{:S(2)}, u32[]{:S(2)}) collective-permute-start(bf16[128,128]{1,0:T(8,128)(2,1)S(1)} %get-tuple-element.94), channel_id=1, source_target_pairs={{32,64},{64,32},{96,128},{128,96},{160,192},{192,160},{224,256},{2... | collective-permute-start | bytes 98312 | tf_op jit(solution)/shard_map/ppermute | solution.py:480
  60.2 8.2 %collective-permute-start.14 = (bf16[128,128]{1,0:T(8,128)(2,1)S(1)}, bf16[128,128]{1,0:T(8,128)(2,1)S(1)}, u32[]{:S(2)}, u32[]{:S(2)}) collective-permute-start(bf16[128,128]{1,0:T(8,128)(2,1)S(1)} %get-tuple-element.95), channel_id=1, source_target_pairs={{0,1},{1,0},{2,3},{3,2},{4,5},{5,4},{6,7},{7,6},{8,9},{9,8},{10,11... | collective-permute-start | bytes 98312 | tf_op jit(solution)/shard_map/ppermute | solution.py:480
  66.2 3.1 %collective-permute-start.15 = (bf16[128,128]{1,0:T(8,128)(2,1)S(1)}, bf16[128,128]{1,0:T(8,128)(2,1)S(1)}, u32[]{:S(2)}, u32[]{:S(2)}) collective-permute-start(bf16[128,128]{1,0:T(8,128)(2,1)S(1)} %get-tuple-element.96), channel_id=1, source_target_pairs={{0,32},{32,0},{64,96},{96,64},{128,160},{160,128},{192,224},{224,1... | collective-permute-start | bytes 98312 | tf_op jit(solution)/shard_map/ppermute | solution.py:480
  71.8 15.6 %collective-permute-start.16 = (bf16[128,128]{1,0:T(8,128)(2,1)S(1)}, bf16[128,128]{1,0:T(8,128)(2,1)S(1)}, u32[]{:S(2)}, u32[]{:S(2)}) collective-permute-start(bf16[128,128]{1,0:T(8,128)(2,1)S(1)} %get-tuple-element.102), channel_id=1, source_target_pairs={{1,2},{2,1},{3,4},{4,3},{5,6},{6,5},{7,8},{8,7},{9,10},{10,9},{11,... | collective-permute-start | bytes 98312 | tf_op jit(solution)/shard_map/ppermute | solution.py:480
  72.5 14.9 %collective-permute-start.17 = (bf16[128,128]{1,0:T(8,128)(2,1)S(1)}, bf16[128,128]{1,0:T(8,128)(2,1)S(1)}, u32[]{:S(2)}, u32[]{:S(2)}) collective-permute-start(bf16[128,128]{1,0:T(8,128)(2,1)S(1)} %get-tuple-element.103), channel_id=1, source_target_pairs={{32,64},{64,32},{96,128},{128,96},{160,192},{192,160},{224,256},{2... | collective-permute-start | bytes 98312 | tf_op jit(solution)/shard_map/ppermute | solution.py:480
  76.1 11.2 %collective-permute-start.18 = (bf16[128,128]{1,0:T(8,128)(2,1)S(1)}, bf16[128,128]{1,0:T(8,128)(2,1)S(1)}, u32[]{:S(2)}, u32[]{:S(2)}) collective-permute-start(bf16[128,128]{1,0:T(8,128)(2,1)S(1)} %get-tuple-element.104), channel_id=1, source_target_pairs={{0,1},{1,0},{2,3},{3,2},{4,5},{5,4},{6,7},{7,6},{8,9},{9,8},{10,11... | collective-permute-start | bytes 98312 | tf_op jit(solution)/shard_map/ppermute | solution.py:480
  85.4 3.1 %collective-permute-start.19 = (bf16[128,128]{1,0:T(8,128)(2,1)S(1)}, bf16[128,128]{1,0:T(8,128)(2,1)S(1)}, u32[]{:S(2)}, u32[]{:S(2)}) collective-permute-start(bf16[128,128]{1,0:T(8,128)(2,1)S(1)} %get-tuple-element.105), channel_id=1, source_target_pairs={{0,32},{32,0},{64,96},{96,64},{128,160},{160,128},{192,224},{224,1... | collective-permute-start | bytes 98312 | tf_op jit(solution)/shard_map/ppermute | solution.py:480

commit v6 on v5

--- a/solution.py
+++ b/solution.py
@@ -80,7 +80,7 @@
 
 def place():
     across, along = lax.axis_index("gx") % 2, lax.axis_index("gy") % 2
-    return (2 + along, across, 3 - along, 1 - across)
+    return (across, 2 + along, 3 - along, 1 - across)
 
 
 def rows_at(index, count):
@@ -473,7 +473,7 @@
 
 def exchange(pieces):
     received = []
-    for piece, (axis, first) in zip(pieces, (("gy", 1), ("gx", 1), ("gy", 0), ("gx", 0)), strict=True):
+    for piece, (axis, first) in zip(pieces, (("gx", 1), ("gy", 1), ("gy", 0), ("gx", 0)), strict=True):
         pairs = []
         for i in range(first, lax.axis_size(axis) - 1, 2):
             pairs += [(i, i + 1), (i + 1, i)]

time: 161 us -> 161 us (level)
  no operation moved by 1% of the time
where the time goes in v6:
time: 161 us
  blocking collectives  68.8 us (43%)
  starting transfers between devices  68.7 us (43%)
  Pallas kernels  18.8 us (12%)
  waiting for transfers between devices  2.66 us (2%)
  between operations  1.64 us (1%)
    ppermute x20, starting transfers between devices, exchange(): received.append(lax.ppermute(piece, axis, pairs))  68.7 us
    all_to_all x1, blocking collectives, reduce_all(): pieces = lax.all_to_all(mine.reshape(along, part, H), 'gy', 0, 0)  22.1 us
    pallas_call x12, Pallas kernels, call(): pl.pallas_call(kernel, out_shape=[jax.ShapeDtypeStruct(shape, dtype) for...  17.4 us
    all_to_all x1, blocking collectives, reduce_all(): pieces = lax.all_to_all(packed.reshape(across, rows, H), 'gx', 0, 0)  16.5 us
    all_to_all x1, blocking collectives, reduce_all(): everything = lax.all_to_all(shared, 'gx', 0, 0).reshape(PACKED, H)  16 us
    all_to_all x1, blocking collectives, reduce_all(): mine = lax.all_to_all(shared, 'gy', 0, 0).reshape(rows, H)  14.1 us
  transfers between devices with their start and end apart: 20, of which 4 were waited for; matrix products, arithmetic and copies ran while one was open for 0% of the time, Pallas kernels for 2%

profile of v6, /device:TPU:1, one launch (start us, length us, event | category | flops | bytes accessed | tf_op | source)
XLA Modules:
  0.0 160.5 jit_solution(3323646706477073927)
XLA Ops:
  0.6 1.4 shard_map.197
  2.0 4.5 %collective-permute-start = (bf16[128,128]{1,0:T(8,128)(2,1)S(1)}, bf16[128,128]{1,0:T(8,128)(2,1)S(1)}, u32[]{:S(2)}, u32[]{:S(2)}) collective-permute-start(bf16[128,128]{1,0:T(8,128)(2,1)S(1)} %get-tuple-element.66), channel_id=1, source_target_pairs={{32,64},{64,32},{96,128},{128,96},{160,192},{192,160},{224,256},{2... | collective-permute-start | bytes 98312 | tf_op jit(solution)/shard_map/ppermute | solution.py:480
  6.6 0.7 collective-permute-start.1
  7.2 9.0 %collective-permute-start.2 = (bf16[128,128]{1,0:T(8,128)(2,1)S(1)}, bf16[128,128]{1,0:T(8,128)(2,1)S(1)}, u32[]{:S(2)}, u32[]{:S(2)}) collective-permute-start(bf16[128,128]{1,0:T(8,128)(2,1)S(1)} %get-tuple-element.68), channel_id=1, source_target_pairs={{0,1},{1,0},{2,3},{3,2},{4,5},{5,4},{6,7},{7,6},{8,9},{9,8},{10,11... | collective-permute-start | bytes 98312 | tf_op jit(solution)/shard_map/ppermute | solution.py:480
  16.2 1.9 %collective-permute-start.3 = (bf16[128,128]{1,0:T(8,128)(2,1)S(1)}, bf16[128,128]{1,0:T(8,128)(2,1)S(1)}, u32[]{:S(2)}, u32[]{:S(2)}) collective-permute-start(bf16[128,128]{1,0:T(8,128)(2,1)S(1)} %get-tuple-element.69), channel_id=1, source_target_pairs={{0,32},{32,0},{64,96},{96,64},{128,160},{160,128},{192,224},{224,1... | collective-permute-start | bytes 98312 | tf_op jit(solution)/shard_map/ppermute | solution.py:480
  18.8 1.1 shard_map.198.own_ref
  19.9 0.0 collective-permute-done.h0
  19.9 0.0 collective-permute-done.2.h2
  20.0 0.0 collective-permute-done.3.h3
  20.0 1.9 %shard_map.199 = (bf16[512,128]{1,0:T(8,128)(2,1)S(1)}, bf16[256,128]{1,0:T(8,128)(2,1)S(1)}, bf16[128,128]{1,0:T(8,128)(2,1)S(1)}, bf16[128,128]{1,0:T(8,128)(2...) custom-call(s32[1]{0:T(128)} %bitcast.20.live_ref, ...), custom_call_target="tpu_custom_call" | custom-call | flops 536870912 | bytes 1048576 | tf_op jit(solution)/shard_map/pallas_call | solution.py:463
  21.9 3.5 %collective-permute-start.4 = (bf16[128,128]{1,0:T(8,128)(2,1)S(1)}, bf16[128,128]{1,0:T(8,128)(2,1)S(1)}, u32[]{:S(2)}, u32[]{:S(2)}) collective-permute-start(bf16[128,128]{1,0:T(8,128)(2,1)S(1)} %get-tuple-element.76), channel_id=1, source_target_pairs={{32,64},{64,32},{96,128},{128,96},{160,192},{192,160},{224,256},{2... | collective-permute-start | bytes 98312 | tf_op jit(solution)/shard_map/ppermute | solution.py:480
  25.4 0.7 collective-permute-start.5
  26.1 5.1 %collective-permute-start.6 = (bf16[128,128]{1,0:T(8,128)(2,1)S(1)}, bf16[128,128]{1,0:T(8,128)(2,1)S(1)}, u32[]{:S(2)}, u32[]{:S(2)}) collective-permute-start(bf16[128,128]{1,0:T(8,128)(2,1)S(1)} %get-tuple-element.78), channel_id=1, source_target_pairs={{0,1},{1,0},{2,3},{3,2},{4,5},{5,4},{6,7},{7,6},{8,9},{9,8},{10,11... | collective-permute-start | bytes 98312 | tf_op jit(solution)/shard_map/ppermute | solution.py:480
  31.2 1.9 %collective-permute-start.7 = (bf16[128,128]{1,0:T(8,128)(2,1)S(1)}, bf16[128,128]{1,0:T(8,128)(2,1)S(1)}, u32[]{:S(2)}, u32[]{:S(2)}) collective-permute-start(bf16[128,128]{1,0:T(8,128)(2,1)S(1)} %get-tuple-element.79), channel_id=1, source_target_pairs={{0,32},{32,0},{64,96},{96,64},{128,160},{160,128},{192,224},{224,1... | collective-permute-start | bytes 98312 | tf_op jit(solution)/shard_map/ppermute | solution.py:480
  33.1 0.9 shard_map.200.own_ref
  34.0 0.0 collective-permute-done.4.h0
  34.0 0.3 collective-permute-done.7.h3
  34.3 1.7 %shard_map.201 = (bf16[256,128]{1,0:T(8,128)(2,1)S(1)}, bf16[128,128]{1,0:T(8,128)(2,1)S(1)}, bf16[128,128]{1,0:T(8,128)(2,1)S(1)}, bf16[128,128]{1,0:T(8,128)(2...) custom-call(s32[1,4]{1,0:T(1,128)S(1)} %get-tuple-element.64.blocks_, ...), custom_call_target="tpu_custom_call" | custom-call | flops 536870912 | bytes 1048576 | tf_op jit(solution)/shard_map/pallas_call | solution.py:463
  36.0 3.0 %collective-permute-start.8 = (bf16[128,128]{1,0:T(8,128)(2,1)S(1)}, bf16[128,128]{1,0:T(8,128)(2,1)S(1)}, u32[]{:S(2)}, u32[]{:S(2)}) collective-permute-start(bf16[128,128]{1,0:T(8,128)(2,1)S(1)} %get-tuple-element.85), channel_id=1, source_target_pairs={{32,64},{64,32},{96,128},{128,96},{160,192},{192,160},{224,256},{2... | collective-permute-start | bytes 98312 | tf_op jit(solution)/shard_map/ppermute | solution.py:480
  39.0 0.7 collective-permute-start.9
  39.6 9.0 %collective-permute-start.10 = (bf16[128,128]{1,0:T(8,128)(2,1)S(1)}, bf16[128,128]{1,0:T(8,128)(2,1)S(1)}, u32[]{:S(2)}, u32[]{:S(2)}) collective-permute-start(bf16[128,128]{1,0:T(8,128)(2,1)S(1)} %get-tuple-element.87), channel_id=1, source_target_pairs={{0,1},{1,0},{2,3},{3,2},{4,5},{5,4},{6,7},{7,6},{8,9},{9,8},{10,11... | collective-permute-start | bytes 98312 | tf_op jit(solution)/shard_map/ppermute | solution.py:480
  48.6 1.9 %collective-permute-start.11 = (bf16[128,128]{1,0:T(8,128)(2,1)S(1)}, bf16[128,128]{1,0:T(8,128)(2,1)S(1)}, u32[]{:S(2)}, u32[]{:S(2)}) collective-permute-start(bf16[128,128]{1,0:T(8,128)(2,1)S(1)} %get-tuple-element.88), channel_id=1, source_target_pairs={{0,32},{32,0},{64,96},{96,64},{128,160},{160,128},{192,224},{224,1... | collective-permute-start | bytes 98312 | tf_op jit(solution)/shard_map/ppermute | solution.py:480
  50.5 0.9 shard_map.202.own_ref
  51.4 0.0 collective-permute-done.9.h1
  51.4 0.0 collective-permute-done.10.h2
  51.5 0.3 collective-permute-done.11.h3
  51.7 4.3 %shard_map.203 = (bf16[512,128]{1,0:T(8,128)(2,1)}, f32[256,128]{1,0:T(8,128)S(1)}, bf16[128,128]{1,0:T(8,128)(2,1)S(1)}, bf16[128,128]{1,0:T(8,128)(2,1)S(1)}, ...) custom-call(bf16[256,128]{1,0:T(8,128)(2,1)S(1)} %get-tuple-element.84.x_ref, ...), custom_call_target="tpu_custom_call" | custom-call | flops 536870912 | bytes 1048576 | tf_op jit(solution)/shard_map/pallas_call | solution.py:463
  56.0 3.2 %collective-permute-start.12 = (bf16[128,128]{1,0:T(8,128)(2,1)S(1)}, bf16[128,128]{1,0:T(8,128)(2,1)S(1)}, u32[]{:S(2)}, u32[]{:S(2)}) collective-permute-start(bf16[128,128]{1,0:T(8,128)(2,1)S(1)} %get-tuple-element.93), channel_id=1, source_target_pairs={{32,64},{64,32},{96,128},{128,96},{160,192},{192,160},{224,256},{2... | collective-permute-start | bytes 98312 | tf_op jit(solution)/shard_map/ppermute | solution.py:480
  59.2 0.7 collective-permute-start.13
  59.9 5.2 %collective-permute-start.14 = (bf16[128,128]{1,0:T(8,128)(2,1)S(1)}, bf16[128,128]{1,0:T(8,128)(2,1)S(1)}, u32[]{:S(2)}, u32[]{:S(2)}) collective-permute-start(bf16[128,128]{1,0:T(8,128)(2,1)S(1)} %get-tuple-element.95), channel_id=1, source_target_pairs={{0,1},{1,0},{2,3},{3,2},{4,5},{5,4},{6,7},{7,6},{8,9},{9,8},{10,11... | collective-permute-start | bytes 98312 | tf_op jit(solution)/shard_map/ppermute | solution.py:480
  65.1 2.1 %collective-permute-start.15 = (bf16[128,128]{1,0:T(8,128)(2,1)S(1)}, bf16[128,128]{1,0:T(8,128)(2,1)S(1)}, u32[]{:S(2)}, u32[]{:S(2)}) collective-permute-start(bf16[128,128]{1,0:T(8,128)(2,1)S(1)} %get-tuple-element.96), channel_id=1, source_target_pairs={{0,32},{32,0},{64,96},{96,64},{128,160},{160,128},{192,224},{224,1... | collective-permute-start | bytes 98312 | tf_op jit(solution)/shard_map/ppermute | solution.py:480
  67.2 0.0 collective-permute-done.14.r2
  67.2 1.0 collective-permute-done.15.r3
  68.2 2.5 %shard_map.204 = (f32[256,128]{1,0:T(8,128)S(1)}, bf16[128,128]{1,0:T(8,128)(2,1)S(1)}, bf16[128,128]{1,0:T(8,128)(2,1)S(1)}, bf16[128,128]{1,0:T(8,128)(2,1)S(1...) custom-call(s32[1,4]{1,0:T(1,128)S(1)} %get-tuple-element.64.blocks_ref, ...), custom_call_target="tpu_custom_call" | custom-call | flops 536870912 | bytes 1048576 | tf_op jit(solution)/shard_map/pallas_call | solution.py:463
  70.7 4.2 %collective-permute-start.16 = (bf16[128,128]{1,0:T(8,128)(2,1)S(1)}, bf16[128,128]{1,0:T(8,128)(2,1)S(1)}, u32[]{:S(2)}, u32[]{:S(2)}) collective-permute-start(bf16[128,128]{1,0:T(8,128)(2,1)S(1)} %get-tuple-element.102), channel_id=1, source_target_pairs={{32,64},{64,32},{96,128},{128,96},{160,192},{192,160},{224,256},{2... | collective-permute-start | bytes 98312 | tf_op jit(solution)/shard_map/ppermute | solution.py:480
  74.9 0.7 collective-permute-start.17
  75.6 9.0 %collective-permute-start.18 = (bf16[128,128]{1,0:T(8,128)(2,1)S(1)}, bf16[128,128]{1,0:T(8,128)(2,1)S(1)}, u32[]{:S(2)}, u32[]{:S(2)}) collective-permute-start(bf16[128,128]{1,0:T(8,128)(2,1)S(1)} %get-tuple-element.104), channel_id=1, source_target_pairs={{0,1},{1,0},{2,3},{3,2},{4,5},{5,4},{6,7},{7,6},{8,9},{9,8},{10,11... | collective-permute-start | bytes 98312 | tf_op jit(solution)/shard_map/ppermute | solution.py:480
  84.6 1.9 %collective-permute-start.19 = (bf16[128,128]{1,0:T(8,128)(2,1)S(1)}, bf16[128,128]{1,0:T(8,128)(2,1)S(1)}, u32[]{:S(2)}, u32[]{:S(2)}) collective-permute-start(bf16[128,128]{1,0:T(8,128)(2,1)S(1)} %get-tuple-element.105), channel_id=1, source_target_pairs={{0,32},{32,0},{64,96},{96,64},{128,160},{160,128},{192,224},{224,1... | collective-permute-start | bytes 98312 | tf_op jit(solution)/shard_map/ppermute | solution.py:480
  86.5 0.0 collective-permute-done.16.r0
  86.5 0.0 collective-permute-done.17.r1
  86.5 1.1 collective-permute-done.19.r3
  87.7 2.9 %shard_map.205 = (f32[256,128]{1,0:T(8,128)}, bf16[2048,128]{1,0:T(8,128)(2,1)S(1)}) custom-call(s32[1]{0:T(128)} %bitcast.21.live_ref, s32[1,4]{1,0:T(1,128)S(1)} %get-tuple-element.64.blocks_ref, f32[256,128]{1,0:T(8,128)S(1)} %get-tuple-element.101.grad_in_ref, bf16[128,128]{1,0:T(8,128)(2,1)S(1)} %collective-permute-done.16.r0, ...), custom_call_target="tpu_custom_call" | custom-call | flops 536870912 | bytes 1048576 | tf_op jit(solution)/shard_map/pallas_call | solution.py:463
  90.6 16.5 %all_to_all.20.parts_ref = bf16[16,128,128]{2,1,0:T(8,128)(2,1)S(1)} all-to-all(bf16[16,128,128]{2,1,0:T(8,128)(2,1)S(1)} %bitcast.22), channel_id=1, replica_groups=mesh['gx'=16,'gy'=32] {'gx'}, dimensions={0} | all-to-all | bytes 1048576 | tf_op jit(solution)/shard_map/all_to_all | solution.py:444
  107.1 0.1 shard_map.206
  107.2 22.1 %all_to_all.21.parts_ref = f32[32,4,128]{2,1,0:T(4,128)S(1)} all-to-all(f32[32,4,128]{2,1,0:T(4,128)S(1)} %bitcast.24), channel_id=1, replica_groups=mesh['gx'=16,'gy'=32] {'gy'}, dimensions={0} | all-to-all | bytes 131072 | tf_op jit(solution)/shard_map/all_to_all | solution.py:446
  129.3 14.1 %all_to_all.22 = f32[32,4,128]{2,1,0:T(4,128)S(1)} all-to-all(f32[32,4,128]{2,1,0:T(4,128)S(1)} %shard_map.207), channel_id=1, replica_groups=mesh['gx'=16,'gy'=32] {'gy'}, dimensions={0} | all-to-all | bytes 131072 | tf_op jit(solution)/shard_map/all_to_all | solution.py:448
  143.5 16.0 %all_to_all.23 = bf16[16,128,128]{2,1,0:T(8,128)(2,1)S(1)} all-to-all(bf16[16,128,128]{2,1,0:T(8,128)(2,1)S(1)} %shard_map.208), channel_id=1, replica_groups=mesh['gx'=16,'gy'=32] {'gx'}, dimensions={0} | all-to-all | bytes 1048576 | tf_op jit(solution)/shard_map/all_to_all | solution.py:450
  159.5 1.0 shard_map.209
  (9 shorter events, 0.1 us)
Async XLA Ops:
  2.0 17.9 %collective-permute-start = (bf16[128,128]{1,0:T(8,128)(2,1)S(1)}, bf16[128,128]{1,0:T(8,128)(2,1)S(1)}, u32[]{:S(2)}, u32[]{:S(2)}) collective-permute-start(bf16[128,128]{1,0:T(8,128)(2,1)S(1)} %get-tuple-element.66), channel_id=1, source_target_pairs={{32,64},{64,32},{96,128},{128,96},{160,192},{192,160},{224,256},{2... | collective-permute-start | bytes 98312 | tf_op jit(solution)/shard_map/ppermute | solution.py:480
  6.6 13.4 %collective-permute-start.1 = (bf16[128,128]{1,0:T(8,128)(2,1)S(1)}, bf16[128,128]{1,0:T(8,128)(2,1)S(1)}, u32[]{:S(2)}, u32[]{:S(2)}) collective-permute-start(bf16[128,128]{1,0:T(8,128)(2,1)S(1)} %get-tuple-element.67), channel_id=1, source_target_pairs={{1,2},{2,1},{3,4},{4,3},{5,6},{6,5},{7,8},{8,7},{9,10},{10,9},{11,... | collective-permute-start | bytes 98312 | tf_op jit(solution)/shard_map/ppermute | solution.py:480
  7.2 12.7 %collective-permute-start.2 = (bf16[128,128]{1,0:T(8,128)(2,1)S(1)}, bf16[128,128]{1,0:T(8,128)(2,1)S(1)}, u32[]{:S(2)}, u32[]{:S(2)}) collective-permute-start(bf16[128,128]{1,0:T(8,128)(2,1)S(1)} %get-tuple-element.68), channel_id=1, source_target_pairs={{0,1},{1,0},{2,3},{3,2},{4,5},{5,4},{6,7},{7,6},{8,9},{9,8},{10,11... | collective-permute-start | bytes 98312 | tf_op jit(solution)/shard_map/ppermute | solution.py:480
  16.2 3.7 %collective-permute-start.3 = (bf16[128,128]{1,0:T(8,128)(2,1)S(1)}, bf16[128,128]{1,0:T(8,128)(2,1)S(1)}, u32[]{:S(2)}, u32[]{:S(2)}) collective-permute-start(bf16[128,128]{1,0:T(8,128)(2,1)S(1)} %get-tuple-element.69), channel_id=1, source_target_pairs={{0,32},{32,0},{64,96},{96,64},{128,160},{160,128},{192,224},{224,1... | collective-permute-start | bytes 98312 | tf_op jit(solution)/shard_map/ppermute | solution.py:480
  21.9 12.1 %collective-permute-start.4 = (bf16[128,128]{1,0:T(8,128)(2,1)S(1)}, bf16[128,128]{1,0:T(8,128)(2,1)S(1)}, u32[]{:S(2)}, u32[]{:S(2)}) collective-permute-start(bf16[128,128]{1,0:T(8,128)(2,1)S(1)} %get-tuple-element.76), channel_id=1, source_target_pairs={{32,64},{64,32},{96,128},{128,96},{160,192},{192,160},{224,256},{2... | collective-permute-start | bytes 98312 | tf_op jit(solution)/shard_map/ppermute | solution.py:480
  25.4 8.6 %collective-permute-start.5 = (bf16[128,128]{1,0:T(8,128)(2,1)S(1)}, bf16[128,128]{1,0:T(8,128)(2,1)S(1)}, u32[]{:S(2)}, u32[]{:S(2)}) collective-permute-start(bf16[128,128]{1,0:T(8,128)(2,1)S(1)} %get-tuple-element.77), channel_id=1, source_target_pairs={{1,2},{2,1},{3,4},{4,3},{5,6},{6,5},{7,8},{8,7},{9,10},{10,9},{11,... | collective-permute-start | bytes 98312 | tf_op jit(solution)/shard_map/ppermute | solution.py:480
  26.1 7.9 %collective-permute-start.6 = (bf16[128,128]{1,0:T(8,128)(2,1)S(1)}, bf16[128,128]{1,0:T(8,128)(2,1)S(1)}, u32[]{:S(2)}, u32[]{:S(2)}) collective-permute-start(bf16[128,128]{1,0:T(8,128)(2,1)S(1)} %get-tuple-element.78), channel_id=1, source_target_pairs={{0,1},{1,0},{2,3},{3,2},{4,5},{5,4},{6,7},{7,6},{8,9},{9,8},{10,11... | collective-permute-start | bytes 98312 | tf_op jit(solution)/shard_map/ppermute | solution.py:480
  31.2 3.1 %collective-permute-start.7 = (bf16[128,128]{1,0:T(8,128)(2,1)S(1)}, bf16[128,128]{1,0:T(8,128)(2,1)S(1)}, u32[]{:S(2)}, u32[]{:S(2)}) collective-permute-start(bf16[128,128]{1,0:T(8,128)(2,1)S(1)} %get-tuple-element.79), channel_id=1, source_target_pairs={{0,32},{32,0},{64,96},{96,64},{128,160},{160,128},{192,224},{224,1... | collective-permute-start | bytes 98312 | tf_op jit(solution)/shard_map/ppermute | solution.py:480
  36.0 15.4 %collective-permute-start.8 = (bf16[128,128]{1,0:T(8,128)(2,1)S(1)}, bf16[128,128]{1,0:T(8,128)(2,1)S(1)}, u32[]{:S(2)}, u32[]{:S(2)}) collective-permute-start(bf16[128,128]{1,0:T(8,128)(2,1)S(1)} %get-tuple-element.85), channel_id=1, source_target_pairs={{32,64},{64,32},{96,128},{128,96},{160,192},{192,160},{224,256},{2... | collective-permute-start | bytes 98312 | tf_op jit(solution)/shard_map/ppermute | solution.py:480
  39.0 12.5 %collective-permute-start.9 = (bf16[128,128]{1,0:T(8,128)(2,1)S(1)}, bf16[128,128]{1,0:T(8,128)(2,1)S(1)}, u32[]{:S(2)}, u32[]{:S(2)}) collective-permute-start(bf16[128,128]{1,0:T(8,128)(2,1)S(1)} %get-tuple-element.86), channel_id=1, source_target_pairs={{1,2},{2,1},{3,4},{4,3},{5,6},{6,5},{7,8},{8,7},{9,10},{10,9},{11,... | collective-permute-start | bytes 98312 | tf_op jit(solution)/shard_map/ppermute | solution.py:480
  39.6 11.8 %collective-permute-start.10 = (bf16[128,128]{1,0:T(8,128)(2,1)S(1)}, bf16[128,128]{1,0:T(8,128)(2,1)S(1)}, u32[]{:S(2)}, u32[]{:S(2)}) collective-permute-start(bf16[128,128]{1,0:T(8,128)(2,1)S(1)} %get-tuple-element.87), channel_id=1, source_target_pairs={{0,1},{1,0},{2,3},{3,2},{4,5},{5,4},{6,7},{7,6},{8,9},{9,8},{10,11... | collective-permute-start | bytes 98312 | tf_op jit(solution)/shard_map/ppermute | solution.py:480
  48.6 3.1 %collective-permute-start.11 = (bf16[128,128]{1,0:T(8,128)(2,1)S(1)}, bf16[128,128]{1,0:T(8,128)(2,1)S(1)}, u32[]{:S(2)}, u32[]{:S(2)}) collective-permute-start(bf16[128,128]{1,0:T(8,128)(2,1)S(1)} %get-tuple-element.88), channel_id=1, source_target_pairs={{0,32},{32,0},{64,96},{96,64},{128,160},{160,128},{192,224},{224,1... | collective-permute-start | bytes 98312 | tf_op jit(solution)/shard_map/ppermute | solution.py:480
  56.0 11.1 %collective-permute-start.12 = (bf16[128,128]{1,0:T(8,128)(2,1)S(1)}, bf16[128,128]{1,0:T(8,128)(2,1)S(1)}, u32[]{:S(2)}, u32[]{:S(2)}) collective-permute-start(bf16[128,128]{1,0:T(8,128)(2,1)S(1)} %get-tuple-element.93), channel_id=1, source_target_pairs={{32,64},{64,32},{96,128},{128,96},{160,192},{192,160},{224,256},{2... | collective-permute-start | bytes 98312 | tf_op jit(solution)/shard_map/ppermute | solution.py:480
  59.2 8.0 %collective-permute-start.13 = (bf16[128,128]{1,0:T(8,128)(2,1)S(1)}, bf16[128,128]{1,0:T(8,128)(2,1)S(1)}, u32[]{:S(2)}, u32[]{:S(2)}) collective-permute-start(bf16[128,128]{1,0:T(8,128)(2,1)S(1)} %get-tuple-element.94), channel_id=1, source_target_pairs={{1,2},{2,1},{3,4},{4,3},{5,6},{6,5},{7,8},{8,7},{9,10},{10,9},{11,... | collective-permute-start | bytes 98312 | tf_op jit(solution)/shard_map/ppermute | solution.py:480
  59.9 7.3 %collective-permute-start.14 = (bf16[128,128]{1,0:T(8,128)(2,1)S(1)}, bf16[128,128]{1,0:T(8,128)(2,1)S(1)}, u32[]{:S(2)}, u32[]{:S(2)}) collective-permute-start(bf16[128,128]{1,0:T(8,128)(2,1)S(1)} %get-tuple-element.95), channel_id=1, source_target_pairs={{0,1},{1,0},{2,3},{3,2},{4,5},{5,4},{6,7},{7,6},{8,9},{9,8},{10,11... | collective-permute-start | bytes 98312 | tf_op jit(solution)/shard_map/ppermute | solution.py:480
  65.1 3.1 %collective-permute-start.15 = (bf16[128,128]{1,0:T(8,128)(2,1)S(1)}, bf16[128,128]{1,0:T(8,128)(2,1)S(1)}, u32[]{:S(2)}, u32[]{:S(2)}) collective-permute-start(bf16[128,128]{1,0:T(8,128)(2,1)S(1)} %get-tuple-element.96), channel_id=1, source_target_pairs={{0,32},{32,0},{64,96},{96,64},{128,160},{160,128},{192,224},{224,1... | collective-permute-start | bytes 98312 | tf_op jit(solution)/shard_map/ppermute | solution.py:480
  70.7 15.8 %collective-permute-start.16 = (bf16[128,128]{1,0:T(8,128)(2,1)S(1)}, bf16[128,128]{1,0:T(8,128)(2,1)S(1)}, u32[]{:S(2)}, u32[]{:S(2)}) collective-permute-start(bf16[128,128]{1,0:T(8,128)(2,1)S(1)} %get-tuple-element.102), channel_id=1, source_target_pairs={{32,64},{64,32},{96,128},{128,96},{160,192},{192,160},{224,256},{2... | collective-permute-start | bytes 98312 | tf_op jit(solution)/shard_map/ppermute | solution.py:480
  74.9 11.6 %collective-permute-start.17 = (bf16[128,128]{1,0:T(8,128)(2,1)S(1)}, bf16[128,128]{1,0:T(8,128)(2,1)S(1)}, u32[]{:S(2)}, u32[]{:S(2)}) collective-permute-start(bf16[128,128]{1,0:T(8,128)(2,1)S(1)} %get-tuple-element.103), channel_id=1, source_target_pairs={{1,2},{2,1},{3,4},{4,3},{5,6},{6,5},{7,8},{8,7},{9,10},{10,9},{11,... | collective-permute-start | bytes 98312 | tf_op jit(solution)/shard_map/ppermute | solution.py:480
  75.6 11.0 %collective-permute-start.18 = (bf16[128,128]{1,0:T(8,128)(2,1)S(1)}, bf16[128,128]{1,0:T(8,128)(2,1)S(1)}, u32[]{:S(2)}, u32[]{:S(2)}) collective-permute-start(bf16[128,128]{1,0:T(8,128)(2,1)S(1)} %get-tuple-element.104), channel_id=1, source_target_pairs={{0,1},{1,0},{2,3},{3,2},{4,5},{5,4},{6,7},{7,6},{8,9},{9,8},{10,11... | collective-permute-start | bytes 98312 | tf_op jit(solution)/shard_map/ppermute | solution.py:480
  84.6 3.1 %collective-permute-start.19 = (bf16[128,128]{1,0:T(8,128)(2,1)S(1)}, bf16[128,128]{1,0:T(8,128)(2,1)S(1)}, u32[]{:S(2)}, u32[]{:S(2)}) collective-permute-start(bf16[128,128]{1,0:T(8,128)(2,1)S(1)} %get-tuple-element.105), channel_id=1, source_target_pairs={{0,32},{32,0},{64,96},{96,64},{128,160},{160,128},{192,224},{224,1... | collective-permute-start | bytes 98312 | tf_op jit(solution)/shard_map/ppermute | solution.py:480
